TPU v7x, 512 devices: a whole 4x4x16 slice. The times are simulated.
512 devices in a mesh: row: 16 (over z), col: 32 (over x, y, core).
Axes of the slice: x: 4, y: 4, z: 16, core: 2. Of those that a mesh axis runs over, the one named last changes fastest.
Arguments:
- magnet: float32 [3, 2048, 2048], P(None, 'col', 'row'), may hold values from -1 to 1, as said below
- stiffness: float32 [2048, 2048], P('col', 'row'), may hold values from 0.5 to 2
- kern: float32 [6, 2048, 4096], P(None, ('row', 'col')), may hold values from -8 to 8
Outputs:
- torque: float32 [3, 2048, 2048], P(None, 'col', 'row')
Inputs may be any that keep to these rules, and one draw needn't show every extreme that they name: `magnet`: each cell's three components form a unit vector.
All inputs are finite; a program needn't handle non-finite values.
Results may differ from a plain program's by a relative error of at most 0.00011.
Values sent between devices are 32-bit elements; how exact they have to be, the bound alone decides.
No kernel may reach another device: no remote copies, remote signals or barrier semaphores. Data moves between devices by JAX's collectives and lax.ppermute only.
A program may use at most 64 MiB of HBM per device.

v0:
```python
import functools
import math

import jax
import jax.numpy as jnp
import ml_dtypes
import numpy as np
from jax import lax
from jax.experimental import pallas as pl
from jax.experimental.pallas import tpu as pltpu
from jax.sharding import PartitionSpec as P

damping = 0.3
anisotropy = 0.8
tensor_slots = ((0, 3, 4), (3, 1, 5), (4, 5, 2))

rows_n = 16
cols_n = 32
cells = 64
lanes = 128
length = 4096
bf16 = jnp.bfloat16
f32 = jnp.float32


def wave(first, second, period):
    angle = 2.0 * math.pi * (np.outer(first, second) % period) / period
    return np.cos(angle), np.sin(angle)


def split_table(table):
    high = table.astype(ml_dtypes.bfloat16)
    low = (table - high.astype(np.float64)).astype(ml_dtypes.bfloat16)
    return high, low


def thick(table):
    high, low = split_table(table)
    return np.concatenate([high, low, high], 1)


def tall(table):
    return np.concatenate(split_table(table), 0)


def tables():
    row = np.arange(rows_n)
    col = np.arange(cols_n)
    y_l = np.arange(lanes)
    k1 = (4 * np.arange(8)[None, :] + np.arange(4)[:, None]).reshape(-1)
    k2 = np.arange(64)
    x_ir = (4 * row[None, :] + np.arange(4)[:, None]).reshape(-1)
    k1x = np.arange(64)
    k2x = (2 * np.arange(32)[None, :] + np.arange(2)[:, None]).reshape(-1)
    x_rci = np.repeat(4 * row[:, None, None] + np.arange(4)[None, None, :], 2, 1).reshape(-1)
    imag_rci = np.repeat(np.repeat(np.arange(2)[None, :, None], rows_n, 0), 4, 2).reshape(-1, 1)
    kappa = (4 * col[None, :] + np.arange(4)[:, None]).reshape(-1)
    y1 = np.arange(32)
    u_order = (4 * row[None, :] + np.arange(4)[:, None]).reshape(-1)

    cos, sin = wave(k1, row, 32)
    y_first = thick(np.concatenate([cos, -sin], 0))
    cos, sin = wave(k1, y_l, length)
    y_twist = np.stack([cos, sin]).astype(np.float32)
    cos, sin = wave(k2, y_l, 128)
    y_last = np.stack([np.concatenate([cos, sin], 1), np.concatenate([-sin, cos], 1)], 1)
    y_last = tall(y_last.reshape(128, 256))

    cos, sin = wave(k1x, col, 64)
    x_first = thick(np.concatenate([cos, sin], 0))
    x_back = tall(np.concatenate([cos, sin], 0).reshape(2, 64, 32).transpose(2, 0, 1).reshape(32, 128))
    cos, sin = wave(k1x, x_ir, length)
    x_twist = np.stack([np.concatenate([cos, cos], 1), np.concatenate([sin, -sin], 1)])
    cos, sin = wave(k2x, x_ir, 64)
    x_last = tall(np.concatenate([cos, sin], 1))
    cos, sin = wave(x_rci, k2x, 64)
    x_lead = tall(np.concatenate([cos, sin], 1))
    cos, sin = wave(x_rci, k1x, length)
    own = np.where(imag_rci == 0, np.concatenate([cos, -cos], 1), np.concatenate([sin, -sin], 1))
    other = np.where(imag_rci == 0, np.concatenate([-sin, -sin], 1), np.concatenate([cos, cos], 1))
    x_untwist = np.stack([own, other])
    x_twists = np.concatenate([x_twist, x_untwist], 1).astype(np.float32)

    cos, sin = wave(y1, row, 32)
    z_first = thick(np.concatenate([np.concatenate([cos, -sin], 1), np.concatenate([sin, cos], 1)], 0))
    cos, sin = wave(y1, kappa, length)
    z_twist = np.stack([cos, sin]).astype(np.float32)
    cos, sin = wave(u_order, kappa, 128)
    z_last = tall(np.concatenate([cos, -sin], 1))
    return {
        "y": (y_first, y_twist, y_last),
        "x": (x_first, x_twists, x_last, x_lead, x_back),
        "z": (z_first, z_twist, z_last),
    }


def split(values):
    high = values.astype(bf16)
    low = (values - high.astype(f32)).astype(bf16)
    return high, low


def stacked_product(table, values):
    high, low = split(values)
    return jnp.dot(table, jnp.concatenate([high, high, low], 0), preferred_element_type=f32)


def split_product(table, values, contract):
    high, low = split(values)
    dims = (((1,), (contract,)), ((), ()))
    size = table.shape[0] // 2
    both = lax.dot_general(table, high, dims, preferred_element_type=f32)
    rest = lax.dot_general(table[:size], low, dims, preferred_element_type=f32)
    return both[:size] + both[size:] + rest


def half_turn(values):
    return pltpu.roll(values, 64, 1)


def lane_index(shape):
    return lax.broadcasted_iota(jnp.int32, shape, len(shape) - 1)


def pack_body(magnet_ref, stiff_ref, out_ref, edge_ref):
    for a in range(3):
        for i in range(4):
            out_ref[pl.ds(4 * a + i, rows_n, stride=16), :] = magnet_ref[
                a, pl.ds(i, rows_n, stride=4), :
            ]
    former = jnp.concatenate([magnet_ref[0], magnet_ref[1]], 0).T
    latter = jnp.concatenate([magnet_ref[2], stiff_ref[...]], 0).T
    for row, piece in enumerate((former[:1], latter[:1], former[127:], latter[127:])):
        out_ref[pl.ds(12 + row, rows_n, stride=16), :] = jnp.broadcast_to(piece, (rows_n, lanes))
    for a in range(3):
        edge_ref[a : a + 1, :] = magnet_ref[a, :1, :]
        edge_ref[4 + a : 5 + a, :] = magnet_ref[a, cells - 1 :, :]
    edge_ref[3:4, :] = stiff_ref[:1, :]
    edge_ref[7:8, :] = stiff_ref[cells - 1 :, :]


def kern_body(kern_ref, out_ref, held_ref):
    for j in range(6):
        for b in range(32):
            held_ref[pl.ds(j * 128 + b, 4, stride=32), :] = kern_ref[j, :, pl.ds(128 * b, 128)]
    low = lane_index((128, 128)) < 64
    for j in range(6):
        part = held_ref[pl.ds(j * 128, 128), :]
        turned = half_turn(part)
        even = jnp.where(low, part, turned)
        odd = jnp.where(low, turned, part)
        for k in range(4):
            out_ref[j, k, 0:32, :] = even[32 * k : 32 * k + 32]
            out_ref[j, k, 32:64, :] = odd[32 * k : 32 * k + 32]


def forward_rows_body(in_ref, first_ref, twist_ref, last_ref, out_ref):
    lines = [in_ref[pl.ds(4 * a + i, rows_n, stride=16), :] for i in range(4) for a in range(3)]
    section = stacked_product(first_ref[...], jnp.concatenate(lines, 1))
    cos, sin = twist_ref[0], twist_ref[1]
    turned = []
    for n in range(12):
        re = section[:32, 128 * n : 128 * n + 128]
        im = section[32:, 128 * n : 128 * n + 128]
        turned.append(jnp.concatenate([re * cos + im * sin, im * cos - re * sin], 1))
    result = split_product(last_ref[...], jnp.concatenate(turned, 0), 1)
    for r in range(rows_n):
        for t in range(3):
            out_ref[24 * r + 8 * t : 24 * r + 8 * t + 8, :] = result[
                8 * r : 8 * r + 8, 128 * t : 128 * t + 128
            ]


def forward_cols_body(place_ref, in_ref, edge_ref, out_ref):
    lane = lane_index((rows_n, 128))
    for k2l in range(4):
        pieces = []
        for part in range(2):
            tiles = [
                in_ref[pl.ds(8 * t + 2 * k2l + part, rows_n, stride=24), :]
                for t in range(3)
            ]
            pieces.append(tiles[0])
            for i in range(1, 4):
                tile, offset = divmod(96 * i, 128)
                piece = pltpu.roll(tiles[tile], 128 - offset, 1)
                if tile < 2:
                    after = pltpu.roll(tiles[tile + 1], 128 - offset, 1)
                    piece = jnp.where(lane < 128 - offset, piece, after)
                pieces.append(piece)
        turned = jnp.concatenate(pieces, 0).T
        for a in range(3):
            for k in range(4):
                out_ref[pl.ds(128 * k2l + 4 * a + k, 8, stride=16), :] = turned[
                    32 * a + 8 * k : 32 * a + 8 * k + 8
                ]
    col = place_ref[1]
    first, last = edge_ref[0:4, :], edge_ref[4:8, :]
    for c in range(cols_n):
        out_ref[16 * c + 12 : 16 * c + 16, :] = jnp.where(c > col, last, first)


def spectral_body(
    place_ref, in_ref, kern_ref, first_ref, twist_ref, last_ref, lead_ref, back_ref, out_ref
):
    columns = [in_ref[pl.ds(j, cols_n, stride=16), :] for j in range(12)]
    section = stacked_product(first_ref[...], jnp.concatenate(columns, 1))
    lane = lane_index((64, 128))
    sign = jnp.where(lane < 64, 1.0, -1.0).astype(f32)
    own, other = twist_ref[0, :64, :], twist_ref[1, :64, :]
    turned = []
    for j in range(12):
        block = section[:, 128 * j : 128 * j + 128]
        block = block[:64] + half_turn(block[64:]) * sign
        block = block * own + half_turn(block) * other
        turned.append(block)
        turned.append(half_turn(block) * sign)
    freq = split_product(last_ref[...], jnp.concatenate(turned, 0), 1)
    sources = []
    for target in range(3):
        for k in range(4):
            total = None
            for b in range(3):
                j = 4 * b + k
                term = kern_ref[tensor_slots[target][b], k] * freq[:, 128 * j : 128 * j + 128]
                total = term if total is None else total + term
            sources.append(jnp.concatenate([total, -half_turn(total) * sign], 0))
    section = split_product(lead_ref[...], jnp.concatenate(sources, 1), 0)
    own, other = twist_ref[0, 64:, :], twist_ref[1, 64:, :]
    turned = []
    for j in range(12):
        block = section[:, 128 * j : 128 * j + 128]
        turned.append(block * own + half_turn(block) * other)
    result = split_product(back_ref[...], jnp.concatenate(turned, 0), 1)
    scale = -1.0 / (length * length)
    lane = lane_index((cols_n, 128))
    zero_weight = jnp.where((lane // 4) % 2 == 0, 1.0, 0.0).astype(f32)
    is_zero = jnp.logical_and(place_ref[0] == 0, place_ref[1] == 0)
    for j in range(12):
        block = result[:, 128 * j : 128 * j + 128]
        weight = jnp.full((cols_n, 128), 2.0, f32)
        if j % 4 == 0:
            weight = jnp.where(is_zero, zero_weight, weight)
        out_ref[pl.ds(j, cols_n, stride=16), :] = block * (weight * scale)
    for j in range(12, 16):
        out_ref[pl.ds(j, cols_n, stride=16), :] = jnp.zeros((cols_n, 128), f32)


def back_cols_body(in_ref, out_ref):
    for a in range(3):
        block = [in_ref[pl.ds(4 * a + k, cols_n, stride=16), :] for k in range(4)]
        turned = jnp.concatenate(block, 0).T
        for r in range(rows_n):
            out_ref[24 * r + 8 * a : 24 * r + 8 * a + 8, :] = turned[8 * r : 8 * r + 8]


def back_rows_body(in_ref, first_ref, twist_ref, last_ref, out_ref):
    columns = []
    for a in range(3):
        for i in range(4):
            re = in_ref[pl.ds(8 * a + i, rows_n, stride=24), :]
            im = in_ref[pl.ds(8 * a + 4 + i, rows_n, stride=24), :]
            columns.append(jnp.concatenate([re, im], 0))
    section = stacked_product(first_ref[...], jnp.concatenate(columns, 1))
    cos, sin = twist_ref[0], twist_ref[1]
    turned = []
    for n in range(12):
        re = section[:32, 128 * n : 128 * n + 128]
        im = section[32:, 128 * n : 128 * n + 128]
        turned.append(jnp.concatenate([re * cos - im * sin, im * cos + re * sin], 1))
    result = split_product(last_ref[...], jnp.concatenate(turned, 0), 1)
    for a in range(3):
        for y2 in range(4):
            out_ref[pl.ds(4 * a + y2, rows_n, stride=16), :] = result[
                16 * y2 : 16 * y2 + 16, 128 * a : 128 * a + 128
            ]
    for j in range(12, 16):
        out_ref[pl.ds(j, rows_n, stride=16), :] = jnp.zeros((rows_n, 128), f32)


def cross(former, latter):
    return (
        former[1] * latter[2] - former[2] * latter[1],
        former[2] * latter[0] - former[0] * latter[2],
        former[0] * latter[1] - former[1] * latter[0],
    )


def torque_body(place_ref, in_ref, magnet_ref, stiff_ref, beside_y_ref, beside_x_ref, out_ref, field_ref):
    row, col = place_ref[0], place_ref[1]
    group = lane_index((rows_n, 128)) // 32
    for a in range(3):
        tiles = [in_ref[pl.ds(4 * a + y2, rows_n, stride=16), :] for y2 in range(4)]
        for i in range(4):
            line = None
            for y2 in range(4):
                shift = (32 * (y2 - i)) % 128
                piece = tiles[y2] if shift == 0 else pltpu.roll(tiles[y2], shift, 1)
                line = piece if line is None else jnp.where(group == y2, piece, line)
            field_ref[a, pl.ds(i, rows_n, stride=4), :] = line
    before_y = beside_y_ref[pl.ds(pl.multiple_of(16 * jnp.maximum(row - 1, 0), 16), 16), :]
    after_y = beside_y_ref[pl.ds(pl.multiple_of(16 * jnp.minimum(row + 1, rows_n - 1), 16), 16), :]
    before_x = beside_x_ref[pl.ds(pl.multiple_of(16 * jnp.maximum(col - 1, 0), 16), 16), :]
    after_x = beside_x_ref[pl.ds(pl.multiple_of(16 * jnp.minimum(col + 1, cols_n - 1), 16), 16), :]
    edges = jnp.concatenate([before_y[14:16], after_y[12:14], jnp.zeros((124, 128), f32)], 0).T
    stack = [magnet_ref[0], magnet_ref[1], magnet_ref[2], stiff_ref[...]]
    lane = lane_index((cells, 128))
    sub = lax.broadcasted_iota(jnp.int32, (cells, 128), 0)

    def neighbour(n, direction):
        centre = stack[n]
        part = slice(64 * (n % 2), 64 * (n % 2) + 64)
        if direction == 0:
            return jnp.where(sub == cells - 1, after_x[12 + n : 13 + n], pltpu.roll(centre, cells - 1, 0))
        if direction == 1:
            return jnp.where(sub == 0, before_x[12 + n : 13 + n], pltpu.roll(centre, 1, 0))
        if direction == 2:
            edge = edges[part, 2 + n // 2 : 3 + n // 2]
            return jnp.where(lane == 127, edge, pltpu.roll(centre, 127, 1))
        edge = edges[part, n // 2 : n // 2 + 1]
        return jnp.where(lane == 0, edge, pltpu.roll(centre, 1, 1))

    absent = (
        jnp.logical_and(sub == cells - 1, col == cols_n - 1),
        jnp.logical_and(sub == 0, col == 0),
        jnp.logical_and(lane == 127, row == rows_n - 1),
        jnp.logical_and(lane == 0, row == 0),
    )
    exchange = [None] * 3
    for direction in range(4):
        coupling = 0.5 * (stack[3] + neighbour(3, direction))
        coupling = jnp.where(absent[direction], 0.0, coupling)
        for a in range(3):
            term = coupling * (neighbour(a, direction) - stack[a])
            exchange[a] = term if exchange[a] is None else exchange[a] + term
    magnet = stack[:3]
    field = [exchange[a] + field_ref[a] for a in range(3)]
    field[2] = field[2] + anisotropy * magnet[2]
    first_cross = cross(magnet, field)
    second_cross = cross(magnet, first_cross)
    factor = -1.0 / (1.0 + damping * damping)
    for a in range(3):
        out_ref[a] = (first_cross[a] + damping * second_cross[a]) * factor


in_vmem = pl.BlockSpec(memory_space=pltpu.VMEM)
in_smem = pl.BlockSpec(memory_space=pltpu.SMEM)


def call(body, out_shapes, *args, scratch=(), place=False, flops=10**8):
    shapes = [jax.ShapeDtypeStruct(shape, f32) for shape in out_shapes]
    specs = [in_smem if place and n == 0 else in_vmem for n in range(len(args))]
    return pl.pallas_call(
        body,
        out_shape=shapes,
        in_specs=specs,
        out_specs=[in_vmem] * len(shapes),
        scratch_shapes=list(scratch),
        compiler_params=pltpu.CompilerParams(vmem_limit_bytes=48 * 1024 * 1024),
        cost_estimate=pl.CostEstimate(flops=flops, bytes_accessed=10**6, transcendentals=0),
    )(*args)


def exchange(array, axis, chunks):
    shape = array.shape
    array = array.reshape(chunks, shape[0] // chunks, shape[1])
    return lax.all_to_all(array, axis, split_axis=0, concat_axis=0, tiled=True).reshape(shape)


def local(magnet, stiffness, kern):
    constant = {name: [jnp.asarray(t) for t in group] for name, group in tables().items()}
    place = jnp.stack([lax.axis_index("row"), lax.axis_index("col")]).astype(jnp.int32)
    packed, edge = call(pack_body, [(256, 128), (8, 128)], magnet, stiffness)
    (spread,) = call(
        kern_body, [(6, 4, 64, 128)], kern, scratch=[pltpu.VMEM((768, 128), f32)]
    )
    lines = exchange(packed, "row", rows_n)
    (along_y,) = call(forward_rows_body, [(384, 128)], lines, *constant["y"])
    along_y = exchange(along_y, "row", rows_n)
    (columns,) = call(forward_cols_body, [(512, 128)], place, along_y, edge, place=True)
    columns = exchange(columns, "col", cols_n)
    (inverse_x,) = call(
        spectral_body, [(512, 128)], place, columns, spread, *constant["x"], place=True
    )
    inverse_x = exchange(inverse_x, "col", cols_n)
    (coef,) = call(back_cols_body, [(384, 128)], inverse_x)
    coef = exchange(coef, "row", rows_n)
    (field,) = call(back_rows_body, [(256, 128)], coef, *constant["z"])
    field = exchange(field, "row", rows_n)
    (torque,) = call(
        torque_body,
        [(3, 64, 128)],
        place,
        field,
        magnet,
        stiffness,
        lines,
        columns,
        place=True,
        scratch=[pltpu.VMEM((3, 64, 128), f32)],
    )
    return torque


def solution(mesh):
    in_specs = (P(None, "col", "row"), P("col", "row"), P(None, ("row", "col"), None))
    out_specs = P(None, "col", "row")
    return jax.shard_map(local, mesh=mesh, in_specs=in_specs, out_specs=out_specs, check_vma=False)
```

profile of v0, /device:TPU:32, one launch (start us, length us, event | category | flops | bytes accessed | tf_op | source)
XLA Modules:
  0.0 128.3 jit_solution(16751454839419509669)
XLA Ops:
  0.0 0.9 copy-done.3
  0.9 0.0 copy-start.7
  0.9 0.8 copy-done.7
  1.7 0.1 shard_map.136
  1.8 0.0 copy-start.2
  1.8 0.0 copy-start.12
  1.8 0.0 copy-start.15
  1.8 29.3 %all_to_all.30 = f32[16,16,128]{2,1,0:T(8,128)S(1)} all-to-all(f32[16,16,128]{2,1,0:T(8,128)S(1)} %bitcast.25), channel_id=1, replica_groups=mesh['row'=16,'col'=32] {'row'}, dimensions={0} | all-to-all | bytes 262144 | tf_op jit(solution)/shard_map/all_to_all | solution.py:367
  31.2 0.0 copy-done.2
  31.2 0.0 copy-done.12
  31.2 0.0 copy-done.15
  31.2 1.1 shard_map.137
  32.3 4.3 %all-to-all-start.1 = ((f32[16,24,128]{2,1,0:T(8,128)}), f32[16,24,128]{2,1,0:T(8,128)S(1)}, u32[]{:S(2)}, u32[]{:S(2)}) async-start(f32[16,24,128]{2,1,0:T(8,128)} %bitcast.4), calls=%async_computation.1 | async-start | bytes 393216 | tf_op jit(solution)/shard_map/all_to_all | solution.py:367
  36.6 0.1 pad_add_fusion.place_ref
  36.7 16.1 %all-to-all-done.1 = f32[16,24,128]{2,1,0:T(8,128)S(1)} async-done(((f32[16,24,128]{2,1,0:T(8,128)}), f32[16,24,128]{2,1,0:T(8,128)S(1)}, u32[]{:S(2)}, u32[]{:S(2)}) %all-to-all-start.1) | async-done | bytes 196640 | tf_op jit(solution)/shard_map/all_to_all | solution.py:367
  52.8 0.0 copy-start
  52.8 1.5 %shard_map.138 = f32[512,128]{1,0:T(8,128)} custom-call(s32[2]{0:T(128)S(1)} %pad_add_fusion.place_ref, f32[384,128]{1,0:T(8,128)S(1)} %bitcast.22, f32[8,128]{1,0:T(8,128)S(1)} %get-tuple-element.8.edge_ref), custom_call_target="tpu_custom_call" | custom-call | flops 100000000 | bytes 1000000 | tf_op jit(solution)/shard_map/pallas_call | solution.py:353
  54.3 7.3 %all-to-all-start.2 = ((f32[32,16,128]{2,1,0:T(8,128)}), f32[32,16,128]{2,1,0:T(8,128)S(1)}, u32[]{:S(2)}, u32[]{:S(2)}) async-start(f32[32,16,128]{2,1,0:T(8,128)} %bitcast.6), calls=%async_computation.2 | async-start | bytes 524288 | tf_op jit(solution)/shard_map/all_to_all | solution.py:367
  61.6 0.0 copy-done
  61.6 0.0 copy-start.1
  61.6 0.0 copy-start.6
  61.6 0.0 copy-start.10
  61.6 0.0 copy-start.11
  61.7 0.0 copy-start.13
  61.7 0.4 shard_map.139.kern_ref
  62.0 8.5 %all-to-all-done.2 = f32[32,16,128]{2,1,0:T(8,128)S(1)} async-done(((f32[32,16,128]{2,1,0:T(8,128)}), f32[32,16,128]{2,1,0:T(8,128)S(1)}, u32[]{:S(2)}, u32[]{:S(2)}) %all-to-all-start.2) | async-done | bytes 262176 | tf_op jit(solution)/shard_map/all_to_all | solution.py:367
  70.5 0.0 copy-done.1
  70.5 0.0 copy-done.6
  70.5 0.0 copy-done.10
  70.6 0.0 copy-done.11
  70.6 0.0 copy-done.13
  70.6 2.4 %shard_map.140 = f32[512,128]{1,0:T(8,128)S(1)} custom-call(s32[2]{0:T(128)S(1)} %pad_add_fusion.place_ref, f32[512,128]{1,0:T(8,128)S(1)} %bitcast.14, f32[6,4,64,128]{3,2,1,0:T(8,128)S(1)} %shard_map.139.kern_ref, bf16[128,96]{1,0:T(8,128)(2,1)S(1)} %copy-done.11, f32[2,192,128]{2,1,0:T(8,128)S(1)} %copy-done.1, bf16[128,128]{1,0:T(8,128)(2,1)S(1)} %copy-done.10, ...), custom_call_target="tpu_custom_call" | custom-call | flops 100000000 | bytes 1000000 | tf_op jit(solution)/shard_map/pallas_call | solution.py:353
  72.9 12.5 %all_to_all.31 = f32[32,16,128]{2,1,0:T(8,128)S(1)} all-to-all(f32[32,16,128]{2,1,0:T(8,128)S(1)} %bitcast.19), channel_id=1, replica_groups=mesh['row'=16,'col'=32] {'col'}, dimensions={0} | all-to-all | bytes 524288 | tf_op jit(solution)/shard_map/all_to_all | solution.py:367
  85.4 0.1 shard_map.141
  85.5 0.0 copy-start.5
  85.6 0.0 copy-start.9
  85.6 0.0 copy-start.14
  85.6 20.9 %all_to_all.32 = f32[16,24,128]{2,1,0:T(8,128)S(1)} all-to-all(f32[16,24,128]{2,1,0:T(8,128)S(1)} %bitcast.21), channel_id=1, replica_groups=mesh['row'=16,'col'=32] {'row'}, dimensions={0} | all-to-all | bytes 393216 | tf_op jit(solution)/shard_map/all_to_all | solution.py:367
  106.5 0.0 copy-done.5
  106.5 0.0 copy-done.9
  106.5 0.0 copy-done.14
  106.5 0.4 shard_map.142
  107.0 0.0 copy-start.4
  107.0 0.0 copy-start.8
  107.0 19.7 %all_to_all.33 = f32[16,16,128]{2,1,0:T(8,128)S(1)} all-to-all(f32[16,16,128]{2,1,0:T(8,128)S(1)} %bitcast.23), channel_id=1, replica_groups=mesh['row'=16,'col'=32] {'row'}, dimensions={0} | all-to-all | bytes 262144 | tf_op jit(solution)/shard_map/all_to_all | solution.py:367
  126.7 0.0 copy-done.4
  126.7 0.0 copy-done.8
  126.7 1.6 %shard_map.143 = f32[3,64,128]{2,1,0:T(8,128)} custom-call(s32[2]{0:T(128)S(1)} %pad_add_fusion.place_ref, f32[256,128]{1,0:T(8,128)S(1)} %bitcast.24, f32[3,64,128]{2,1,0:T(8,128)S(1)} %copy-done.4, f32[64,128]{1,0:T(8,128)S(1)} %copy-done.8, f32[256,128]{1,0:T(8,128)S(1)} %bitcast.17, f32[512,128]{1,0:T(8,128)S(1)} %bitcast.15), custom_call_target="tpu_custom_call" | custom-call | flops 100000000 | bytes 1000000 | tf_op jit(solution)/shard_map/pallas_call | solution.py:353
  (1 shorter events, 0.0 us)
Async XLA Ops:
  0.0 0.9 copy-start.3
  0.9 0.8 copy-start.7
  1.8 29.4 %copy-start.2 = (bf16[256,256]{1,0:T(8,128)(2,1)S(1)}, bf16[256,256]{1,0:T(8,128)(2,1)}, u32[]{:S(2)}) copy-start(bf16[256,256]{1,0:T(8,128)(2,1)} %constant.33.clone.last_ref) | copy-start | bytes 393220
  1.8 29.4 %copy-start.12 = (f32[2,32,128]{2,1,0:T(8,128)S(1)}, f32[2,32,128]{2,1,0:T(8,128)}, u32[]{:S(2)}) copy-start(f32[2,32,128]{2,1,0:T(8,128)} %constant.32.clone.twist_ref) | copy-start | bytes 98308
  1.8 29.4 %copy-start.15 = (bf16[64,48]{1,0:T(8,128)(2,1)S(1)}, bf16[64,48]{1,0:T(8,128)(2,1)}, u32[]{:S(2)}) copy-start(bf16[64,48]{1,0:T(8,128)(2,1)} %constant.31.clone.first_ref) | copy-start | bytes 18436
  32.3 20.5 %all-to-all-start.1 = ((f32[16,24,128]{2,1,0:T(8,128)}), f32[16,24,128]{2,1,0:T(8,128)S(1)}, u32[]{:S(2)}, u32[]{:S(2)}) async-start(f32[16,24,128]{2,1,0:T(8,128)} %bitcast.4), calls=%async_computation.1 | async-start | bytes 393216 | tf_op jit(solution)/shard_map/all_to_all | solution.py:367
  52.8 8.8 %copy-start = (f32[6,4,4096]{2,1,0:T(4,128)S(1)}, f32[6,4,4096]{2,1,0:T(4,128)}, u32[]{:S(2)}) copy-start(f32[6,4,4096]{2,1,0:T(4,128)} %kern_ref.1) | copy-start | bytes 1179652
  54.3 16.3 %all-to-all-start.2 = ((f32[32,16,128]{2,1,0:T(8,128)}), f32[32,16,128]{2,1,0:T(8,128)S(1)}, u32[]{:S(2)}, u32[]{:S(2)}) async-start(f32[32,16,128]{2,1,0:T(8,128)} %bitcast.6), calls=%async_computation.2 | async-start | bytes 524288 | tf_op jit(solution)/shard_map/all_to_all | solution.py:367
  61.6 8.9 %copy-start.1 = (f32[2,192,128]{2,1,0:T(8,128)S(1)}, f32[2,192,128]{2,1,0:T(8,128)}, u32[]{:S(2)}) copy-start(f32[2,192,128]{2,1,0:T(8,128)} %constant.35.clone.twist_ref) | copy-start | bytes 589828
  61.6 8.9 %copy-start.6 = (bf16[256,128]{1,0:T(8,128)(2,1)S(1)}, bf16[256,128]{1,0:T(8,128)(2,1)}, u32[]{:S(2)}) copy-start(bf16[256,128]{1,0:T(8,128)(2,1)} %constant.37.clone.lead_ref) | copy-start | bytes 196612
  61.6 8.9 %copy-start.10 = (bf16[128,128]{1,0:T(8,128)(2,1)S(1)}, bf16[128,128]{1,0:T(8,128)(2,1)}, u32[]{:S(2)}) copy-start(bf16[128,128]{1,0:T(8,128)(2,1)} %constant.36.clone.last_ref) | copy-start | bytes 98308
  61.6 8.9 %copy-start.11 = (bf16[128,96]{1,0:T(8,128)(2,1)S(1)}, bf16[128,96]{1,0:T(8,128)(2,1)}, u32[]{:S(2)}) copy-start(bf16[128,96]{1,0:T(8,128)(2,1)} %constant.34.clone.first_ref) | copy-start | bytes 73732
  61.7 8.9 %copy-start.13 = (bf16[64,128]{1,0:T(8,128)(2,1)S(1)}, bf16[64,128]{1,0:T(8,128)(2,1)}, u32[]{:S(2)}) copy-start(bf16[64,128]{1,0:T(8,128)(2,1)} %constant.38.clone.back_ref) | copy-start | bytes 49156
  85.5 21.0 %copy-start.5 = (bf16[128,256]{1,0:T(8,128)(2,1)S(1)}, bf16[128,256]{1,0:T(8,128)(2,1)}, u32[]{:S(2)}) copy-start(bf16[128,256]{1,0:T(8,128)(2,1)} %constant.41.clone.last_ref) | copy-start | bytes 196612
  85.6 21.0 %copy-start.9 = (f32[2,32,128]{2,1,0:T(8,128)S(1)}, f32[2,32,128]{2,1,0:T(8,128)}, u32[]{:S(2)}) copy-start(f32[2,32,128]{2,1,0:T(8,128)} %constant.40.clone.twist_ref) | copy-start | bytes 98308
  85.6 20.9 %copy-start.14 = (bf16[64,96]{1,0:T(8,128)(2,1)S(1)}, bf16[64,96]{1,0:T(8,128)(2,1)}, u32[]{:S(2)}) copy-start(bf16[64,96]{1,0:T(8,128)(2,1)} %constant.39.clone.first_ref) | copy-start | bytes 36868
  107.0 19.8 %copy-start.4 = (f32[3,64,128]{2,1,0:T(8,128)S(1)}, f32[3,64,128]{2,1,0:T(8,128)}, u32[]{:S(2)}) copy-start(f32[3,64,128]{2,1,0:T(8,128)} %magnet_ref.3) | copy-start | bytes 294916
  107.0 19.7 %copy-start.8 = (f32[64,128]{1,0:T(8,128)S(1)}, f32[64,128]{1,0:T(8,128)}, u32[]{:S(2)}) copy-start(f32[64,128]{1,0:T(8,128)} %stiff_ref.3) | copy-start | bytes 98308
where the time goes:
time: 129 us; the launch traced here: 128 us
  blocking collectives  82.5 us (64%)
  waiting for transfers between devices  24.6 us (19%)
  starting transfers between devices  11.7 us (9%)
  Pallas kernels  7.58 us (6%)
  local copies, waits for them, and re-layouts  1.74 us (1%)
    all_to_all x4, blocking collectives, exchange(): lax.all_to_all(array, axis, split_axis=0, concat_axis=0, tiled=True)  82.5 us
    all_to_all x2, waiting for transfers between devices, exchange(): lax.all_to_all(array, axis, split_axis=0, concat_axis=0, tiled=True)  24.6 us
    all_to_all x2, starting transfers between devices, exchange(): lax.all_to_all(array, axis, split_axis=0, concat_axis=0, tiled=True)  11.7 us
    pallas_call x8, Pallas kernels, call(): pl.pallas_call(body, out_shape=shapes, in_specs=specs, out_specs=[in_vmem...  7.58 us
  transfers between devices with their start and end apart: 2, of which 2 were waited for; matrix products, arithmetic and copies ran while one was open for 0% of the time, Pallas kernels for 0%

commit v1 on v0

--- a/solution.py
+++ b/solution.py
@@ -1,4 +1,3 @@
-import functools
 import math
 
 import jax
@@ -122,7 +121,15 @@
     return lax.broadcasted_iota(jnp.int32, shape, len(shape) - 1)
 
 
-def pack_body(magnet_ref, stiff_ref, out_ref, edge_ref):
+def pack_body(magnet_hbm, stiff_hbm, out_ref, edge_ref, magnet_ref, stiff_ref, sems):
+    copies = [
+        pltpu.make_async_copy(magnet_hbm, magnet_ref, sems.at[0]),
+        pltpu.make_async_copy(stiff_hbm, stiff_ref, sems.at[1]),
+    ]
+    for copy in copies:
+        copy.start()
+    for copy in copies:
+        copy.wait()
     for a in range(3):
         for i in range(4):
             out_ref[pl.ds(4 * a + i, rows_n, stride=16), :] = magnet_ref[
@@ -139,19 +146,20 @@
     edge_ref[7:8, :] = stiff_ref[cells - 1 :, :]
 
 
-def kern_body(kern_ref, out_ref, held_ref):
+def spread_kern(kern_ref, held_ref):
     for j in range(6):
         for b in range(32):
             held_ref[pl.ds(j * 128 + b, 4, stride=32), :] = kern_ref[j, :, pl.ds(128 * b, 128)]
-    low = lane_index((128, 128)) < 64
+    low = lane_index((32, 128)) < 64
+    spread = []
     for j in range(6):
-        part = held_ref[pl.ds(j * 128, 128), :]
-        turned = half_turn(part)
-        even = jnp.where(low, part, turned)
-        odd = jnp.where(low, turned, part)
+        spread.append([])
         for k in range(4):
-            out_ref[j, k, 0:32, :] = even[32 * k : 32 * k + 32]
-            out_ref[j, k, 32:64, :] = odd[32 * k : 32 * k + 32]
+            part = held_ref[pl.ds(j * 128 + 32 * k, 32), :]
+            turned = half_turn(part)
+            halves = [jnp.where(low, part, turned), jnp.where(low, turned, part)]
+            spread[j].append(jnp.concatenate(halves, 0))
+    return spread
 
 
 def forward_rows_body(in_ref, first_ref, twist_ref, last_ref, out_ref):
@@ -171,7 +179,7 @@
             ]
 
 
-def forward_cols_body(place_ref, in_ref, edge_ref, out_ref):
+def forward_cols_body(in_ref, edge_ref, out_ref):
     lane = lane_index((rows_n, 128))
     for k2l in range(4):
         pieces = []
@@ -194,14 +202,14 @@
                 out_ref[pl.ds(128 * k2l + 4 * a + k, 8, stride=16), :] = turned[
                     32 * a + 8 * k : 32 * a + 8 * k + 8
                 ]
-    col = place_ref[1]
+    col = lax.axis_index("col")
     first, last = edge_ref[0:4, :], edge_ref[4:8, :]
     for c in range(cols_n):
         out_ref[16 * c + 12 : 16 * c + 16, :] = jnp.where(c > col, last, first)
 
 
 def spectral_body(
-    place_ref, in_ref, kern_ref, first_ref, twist_ref, last_ref, lead_ref, back_ref, out_ref
+    in_ref, kern_ref, first_ref, twist_ref, last_ref, lead_ref, back_ref, out_ref, held_ref
 ):
     columns = [in_ref[pl.ds(j, cols_n, stride=16), :] for j in range(12)]
     section = stacked_product(first_ref[...], jnp.concatenate(columns, 1))
@@ -216,13 +224,14 @@
         turned.append(block)
         turned.append(half_turn(block) * sign)
     freq = split_product(last_ref[...], jnp.concatenate(turned, 0), 1)
+    kern = spread_kern(kern_ref, held_ref)
     sources = []
     for target in range(3):
         for k in range(4):
             total = None
             for b in range(3):
                 j = 4 * b + k
-                term = kern_ref[tensor_slots[target][b], k] * freq[:, 128 * j : 128 * j + 128]
+                term = kern[tensor_slots[target][b]][k] * freq[:, 128 * j : 128 * j + 128]
                 total = term if total is None else total + term
             sources.append(jnp.concatenate([total, -half_turn(total) * sign], 0))
     section = split_product(lead_ref[...], jnp.concatenate(sources, 1), 0)
@@ -235,7 +244,7 @@
     scale = -1.0 / (length * length)
     lane = lane_index((cols_n, 128))
     zero_weight = jnp.where((lane // 4) % 2 == 0, 1.0, 0.0).astype(f32)
-    is_zero = jnp.logical_and(place_ref[0] == 0, place_ref[1] == 0)
+    is_zero = jnp.logical_and(lax.axis_index("row") == 0, lax.axis_index("col") == 0)
     for j in range(12):
         block = result[:, 128 * j : 128 * j + 128]
         weight = jnp.full((cols_n, 128), 2.0, f32)
@@ -286,8 +295,8 @@
     )
 
 
-def torque_body(place_ref, in_ref, magnet_ref, stiff_ref, beside_y_ref, beside_x_ref, out_ref, field_ref):
-    row, col = place_ref[0], place_ref[1]
+def torque_body(in_ref, magnet_ref, stiff_ref, beside_y_ref, beside_x_ref, out_ref, field_ref):
+    row, col = lax.axis_index("row"), lax.axis_index("col")
     group = lane_index((rows_n, 128)) // 32
     for a in range(3):
         tiles = [in_ref[pl.ds(4 * a + y2, rows_n, stride=16), :] for y2 in range(4)]
@@ -344,16 +353,15 @@
 
 
 in_vmem = pl.BlockSpec(memory_space=pltpu.VMEM)
-in_smem = pl.BlockSpec(memory_space=pltpu.SMEM)
-
-
-def call(body, out_shapes, *args, scratch=(), place=False, flops=10**8):
+in_any = pl.BlockSpec(memory_space=pl.ANY)
+
+
+def call(body, out_shapes, *args, scratch=(), in_spec=in_vmem, flops=10**8):
     shapes = [jax.ShapeDtypeStruct(shape, f32) for shape in out_shapes]
-    specs = [in_smem if place and n == 0 else in_vmem for n in range(len(args))]
     return pl.pallas_call(
         body,
         out_shape=shapes,
-        in_specs=specs,
+        in_specs=[in_spec] * len(args),
         out_specs=[in_vmem] * len(shapes),
         scratch_shapes=list(scratch),
         compiler_params=pltpu.CompilerParams(vmem_limit_bytes=48 * 1024 * 1024),
@@ -369,18 +377,30 @@
 
 def local(magnet, stiffness, kern):
     constant = {name: [jnp.asarray(t) for t in group] for name, group in tables().items()}
-    place = jnp.stack([lax.axis_index("row"), lax.axis_index("col")]).astype(jnp.int32)
-    packed, edge = call(pack_body, [(256, 128), (8, 128)], magnet, stiffness)
-    (spread,) = call(
-        kern_body, [(6, 4, 64, 128)], kern, scratch=[pltpu.VMEM((768, 128), f32)]
+    packed, edge = call(
+        pack_body,
+        [(256, 128), (8, 128)],
+        magnet,
+        stiffness,
+        in_spec=in_any,
+        scratch=[
+            pltpu.VMEM((3, cells, lanes), f32),
+            pltpu.VMEM((cells, lanes), f32),
+            pltpu.SemaphoreType.DMA((2,)),
+        ],
     )
     lines = exchange(packed, "row", rows_n)
     (along_y,) = call(forward_rows_body, [(384, 128)], lines, *constant["y"])
     along_y = exchange(along_y, "row", rows_n)
-    (columns,) = call(forward_cols_body, [(512, 128)], place, along_y, edge, place=True)
+    (columns,) = call(forward_cols_body, [(512, 128)], along_y, edge)
     columns = exchange(columns, "col", cols_n)
     (inverse_x,) = call(
-        spectral_body, [(512, 128)], place, columns, spread, *constant["x"], place=True
+        spectral_body,
+        [(512, 128)],
+        columns,
+        kern,
+        *constant["x"],
+        scratch=[pltpu.VMEM((768, 128), f32)],
     )
     inverse_x = exchange(inverse_x, "col", cols_n)
     (coef,) = call(back_cols_body, [(384, 128)], inverse_x)
@@ -390,13 +410,11 @@
     (torque,) = call(
         torque_body,
         [(3, 64, 128)],
-        place,
         field,
         magnet,
         stiffness,
         lines,
         columns,
-        place=True,
         scratch=[pltpu.VMEM((3, 64, 128), f32)],
     )
     return torque

time: 129 us -> 126 us (0.977)
  blocking collectives: 82.5 us -> 119 us
  waiting for transfers between devices: 24.6 us -> 0 us
  starting transfers between devices: 11.7 us -> 0 us
  Pallas kernels: 7.58 us -> 4.69 us
    all_to_all x4 -> x6, blocking collectives: 82.5 us -> 119 us  [exchange(): lax.all_to_all(array, axis, split_axis=0, concat_axis=0, tiled=True)]
    all_to_all x2 -> x0, waiting for transfers between devices: 24.6 us -> none  [exchange(): lax.all_to_all(array, axis, split_axis=0, concat_axis=0, tiled=True)]
    all_to_all x2 -> x0, starting transfers between devices: 11.7 us -> none  [exchange(): lax.all_to_all(array, axis, split_axis=0, concat_axis=0, tiled=True)]
    pallas_call x8 -> x7, Pallas kernels: 7.58 us -> 4.69 us  [call(): pl.pallas_call(body, out_shape=shapes, in_specs=[in_spec] * len(args), ou...]
  transfers between devices with their start and end apart: 2 -> 0, of which waited for: 2 -> 0; matrix products, arithmetic and copies ran while one was open for 0% -> 0% of each run, Pallas kernels for 0% -> 0%
where the time goes in v1:
time: 126 us
  blocking collectives  119 us (94%)
  Pallas kernels  4.69 us (4%)
  local copies, waits for them, and re-layouts  1.74 us (1%)
    all_to_all x6, blocking collectives, exchange(): lax.all_to_all(array, axis, split_axis=0, concat_axis=0, tiled=True)  119 us
    pallas_call x7, Pallas kernels, call(): pl.pallas_call(body, out_shape=shapes, in_specs=[in_spec] * len(args), ou...  4.69 us

profile of v1, /device:TPU:32, one launch (start us, length us, event | category | flops | bytes accessed | tf_op | source)
XLA Modules:
  0.0 125.6 jit_solution(3788857401569003086)
XLA Ops:
  0.0 0.0 copy-start.3
  0.0 0.9 copy-done.3
  0.9 0.0 copy-start.7
  0.9 0.8 copy-done.7
  1.7 0.3 shard_map.136
  2.0 0.0 copy-start.2
  2.0 0.0 copy-start.12
  2.0 0.0 copy-start.15
  2.0 29.3 %all_to_all.30 = f32[16,16,128]{2,1,0:T(8,128)S(1)} all-to-all(f32[16,16,128]{2,1,0:T(8,128)S(1)} %bitcast.25), channel_id=1, replica_groups=mesh['row'=16,'col'=32] {'row'}, dimensions={0} | all-to-all | bytes 262144 | tf_op jit(solution)/shard_map/all_to_all | solution.py:375
  31.3 0.0 copy-done.2
  31.3 0.0 copy-done.12
  31.3 0.0 copy-done.15
  31.3 0.5 shard_map.137
  31.8 20.3 %all_to_all.31 = f32[16,24,128]{2,1,0:T(8,128)S(1)} all-to-all(f32[16,24,128]{2,1,0:T(8,128)S(1)} %bitcast.22), channel_id=1, replica_groups=mesh['row'=16,'col'=32] {'row'}, dimensions={0} | all-to-all | bytes 393216 | tf_op jit(solution)/shard_map/all_to_all | solution.py:375
  52.1 0.0 copy-start
  52.1 0.2 shard_map.138
  52.3 0.0 copy-start.1
  52.3 0.0 copy-start.6
  52.4 0.0 copy-start.10
  52.4 0.0 copy-start.11
  52.4 0.0 copy-start.13
  52.4 16.2 %all_to_all.32 = f32[32,16,128]{2,1,0:T(8,128)S(1)} all-to-all(f32[32,16,128]{2,1,0:T(8,128)S(1)} %bitcast.17), channel_id=1, replica_groups=mesh['row'=16,'col'=32] {'col'}, dimensions={0} | all-to-all | bytes 524288 | tf_op jit(solution)/shard_map/all_to_all | solution.py:375
  68.6 0.0 copy-done
  68.6 0.0 copy-done.1
  68.6 0.0 copy-done.6
  68.6 0.0 copy-done.10
  68.6 0.0 copy-done.11
  68.6 0.0 copy-done.13
  68.6 2.1 %shard_map.139 = f32[512,128]{1,0:T(8,128)S(1)} custom-call(f32[512,128]{1,0:T(8,128)S(1)} %bitcast.12, f32[6,4,4096]{2,1,0:T(4,128)S(1)} %copy-done, bf16[128,96]{1,0:T(8,128)(2,1)S(1)} %copy-done.11, f32[2,192,128]{2,1,0:T(8,128)S(1)} %copy-done.1, bf16[128,128]{1,0:T(8,128)(2,1)S(1)} %copy-done.10, bf16[256,128]{1,0:T(8,128)(2,1)S(1)} %copy-done.6, ...), custom_call_target="tpu_custom_call" | custom-call | flops 100000000 | bytes 1000000 | tf_op jit(solution)/shard_map/pallas_call | solution.py:361
  70.7 12.5 %all_to_all.33 = f32[32,16,128]{2,1,0:T(8,128)S(1)} all-to-all(f32[32,16,128]{2,1,0:T(8,128)S(1)} %bitcast.16), channel_id=1, replica_groups=mesh['row'=16,'col'=32] {'col'}, dimensions={0} | all-to-all | bytes 524288 | tf_op jit(solution)/shard_map/all_to_all | solution.py:375
  83.2 0.1 shard_map.140
  83.3 0.0 copy-start.5
  83.3 0.0 copy-start.9
  83.4 0.0 copy-start.14
  83.4 20.9 %all_to_all.34 = f32[16,24,128]{2,1,0:T(8,128)S(1)} all-to-all(f32[16,24,128]{2,1,0:T(8,128)S(1)} %bitcast.21), channel_id=1, replica_groups=mesh['row'=16,'col'=32] {'row'}, dimensions={0} | all-to-all | bytes 393216 | tf_op jit(solution)/shard_map/all_to_all | solution.py:375
  104.3 0.0 copy-done.5
  104.3 0.0 copy-done.9
  104.3 0.0 copy-done.14
  104.3 0.4 shard_map.141
  104.8 0.0 copy-start.4
  104.8 0.0 copy-start.8
  104.8 19.7 %all_to_all.35 = f32[16,16,128]{2,1,0:T(8,128)S(1)} all-to-all(f32[16,16,128]{2,1,0:T(8,128)S(1)} %bitcast.23), channel_id=1, replica_groups=mesh['row'=16,'col'=32] {'row'}, dimensions={0} | all-to-all | bytes 262144 | tf_op jit(solution)/shard_map/all_to_all | solution.py:375
  124.5 0.0 copy-done.4
  124.5 0.0 copy-done.8
  124.5 1.0 shard_map.142
Async XLA Ops:
  0.0 0.9 copy-start.3
  0.9 0.8 copy-start.7
  2.0 29.4 %copy-start.2 = (bf16[256,256]{1,0:T(8,128)(2,1)S(1)}, bf16[256,256]{1,0:T(8,128)(2,1)}, u32[]{:S(2)}) copy-start(bf16[256,256]{1,0:T(8,128)(2,1)} %constant.24.clone.last_ref) | copy-start | bytes 393220
  2.0 29.4 %copy-start.12 = (f32[2,32,128]{2,1,0:T(8,128)S(1)}, f32[2,32,128]{2,1,0:T(8,128)}, u32[]{:S(2)}) copy-start(f32[2,32,128]{2,1,0:T(8,128)} %constant.23.clone.twist_ref) | copy-start | bytes 98308
  2.0 29.4 %copy-start.15 = (bf16[64,48]{1,0:T(8,128)(2,1)S(1)}, bf16[64,48]{1,0:T(8,128)(2,1)}, u32[]{:S(2)}) copy-start(bf16[64,48]{1,0:T(8,128)(2,1)} %constant.22.clone.first_ref) | copy-start | bytes 18436
  52.1 16.5 %copy-start = (f32[6,4,4096]{2,1,0:T(4,128)S(1)}, f32[6,4,4096]{2,1,0:T(4,128)}, u32[]{:S(2)}) copy-start(f32[6,4,4096]{2,1,0:T(4,128)} %kern_ref.1) | copy-start | bytes 1179652
  52.3 16.3 %copy-start.1 = (f32[2,192,128]{2,1,0:T(8,128)S(1)}, f32[2,192,128]{2,1,0:T(8,128)}, u32[]{:S(2)}) copy-start(f32[2,192,128]{2,1,0:T(8,128)} %constant.26.clone.twist_ref) | copy-start | bytes 589828
  52.3 16.2 %copy-start.6 = (bf16[256,128]{1,0:T(8,128)(2,1)S(1)}, bf16[256,128]{1,0:T(8,128)(2,1)}, u32[]{:S(2)}) copy-start(bf16[256,128]{1,0:T(8,128)(2,1)} %constant.28.clone.lead_ref) | copy-start | bytes 196612
  52.4 16.2 %copy-start.10 = (bf16[128,128]{1,0:T(8,128)(2,1)S(1)}, bf16[128,128]{1,0:T(8,128)(2,1)}, u32[]{:S(2)}) copy-start(bf16[128,128]{1,0:T(8,128)(2,1)} %constant.27.clone.last_ref) | copy-start | bytes 98308
  52.4 16.2 %copy-start.11 = (bf16[128,96]{1,0:T(8,128)(2,1)S(1)}, bf16[128,96]{1,0:T(8,128)(2,1)}, u32[]{:S(2)}) copy-start(bf16[128,96]{1,0:T(8,128)(2,1)} %constant.25.clone.first_ref) | copy-start | bytes 73732
  52.4 16.2 %copy-start.13 = (bf16[64,128]{1,0:T(8,128)(2,1)S(1)}, bf16[64,128]{1,0:T(8,128)(2,1)}, u32[]{:S(2)}) copy-start(bf16[64,128]{1,0:T(8,128)(2,1)} %constant.29.clone.back_ref) | copy-start | bytes 49156
  83.3 21.0 %copy-start.5 = (bf16[128,256]{1,0:T(8,128)(2,1)S(1)}, bf16[128,256]{1,0:T(8,128)(2,1)}, u32[]{:S(2)}) copy-start(bf16[128,256]{1,0:T(8,128)(2,1)} %constant.32.clone.last_ref) | copy-start | bytes 196612
  83.3 21.0 %copy-start.9 = (f32[2,32,128]{2,1,0:T(8,128)S(1)}, f32[2,32,128]{2,1,0:T(8,128)}, u32[]{:S(2)}) copy-start(f32[2,32,128]{2,1,0:T(8,128)} %constant.31.clone.twist_ref) | copy-start | bytes 98308
  83.4 21.0 %copy-start.14 = (bf16[64,96]{1,0:T(8,128)(2,1)S(1)}, bf16[64,96]{1,0:T(8,128)(2,1)}, u32[]{:S(2)}) copy-start(bf16[64,96]{1,0:T(8,128)(2,1)} %constant.30.clone.first_ref) | copy-start | bytes 36868
  104.8 19.8 %copy-start.4 = (f32[3,64,128]{2,1,0:T(8,128)S(1)}, f32[3,64,128]{2,1,0:T(8,128)}, u32[]{:S(2)}) copy-start(f32[3,64,128]{2,1,0:T(8,128)} %magnet_ref.1) | copy-start | bytes 294916
  104.8 19.7 %copy-start.8 = (f32[64,128]{1,0:T(8,128)S(1)}, f32[64,128]{1,0:T(8,128)}, u32[]{:S(2)}) copy-start(f32[64,128]{1,0:T(8,128)} %stiff_ref.1) | copy-start | bytes 98308

commit v2 on v1

--- a/solution.py
+++ b/solution.py
@@ -132,13 +132,14 @@
         copy.wait()
     for a in range(3):
         for i in range(4):
-            out_ref[pl.ds(4 * a + i, rows_n, stride=16), :] = magnet_ref[
+            out_ref[pl.ds(4 * a + i, rows_n, stride=14), :] = magnet_ref[
                 a, pl.ds(i, rows_n, stride=4), :
             ]
     former = jnp.concatenate([magnet_ref[0], magnet_ref[1]], 0).T
     latter = jnp.concatenate([magnet_ref[2], stiff_ref[...]], 0).T
-    for row, piece in enumerate((former[:1], latter[:1], former[127:], latter[127:])):
-        out_ref[pl.ds(12 + row, rows_n, stride=16), :] = jnp.broadcast_to(piece, (rows_n, lanes))
+    after = lax.broadcasted_iota(jnp.int32, (rows_n, lanes), 0) > lax.axis_index("row")
+    for n, sides in enumerate((former, latter)):
+        out_ref[pl.ds(12 + n, rows_n, stride=14), :] = jnp.where(after, sides[127:], sides[:1])
     for a in range(3):
         edge_ref[a : a + 1, :] = magnet_ref[a, :1, :]
         edge_ref[4 + a : 5 + a, :] = magnet_ref[a, cells - 1 :, :]
@@ -163,7 +164,7 @@
 
 
 def forward_rows_body(in_ref, first_ref, twist_ref, last_ref, out_ref):
-    lines = [in_ref[pl.ds(4 * a + i, rows_n, stride=16), :] for i in range(4) for a in range(3)]
+    lines = [in_ref[pl.ds(4 * a + i, rows_n, stride=14), :] for i in range(4) for a in range(3)]
     section = stacked_product(first_ref[...], jnp.concatenate(lines, 1))
     cos, sin = twist_ref[0], twist_ref[1]
     turned = []
@@ -250,14 +251,12 @@
         weight = jnp.full((cols_n, 128), 2.0, f32)
         if j % 4 == 0:
             weight = jnp.where(is_zero, zero_weight, weight)
-        out_ref[pl.ds(j, cols_n, stride=16), :] = block * (weight * scale)
-    for j in range(12, 16):
-        out_ref[pl.ds(j, cols_n, stride=16), :] = jnp.zeros((cols_n, 128), f32)
+        out_ref[pl.ds(j, cols_n, stride=12), :] = block * (weight * scale)
 
 
 def back_cols_body(in_ref, out_ref):
     for a in range(3):
-        block = [in_ref[pl.ds(4 * a + k, cols_n, stride=16), :] for k in range(4)]
+        block = [in_ref[pl.ds(4 * a + k, cols_n, stride=12), :] for k in range(4)]
         turned = jnp.concatenate(block, 0).T
         for r in range(rows_n):
             out_ref[24 * r + 8 * a : 24 * r + 8 * a + 8, :] = turned[8 * r : 8 * r + 8]
@@ -280,11 +279,9 @@
     result = split_product(last_ref[...], jnp.concatenate(turned, 0), 1)
     for a in range(3):
         for y2 in range(4):
-            out_ref[pl.ds(4 * a + y2, rows_n, stride=16), :] = result[
+            out_ref[pl.ds(4 * a + y2, rows_n, stride=12), :] = result[
                 16 * y2 : 16 * y2 + 16, 128 * a : 128 * a + 128
             ]
-    for j in range(12, 16):
-        out_ref[pl.ds(j, rows_n, stride=16), :] = jnp.zeros((rows_n, 128), f32)
 
 
 def cross(former, latter):
@@ -299,7 +296,7 @@
     row, col = lax.axis_index("row"), lax.axis_index("col")
     group = lane_index((rows_n, 128)) // 32
     for a in range(3):
-        tiles = [in_ref[pl.ds(4 * a + y2, rows_n, stride=16), :] for y2 in range(4)]
+        tiles = [in_ref[pl.ds(4 * a + y2, rows_n, stride=12), :] for y2 in range(4)]
         for i in range(4):
             line = None
             for y2 in range(4):
@@ -307,11 +304,11 @@
                 piece = tiles[y2] if shift == 0 else pltpu.roll(tiles[y2], shift, 1)
                 line = piece if line is None else jnp.where(group == y2, piece, line)
             field_ref[a, pl.ds(i, rows_n, stride=4), :] = line
-    before_y = beside_y_ref[pl.ds(pl.multiple_of(16 * jnp.maximum(row - 1, 0), 16), 16), :]
-    after_y = beside_y_ref[pl.ds(pl.multiple_of(16 * jnp.minimum(row + 1, rows_n - 1), 16), 16), :]
+    before_y = beside_y_ref[pl.ds(14 * jnp.maximum(row - 1, 0) + 12, 2), :]
+    after_y = beside_y_ref[pl.ds(14 * jnp.minimum(row + 1, rows_n - 1) + 12, 2), :]
     before_x = beside_x_ref[pl.ds(pl.multiple_of(16 * jnp.maximum(col - 1, 0), 16), 16), :]
     after_x = beside_x_ref[pl.ds(pl.multiple_of(16 * jnp.minimum(col + 1, cols_n - 1), 16), 16), :]
-    edges = jnp.concatenate([before_y[14:16], after_y[12:14], jnp.zeros((124, 128), f32)], 0).T
+    edges = jnp.concatenate([before_y, after_y, jnp.zeros((124, 128), f32)], 0).T
     stack = [magnet_ref[0], magnet_ref[1], magnet_ref[2], stiff_ref[...]]
     lane = lane_index((cells, 128))
     sub = lax.broadcasted_iota(jnp.int32, (cells, 128), 0)
@@ -353,10 +350,10 @@
 
 
 in_vmem = pl.BlockSpec(memory_space=pltpu.VMEM)
-in_any = pl.BlockSpec(memory_space=pl.ANY)
-
-
-def call(body, out_shapes, *args, scratch=(), in_spec=in_vmem, flops=10**8):
+in_hbm = pl.BlockSpec(memory_space=pltpu.HBM)
+
+
+def call(body, out_shapes, *args, scratch=(), in_spec=in_vmem, vmem=32 * 2**20, flops=10**8):
     shapes = [jax.ShapeDtypeStruct(shape, f32) for shape in out_shapes]
     return pl.pallas_call(
         body,
@@ -364,14 +361,16 @@
         in_specs=[in_spec] * len(args),
         out_specs=[in_vmem] * len(shapes),
         scratch_shapes=list(scratch),
-        compiler_params=pltpu.CompilerParams(vmem_limit_bytes=48 * 1024 * 1024),
+        compiler_params=pltpu.CompilerParams(vmem_limit_bytes=vmem),
         cost_estimate=pl.CostEstimate(flops=flops, bytes_accessed=10**6, transcendentals=0),
     )(*args)
 
 
 def exchange(array, axis, chunks):
     shape = array.shape
-    array = array.reshape(chunks, shape[0] // chunks, shape[1])
+    rows = shape[0] // chunks
+    tile = math.gcd(rows, 8)
+    array = array.reshape(chunks, rows // tile, tile, shape[1])
     return lax.all_to_all(array, axis, split_axis=0, concat_axis=0, tiled=True).reshape(shape)
 
 
@@ -379,10 +378,11 @@
     constant = {name: [jnp.asarray(t) for t in group] for name, group in tables().items()}
     packed, edge = call(
         pack_body,
-        [(256, 128), (8, 128)],
+        [(224, 128), (8, 128)],
         magnet,
         stiffness,
-        in_spec=in_any,
+        in_spec=in_hbm,
+        vmem=60 * 2**20,
         scratch=[
             pltpu.VMEM((3, cells, lanes), f32),
             pltpu.VMEM((cells, lanes), f32),
@@ -396,7 +396,7 @@
     columns = exchange(columns, "col", cols_n)
     (inverse_x,) = call(
         spectral_body,
-        [(512, 128)],
+        [(384, 128)],
         columns,
         kern,
         *constant["x"],
@@ -405,7 +405,7 @@
     inverse_x = exchange(inverse_x, "col", cols_n)
     (coef,) = call(back_cols_body, [(384, 128)], inverse_x)
     coef = exchange(coef, "row", rows_n)
-    (field,) = call(back_rows_body, [(256, 128)], coef, *constant["z"])
+    (field,) = call(back_rows_body, [(192, 128)], coef, *constant["z"])
     field = exchange(field, "row", rows_n)
     (torque,) = call(
         torque_body,

time: 126 us -> 123 us (0.976)
  blocking collectives: 119 us -> 117 us
  local copies, waits for them, and re-layouts: 1.74 us -> 0.1 us
  Pallas kernels: 4.69 us -> 6.01 us
    all_to_all x6, blocking collectives: 119 us -> 117 us  [exchange(): lax.all_to_all(array, axis, split_axis=0, concat_axis=0, tiled=True)]
    unnamed x32 -> x30, local copies, waits for them, and re-layouts: 1.74 us -> 0.1 us
    pallas_call x7, Pallas kernels: 4.69 us -> 6.01 us  [call(): pl.pallas_call(body, out_shape=shapes, in_specs=[in_spec] * len(args), ou...]
where the time goes in v2:
time: 123 us
  blocking collectives  117 us (95%)
  Pallas kernels  6.01 us (5%)
    all_to_all x6, blocking collectives, exchange(): lax.all_to_all(array, axis, split_axis=0, concat_axis=0, tiled=True)  117 us
    pallas_call x7, Pallas kernels, call(): pl.pallas_call(body, out_shape=shapes, in_specs=[in_spec] * len(args), ou...  6.01 us

profile of v2, /device:TPU:32, one launch (start us, length us, event | category | flops | bytes accessed | tf_op | source)
XLA Modules:
  0.0 122.9 jit_solution(2273092409838384573)
XLA Ops:
  0.0 1.7 %shard_map.136 = (f32[224,128]{1,0:T(8,128)}, f32[8,128]{1,0:T(8,128)}) custom-call(f32[3,64,128]{2,1,0:T(8,128)} %magnet_ref.1, f32[64,128]{1,0:T(8,128)} %stiff_ref.1), custom_call_target="tpu_custom_call" | custom-call | flops 100000000 | bytes 1000000 | tf_op jit(solution)/shard_map/pallas_call | solution.py:358
  1.7 0.0 copy-start.2
  1.7 0.0 copy-start.10
  1.7 0.0 copy-start.13
  1.7 28.9 %all_to_all.30 = f32[16,7,2,128]{3,2,1,0:T(2,128)S(1)} all-to-all(f32[16,7,2,128]{3,2,1,0:T(2,128)} %bitcast.25), channel_id=1, replica_groups=mesh['row'=16,'col'=32] {'row'}, dimensions={0} | all-to-all | bytes 229376 | tf_op jit(solution)/shard_map/all_to_all | solution.py:374
  30.6 0.0 copy-done.2
  30.6 0.0 copy-done.10
  30.6 0.0 copy-done.13
  30.6 0.4 shard_map.137
  31.1 0.0 copy-start.14
  31.1 19.3 %all_to_all.31 = f32[16,3,8,128]{3,2,1,0:T(8,128)S(1)} all-to-all(f32[16,3,8,128]{3,2,1,0:T(8,128)S(1)} %bitcast.22), channel_id=1, replica_groups=mesh['row'=16,'col'=32] {'row'}, dimensions={0} | all-to-all | bytes 393216 | tf_op jit(solution)/shard_map/all_to_all | solution.py:374
  50.4 0.0 copy-done.14
  50.4 0.0 copy-start
  50.4 0.2 shard_map.138
  50.6 0.0 copy-start.1
  50.6 0.0 copy-start.5
  50.6 0.0 copy-start.8
  50.7 0.0 copy-start.9
  50.7 0.0 copy-start.11
  50.7 16.2 %all_to_all.32 = f32[32,2,8,128]{3,2,1,0:T(8,128)S(1)} all-to-all(f32[32,2,8,128]{3,2,1,0:T(8,128)S(1)} %bitcast.14), channel_id=1, replica_groups=mesh['row'=16,'col'=32] {'col'}, dimensions={0} | all-to-all | bytes 524288 | tf_op jit(solution)/shard_map/all_to_all | solution.py:374
  66.9 0.0 copy-done
  66.9 0.0 copy-done.1
  66.9 0.0 copy-done.5
  66.9 0.0 copy-done.8
  66.9 0.0 copy-done.9
  66.9 0.0 copy-done.11
  66.9 2.1 %shard_map.139 = f32[384,128]{1,0:T(8,128)S(1)} custom-call(f32[512,128]{1,0:T(8,128)S(1)} %bitcast.12, f32[6,4,4096]{2,1,0:T(4,128)S(1)} %copy-done, bf16[128,96]{1,0:T(8,128)(2,1)S(1)} %copy-done.9, f32[2,192,128]{2,1,0:T(8,128)S(1)} %copy-done.1, bf16[128,128]{1,0:T(8,128)(2,1)S(1)} %copy-done.8, bf16[256,128]{1,0:T(8,128)(2,1)S(1)} %copy-done.5, ...), custom_call_target="tpu_custom_call" | custom-call | flops 100000000 | bytes 1000000 | tf_op jit(solution)/shard_map/pallas_call | solution.py:358
  69.0 11.9 %all_to_all.33 = f32[32,3,4,128]{3,2,1,0:T(4,128)S(1)} all-to-all(f32[32,3,4,128]{3,2,1,0:T(4,128)S(1)} %bitcast.17), channel_id=1, replica_groups=mesh['row'=16,'col'=32] {'col'}, dimensions={0} | all-to-all | bytes 393216 | tf_op jit(solution)/shard_map/all_to_all | solution.py:374
  80.9 0.1 shard_map.140
  81.0 0.0 copy-start.4
  81.0 0.0 copy-start.7
  81.0 0.0 copy-start.12
  81.0 22.0 %all_to_all.34 = f32[16,3,8,128]{3,2,1,0:T(8,128)S(1)} all-to-all(f32[16,3,8,128]{3,2,1,0:T(8,128)S(1)} %bitcast.21), channel_id=1, replica_groups=mesh['row'=16,'col'=32] {'row'}, dimensions={0} | all-to-all | bytes 393216 | tf_op jit(solution)/shard_map/all_to_all | solution.py:374
  103.0 0.0 copy-done.4
  103.0 0.0 copy-done.7
  103.0 0.0 copy-done.12
  103.0 0.4 shard_map.141
  103.5 0.0 copy-start.3
  103.5 0.0 copy-start.6
  103.5 18.4 %all_to_all.35 = f32[16,3,4,128]{3,2,1,0:T(4,128)S(1)} all-to-all(f32[16,3,4,128]{3,2,1,0:T(4,128)S(1)} %bitcast.23), channel_id=1, replica_groups=mesh['row'=16,'col'=32] {'row'}, dimensions={0} | all-to-all | bytes 196608 | tf_op jit(solution)/shard_map/all_to_all | solution.py:374
  121.9 0.0 copy-done.3
  121.9 0.0 copy-done.6
  121.9 1.0 shard_map.142
Async XLA Ops:
  1.7 29.0 %copy-start.2 = (bf16[256,256]{1,0:T(8,128)(2,1)S(1)}, bf16[256,256]{1,0:T(8,128)(2,1)}, u32[]{:S(2)}) copy-start(bf16[256,256]{1,0:T(8,128)(2,1)} %constant.24.clone.last_ref) | copy-start | bytes 393220
  1.7 29.0 %copy-start.10 = (f32[2,32,128]{2,1,0:T(8,128)S(1)}, f32[2,32,128]{2,1,0:T(8,128)}, u32[]{:S(2)}) copy-start(f32[2,32,128]{2,1,0:T(8,128)} %constant.23.clone.twist_ref) | copy-start | bytes 98308
  1.7 28.9 %copy-start.13 = (bf16[64,48]{1,0:T(8,128)(2,1)S(1)}, bf16[64,48]{1,0:T(8,128)(2,1)}, u32[]{:S(2)}) copy-start(bf16[64,48]{1,0:T(8,128)(2,1)} %constant.22.clone.first_ref) | copy-start | bytes 18436
  31.1 19.3 %copy-start.14 = (f32[8,128]{1,0:T(8,128)S(1)}, f32[8,128]{1,0:T(8,128)}, u32[]{:S(2)}) copy-start(f32[8,128]{1,0:T(8,128)} %get-tuple-element.8.edge_ref) | copy-start | bytes 12292
  50.4 16.5 %copy-start = (f32[6,4,4096]{2,1,0:T(4,128)S(1)}, f32[6,4,4096]{2,1,0:T(4,128)}, u32[]{:S(2)}) copy-start(f32[6,4,4096]{2,1,0:T(4,128)} %kern_ref.1) | copy-start | bytes 1179652
  50.6 16.2 %copy-start.1 = (f32[2,192,128]{2,1,0:T(8,128)S(1)}, f32[2,192,128]{2,1,0:T(8,128)}, u32[]{:S(2)}) copy-start(f32[2,192,128]{2,1,0:T(8,128)} %constant.26.clone.twist_ref) | copy-start | bytes 589828
  50.6 16.2 %copy-start.5 = (bf16[256,128]{1,0:T(8,128)(2,1)S(1)}, bf16[256,128]{1,0:T(8,128)(2,1)}, u32[]{:S(2)}) copy-start(bf16[256,128]{1,0:T(8,128)(2,1)} %constant.28.clone.lead_ref) | copy-start | bytes 196612
  50.6 16.2 %copy-start.8 = (bf16[128,128]{1,0:T(8,128)(2,1)S(1)}, bf16[128,128]{1,0:T(8,128)(2,1)}, u32[]{:S(2)}) copy-start(bf16[128,128]{1,0:T(8,128)(2,1)} %constant.27.clone.last_ref) | copy-start | bytes 98308
  50.7 16.2 %copy-start.9 = (bf16[128,96]{1,0:T(8,128)(2,1)S(1)}, bf16[128,96]{1,0:T(8,128)(2,1)}, u32[]{:S(2)}) copy-start(bf16[128,96]{1,0:T(8,128)(2,1)} %constant.25.clone.first_ref) | copy-start | bytes 73732
  50.7 16.2 %copy-start.11 = (bf16[64,128]{1,0:T(8,128)(2,1)S(1)}, bf16[64,128]{1,0:T(8,128)(2,1)}, u32[]{:S(2)}) copy-start(bf16[64,128]{1,0:T(8,128)(2,1)} %constant.29.clone.back_ref) | copy-start | bytes 49156
  81.0 22.0 %copy-start.4 = (bf16[128,256]{1,0:T(8,128)(2,1)S(1)}, bf16[128,256]{1,0:T(8,128)(2,1)}, u32[]{:S(2)}) copy-start(bf16[128,256]{1,0:T(8,128)(2,1)} %constant.32.clone.last_ref) | copy-start | bytes 196612
  81.0 22.0 %copy-start.7 = (f32[2,32,128]{2,1,0:T(8,128)S(1)}, f32[2,32,128]{2,1,0:T(8,128)}, u32[]{:S(2)}) copy-start(f32[2,32,128]{2,1,0:T(8,128)} %constant.31.clone.twist_ref) | copy-start | bytes 98308
  81.0 22.0 %copy-start.12 = (bf16[64,96]{1,0:T(8,128)(2,1)S(1)}, bf16[64,96]{1,0:T(8,128)(2,1)}, u32[]{:S(2)}) copy-start(bf16[64,96]{1,0:T(8,128)(2,1)} %constant.30.clone.first_ref) | copy-start | bytes 36868
  103.5 18.4 %copy-start.3 = (f32[3,64,128]{2,1,0:T(8,128)S(1)}, f32[3,64,128]{2,1,0:T(8,128)}, u32[]{:S(2)}) copy-start(f32[3,64,128]{2,1,0:T(8,128)} %magnet_ref.1) | copy-start | bytes 294916
  103.5 18.4 %copy-start.6 = (f32[64,128]{1,0:T(8,128)S(1)}, f32[64,128]{1,0:T(8,128)}, u32[]{:S(2)}) copy-start(f32[64,128]{1,0:T(8,128)} %stiff_ref.1) | copy-start | bytes 98308

commit v3 on v2

v3 whole, which is shorter than its diff:
```python
import math

import jax
import jax.numpy as jnp
import ml_dtypes
import numpy as np
from jax import lax
from jax.experimental import pallas as pl
from jax.experimental.pallas import tpu as pltpu
from jax.sharding import PartitionSpec as P

damping = 0.3
anisotropy = 0.8
tensor_slots = ((0, 3, 4), (3, 1, 5), (4, 5, 2))

rows_n = 16
cols_n = 32
cells = 64
lanes = 128
length = 4096
bf16 = jnp.bfloat16
f32 = jnp.float32


modes = 16


def wave(first, second, period):
    angle = 2.0 * math.pi * (np.outer(first, second) % period) / period
    return np.cos(angle), np.sin(angle)


def split_table(table):
    high = table.astype(ml_dtypes.bfloat16)
    low = (table - high.astype(np.float64)).astype(ml_dtypes.bfloat16)
    return high, low


def thick(table):
    high, low = split_table(table)
    return np.concatenate([high, low, high], 1)


def tall(table):
    return np.concatenate(split_table(table), 0)


def deep(table):
    high, low = split_table(table)
    return np.concatenate(
        [np.concatenate([high, high], 1), np.concatenate([low, np.zeros_like(low)], 1)], 0
    )


def factors(count):
    place = np.arange(lanes) - 0.5 * (lanes - 1)
    angle = 2.0 * math.pi * np.outer(place, place) / length
    values, vectors, units = [], [], []
    for part, unit in ((np.cos(angle), 1.0), (np.sin(angle), -1j)):
        value, vector = np.linalg.eigh(part)
        values.append(value)
        vectors.append(vector * np.where(vector[-1] < 0.0, -1.0, 1.0))
        units.append(np.full(lanes, unit))
    values, vectors = np.concatenate(values), np.concatenate(vectors, 1)
    units = np.concatenate(units)
    kept = np.argsort(-np.abs(values), kind="stable")[:count]
    side = vectors[:, kept] * np.sqrt(np.abs(values[kept]))
    weight = units[kept] * np.sign(values[kept])
    return np.pad(side, ((0, 0), (0, modes - count))), np.pad(weight, (0, modes - count))


def row_transform(count):
    side, weight = factors(count)
    place = np.arange(lanes) - 0.5 * (lanes - 1)
    centre = lanes * np.arange(rows_n) + 0.5 * (lanes - 1)
    turn = np.exp(-2j * math.pi * np.outer(centre, place) / length)
    offset = 0.5 * (lanes - 1)
    phase = np.exp(-2j * math.pi * np.arange(rows_n) * lanes * offset / length)
    constant = np.exp(-2j * math.pi * offset * offset / length)
    gather = side.T[None] * turn[:, None, :] * phase[:, None, None]
    expand = (side * weight)[:, None, :] * turn.T[:, :, None] * phase[None, :, None] * constant
    return gather.reshape(rows_n * modes, lanes), expand.reshape(lanes, rows_n * modes)


def parts(table):
    return np.concatenate([table.real, table.imag], 0)


def tables():
    col = np.arange(cols_n)
    x_l = np.arange(cells)
    k1x = np.arange(64)
    k2x = (2 * np.arange(32)[None, :] + np.arange(2)[:, None]).reshape(-1)
    kappa = (4 * col[None, :] + np.arange(4)[:, None]).reshape(-1)

    gather, expand = row_transform(modes - 1)
    y_gather = deep(parts(gather))
    y_expand = tall(parts(expand[kappa]))
    gather, expand = row_transform(modes)
    z_gather = deep(parts(gather[:, kappa]))
    z_expand = tall(parts(expand))

    cos, sin = wave(k1x, col, 64)
    x_first = thick(np.concatenate([cos, sin], 0))
    x_back = deep(np.concatenate([cos, sin], 0).reshape(2, 64, 32).transpose(2, 0, 1).reshape(32, 128))
    cos, sin = wave(k1x, x_l, length)
    x_twist = np.stack([np.concatenate([cos, cos], 1), np.concatenate([sin, -sin], 1)])
    cos, sin = wave(k2x, x_l, 64)
    x_last = deep(np.concatenate([cos, sin], 1))
    cos, sin = wave(x_l, k2x, 64)
    x_lead = deep(np.concatenate([np.concatenate([cos, sin], 1)] * 2, 0))
    cos, sin = wave(x_l, k1x, length)
    own = np.concatenate([np.concatenate([cos, -cos], 1), np.concatenate([sin, -sin], 1)], 0)
    other = np.concatenate([np.concatenate([-sin, -sin], 1), np.concatenate([cos, cos], 1)], 0)
    x_twists = np.concatenate([x_twist, np.stack([own, other])], 1).astype(np.float32)
    return {
        "y": (y_gather, y_expand),
        "x": (x_first, x_twists, x_last, x_lead, x_back),
        "z": (z_gather, z_expand),
    }


def split(values):
    high = values.astype(bf16)
    low = (values - high.astype(f32)).astype(bf16)
    return high, low


def stacked_product(table, values):
    high, low = split(values)
    return jnp.dot(table, jnp.concatenate([high, high, low], 0), preferred_element_type=f32)


def tall_product(table, values):
    high, low = split(values)
    size = table.shape[0] // 2
    both = jnp.dot(table, high, preferred_element_type=f32)
    rest = jnp.dot(table[:size], low, preferred_element_type=f32)
    return both[:size] + both[size:] + rest


def deep_product(table, values, contract):
    both = jnp.concatenate(split(values), contract)
    dims = (((1,), (contract,)), ((), ()))
    both = lax.dot_general(table, both, dims, preferred_element_type=f32)
    size = table.shape[0] // 2
    return both[:size] + both[size:]


def half_turn(values):
    return pltpu.roll(values, 64, 1)


def lane_index(shape):
    return lax.broadcasted_iota(jnp.int32, shape, len(shape) - 1)


def half_sign(rows):
    return jnp.where(lane_index((rows, 128)) < 64, 1.0, -1.0).astype(f32)


def pack_body(
    magnet_hbm, stiff_hbm, gather_hbm, out_ref, edge_ref, magnet_ref, stiff_ref, gather_ref, sems
):
    copies = [
        pltpu.make_async_copy(magnet_hbm, magnet_ref, sems.at[0]),
        pltpu.make_async_copy(stiff_hbm, stiff_ref, sems.at[1]),
        pltpu.make_async_copy(gather_hbm, gather_ref, sems.at[2]),
    ]
    for copy in copies:
        copy.start()
    for copy in copies:
        copy.wait()
    values = jnp.concatenate([magnet_ref[0], magnet_ref[1], magnet_ref[2]], 0)
    sums = deep_product(gather_ref[...], values, 1)
    size = rows_n * modes
    low = lane_index((size, 128)) < 64
    re, im = sums[:size, :128], sums[size:, :128]
    last = jnp.concatenate([sums[:size, 128:], sums[size:, 128:]], 1)
    blocks = (jnp.where(low, re, half_turn(im)), jnp.where(low, half_turn(re), im), last)
    for a in range(3):
        for r in range(rows_n):
            out_ref[48 * r + 16 * a : 48 * r + 16 * a + 16, :] = blocks[a][16 * r : 16 * r + 16]
    former = jnp.concatenate([magnet_ref[0], magnet_ref[1]], 0).T
    latter = jnp.concatenate([magnet_ref[2], stiff_ref[...]], 0).T
    after = lax.broadcasted_iota(jnp.int32, (rows_n, lanes), 0) > lax.axis_index("row")
    for n, sides in enumerate((former, latter)):
        out_ref[pl.ds(16 * n + 15, rows_n, stride=48), :] = jnp.where(after, sides[127:], sides[:1])
    for a in range(3):
        edge_ref[a : a + 1, :] = magnet_ref[a, :1, :]
        edge_ref[4 + a : 5 + a, :] = magnet_ref[a, cells - 1 :, :]
    edge_ref[3:4, :] = stiff_ref[:1, :]
    edge_ref[7:8, :] = stiff_ref[cells - 1 :, :]


def spread_kern(kern_ref):
    low = lane_index((32, 128)) < 64
    spread = []
    for j in range(6):
        spread.append([])
        for k in range(4):
            part = kern_ref[pl.ds(128 * j + k, 32, stride=4), :]
            turned = half_turn(part)
            halves = [jnp.where(low, part, turned), jnp.where(low, turned, part)]
            spread[j].append(jnp.concatenate(halves, 0))
    return spread


def chunk_blocks(in_ref):
    columns = []
    for a in range(3):
        block = [in_ref[48 * r + 16 * a : 48 * r + 16 * a + 16, :] for r in range(rows_n)]
        columns.append(jnp.concatenate(block, 0))
    return jnp.concatenate(columns, 1)


def forward_body(in_ref, edge_ref, expand_ref, out_ref):
    sums = tall_product(expand_ref[...], chunk_blocks(in_ref))
    sign = half_sign(128)
    for a in range(3):
        block = sums[:, 128 * a : 128 * a + 128]
        block = block[:128] - half_turn(block[128:]) * sign
        for k in range(4):
            out_ref[pl.ds(4 * a + k, cols_n, stride=16), :] = block[32 * k : 32 * k + 32]
    col = lax.axis_index("col")
    first, last = edge_ref[0:4, :], edge_ref[4:8, :]
    for c in range(cols_n):
        out_ref[16 * c + 12 : 16 * c + 16, :] = jnp.where(c > col, last, first)


def spectral_body(
    in_ref, kern_ref, first_ref, twist_ref, last_ref, lead_ref, back_ref, out_ref
):
    columns = [in_ref[pl.ds(j, cols_n, stride=16), :] for j in range(12)]
    section = stacked_product(first_ref[...], jnp.concatenate(columns, 1))
    sign = half_sign(64)
    own, other = twist_ref[0, :64, :], twist_ref[1, :64, :]
    turned = []
    for j in range(12):
        block = section[:, 128 * j : 128 * j + 128]
        block = block[:64] + half_turn(block[64:]) * sign
        block = block * own + half_turn(block) * other
        turned.append(block)
        turned.append(half_turn(block) * sign)
    freq = deep_product(last_ref[...], jnp.concatenate(turned, 0), 1)
    kern = spread_kern(kern_ref)
    sources = []
    for target in range(3):
        for k in range(4):
            total = None
            for b in range(3):
                j = 4 * b + k
                term = kern[tensor_slots[target][b]][k] * freq[:, 128 * j : 128 * j + 128]
                total = term if total is None else total + term
            sources.append(jnp.concatenate([total, -half_turn(total) * sign], 0))
    section = deep_product(lead_ref[...], jnp.concatenate(sources, 1), 0)
    own, other = twist_ref[0, 64:, :], twist_ref[1, 64:, :]
    turned = []
    for j in range(12):
        block = section[:, 128 * j : 128 * j + 128]
        turned.append(block * own + half_turn(block) * other)
    result = deep_product(back_ref[...], jnp.concatenate(turned, 0), 1)
    scale = -1.0 / (length * length)
    lane = lane_index((cols_n, 128))
    zero_weight = jnp.where(lane < 64, 1.0, 0.0).astype(f32)
    is_zero = jnp.logical_and(lax.axis_index("row") == 0, lax.axis_index("col") == 0)
    for j in range(12):
        block = result[:, 128 * j : 128 * j + 128]
        weight = jnp.full((cols_n, 128), 2.0, f32)
        if j % 4 == 0:
            weight = jnp.where(is_zero, zero_weight, weight)
        out_ref[pl.ds(j, cols_n, stride=12), :] = block * (weight * scale)


def back_body(in_ref, gather_ref, out_ref):
    columns = []
    for a in range(3):
        block = [in_ref[pl.ds(4 * a + k, cols_n, stride=12), :] for k in range(4)]
        columns.append(jnp.concatenate(block, 0))
    sums = deep_product(gather_ref[...], jnp.concatenate(columns, 1), 0)
    size = rows_n * modes
    sign = half_sign(size)
    for a in range(3):
        block = sums[:, 128 * a : 128 * a + 128]
        block = block[:size] + half_turn(block[size:]) * sign
        for r in range(rows_n):
            out_ref[48 * r + 16 * a : 48 * r + 16 * a + 16, :] = block[16 * r : 16 * r + 16]


def cross(former, latter):
    return (
        former[1] * latter[2] - former[2] * latter[1],
        former[2] * latter[0] - former[0] * latter[2],
        former[0] * latter[1] - former[1] * latter[0],
    )


def torque_body(in_ref, magnet_ref, stiff_ref, beside_y_ref, beside_x_ref, expand_ref, out_ref):
    row, col = lax.axis_index("row"), lax.axis_index("col")
    sums = tall_product(expand_ref[...], chunk_blocks(in_ref))
    demag = []
    for a in range(3):
        block = sums[:, 128 * a : 128 * a + 128]
        demag.append(block[:128] + half_turn(block[128:]))
    low = lane_index((128, 128)) < 64
    former = jnp.where(low, demag[0], half_turn(demag[1])).T
    demag = [former[:64], former[64:], demag[2].T[:64]]

    def side(index):
        start = 48 * index
        rows = [beside_y_ref[pl.ds(pl.multiple_of(start + 16 * n + 8, 8), 8), :] for n in range(2)]
        return [block[7:8] for block in rows]

    before_y = side(jnp.maximum(row - 1, 0))
    after_y = side(jnp.minimum(row + 1, rows_n - 1))
    before_x = beside_x_ref[pl.ds(pl.multiple_of(16 * jnp.maximum(col - 1, 0), 16), 16), :]
    after_x = beside_x_ref[pl.ds(pl.multiple_of(16 * jnp.minimum(col + 1, cols_n - 1), 16), 16), :]
    edges = jnp.concatenate(before_y + after_y + [jnp.zeros((124, 128), f32)], 0).T
    stack = [magnet_ref[0], magnet_ref[1], magnet_ref[2], stiff_ref[...]]
    lane = lane_index((cells, 128))
    sub = lax.broadcasted_iota(jnp.int32, (cells, 128), 0)

    def neighbour(n, direction):
        centre = stack[n]
        part = slice(64 * (n % 2), 64 * (n % 2) + 64)
        if direction == 0:
            return jnp.where(sub == cells - 1, after_x[12 + n : 13 + n], pltpu.roll(centre, cells - 1, 0))
        if direction == 1:
            return jnp.where(sub == 0, before_x[12 + n : 13 + n], pltpu.roll(centre, 1, 0))
        if direction == 2:
            edge = edges[part, 2 + n // 2 : 3 + n // 2]
            return jnp.where(lane == 127, edge, pltpu.roll(centre, 127, 1))
        edge = edges[part, n // 2 : n // 2 + 1]
        return jnp.where(lane == 0, edge, pltpu.roll(centre, 1, 1))

    absent = (
        jnp.logical_and(sub == cells - 1, col == cols_n - 1),
        jnp.logical_and(sub == 0, col == 0),
        jnp.logical_and(lane == 127, row == rows_n - 1),
        jnp.logical_and(lane == 0, row == 0),
    )
    exchange = [None] * 3
    for direction in range(4):
        coupling = 0.5 * (stack[3] + neighbour(3, direction))
        coupling = jnp.where(absent[direction], 0.0, coupling)
        for a in range(3):
            term = coupling * (neighbour(a, direction) - stack[a])
            exchange[a] = term if exchange[a] is None else exchange[a] + term
    magnet = stack[:3]
    field = [exchange[a] + demag[a] for a in range(3)]
    field[2] = field[2] + anisotropy * magnet[2]
    first_cross = cross(magnet, field)
    second_cross = cross(magnet, first_cross)
    factor = -1.0 / (1.0 + damping * damping)
    for a in range(3):
        out_ref[a] = (first_cross[a] + damping * second_cross[a]) * factor


in_vmem = pl.BlockSpec(memory_space=pltpu.VMEM)
in_hbm = pl.BlockSpec(memory_space=pltpu.HBM)


def call(body, out_shapes, *args, scratch=(), in_spec=in_vmem, vmem=32 * 2**20, flops=10**8):
    shapes = [jax.ShapeDtypeStruct(shape, f32) for shape in out_shapes]
    return pl.pallas_call(
        body,
        out_shape=shapes,
        in_specs=[in_spec] * len(args),
        out_specs=[in_vmem] * len(shapes),
        scratch_shapes=list(scratch),
        compiler_params=pltpu.CompilerParams(vmem_limit_bytes=vmem),
        cost_estimate=pl.CostEstimate(flops=flops, bytes_accessed=10**6, transcendentals=0),
    )(*args)


def exchange(array, axis, chunks):
    shape = array.shape
    rows = shape[0] // chunks
    tile = math.gcd(rows, 8)
    array = array.reshape(chunks, rows // tile, tile, shape[1])
    return lax.all_to_all(array, axis, split_axis=0, concat_axis=0, tiled=True).reshape(shape)


def local(magnet, stiffness, kern):
    constant = {name: [jnp.asarray(t) for t in group] for name, group in tables().items()}
    packed, edge = call(
        pack_body,
        [(768, 128), (8, 128)],
        magnet,
        stiffness,
        constant["y"][0],
        in_spec=in_hbm,
        vmem=55208 * 2**10,
        scratch=[
            pltpu.VMEM((3, cells, lanes), f32),
            pltpu.VMEM((cells, lanes), f32),
            pltpu.VMEM(constant["y"][0].shape, bf16),
            pltpu.SemaphoreType.DMA((3,)),
        ],
    )
    sums = exchange(packed, "row", rows_n)
    (columns,) = call(forward_body, [(512, 128)], sums, edge, constant["y"][1])
    columns = exchange(columns, "col", cols_n)
    tensor = kern.reshape(6, 4, 32, 128).transpose(0, 2, 1, 3).reshape(768, 128)
    (inverse_x,) = call(spectral_body, [(384, 128)], columns, tensor, *constant["x"])
    inverse_x = exchange(inverse_x, "col", cols_n)
    (coef,) = call(back_body, [(768, 128)], inverse_x, constant["z"][0])
    coef = exchange(coef, "row", rows_n)
    (torque,) = call(
        torque_body, [(3, 64, 128)], coef, magnet, stiffness, sums, columns, constant["z"][1]
    )
    return torque


def solution(mesh):
    in_specs = (P(None, "col", "row"), P("col", "row"), P(None, ("row", "col"), None))
    out_specs = P(None, "col", "row")
    return jax.shard_map(local, mesh=mesh, in_specs=in_specs, out_specs=out_specs, check_vma=False)
```

time: 123 us -> 104 us (0.85)
  the two profiles are of different devices: /device:TPU:32 before, /device:TPU:2 now
where the time goes in v3:
time: 104 us; the launch traced here: 103 us
  blocking collectives  96.7 us (93%)
  Pallas kernels  6.38 us (6%)
    all_to_all x4, blocking collectives, exchange(): lax.all_to_all(array, axis, split_axis=0, concat_axis=0, tiled=True)  96.7 us
    pallas_call x5, Pallas kernels, call(): pl.pallas_call(body, out_shape=shapes, in_specs=[in_spec] * len(args), ou...  6.38 us

profile of v3, /device:TPU:2, one launch (start us, length us, event | category | flops | bytes accessed | tf_op | source)
XLA Modules:
  0.0 103.2 jit_solution(5796375887565069505)
XLA Ops:
  0.0 2.3 %shard_map.118 = (f32[768,128]{1,0:T(8,128)}, f32[8,128]{1,0:T(8,128)S(1)}) custom-call(f32[3,64,128]{2,1,0:T(8,128)} %magnet_ref.1, f32[64,128]{1,0:T(8,128)} %stiff_ref.1, bf16[1024,256]{1,0:T(8,128)(2,1)} %constant.18.clone.gather_hbm), custom_call_target="tpu_custom_call" | custom-call | flops 100000000 | bytes 1000000 | tf_op jit(solution)/shard_map/pallas_call | solution.py:365
  2.3 0.0 copy-start.3
  2.4 39.1 %all_to_all.20 = f32[16,6,8,128]{3,2,1,0:T(8,128)S(1)} all-to-all(f32[16,6,8,128]{3,2,1,0:T(8,128)} %bitcast.23), channel_id=1, replica_groups=mesh['row'=16,'col'=32] {'row'}, dimensions={0} | all-to-all | bytes 786432 | tf_op jit(solution)/shard_map/all_to_all | solution.py:381
  41.5 0.0 copy-done.3
  41.5 0.0 copy-start.5
  41.5 0.0 copy-start.8
  41.5 0.0 copy-start.9
  41.5 0.0 copy-start.10
  41.5 0.5 shard_map.119
  42.0 0.0 copy-start.2
  42.0 0.0 copy-start.6
  42.0 15.3 %all_to_all.21 = f32[32,2,8,128]{3,2,1,0:T(8,128)S(1)} all-to-all(f32[32,2,8,128]{3,2,1,0:T(8,128)S(1)} %bitcast.19), channel_id=1, replica_groups=mesh['row'=16,'col'=32] {'col'}, dimensions={0} | all-to-all | bytes 524288 | tf_op jit(solution)/shard_map/all_to_all | solution.py:381
  57.3 0.0 copy-done.5
  57.3 0.0 copy-done.8
  57.3 0.0 copy-done.9
  57.3 0.0 copy-done.10
  57.3 0.0 copy-done.2
  57.3 0.0 copy-done.6
  57.3 0.0 copy-start
  57.3 1.7 %shard_map.120 = f32[384,128]{1,0:T(8,128)S(1)} custom-call(f32[512,128]{1,0:T(8,128)S(1)} %bitcast.15, f32[768,128]{1,0:T(8,128)S(1)} %bitcast.22, bf16[128,96]{1,0:T(8,128)(2,1)S(1)} %copy-done.10, f32[2,192,128]{2,1,0:T(8,128)S(1)} %copy-done.5, bf16[128,256]{1,0:T(8,128)(2,1)S(1)} %copy-done.8, bf16[256,256]{1,0:T(8,128)(2,1)S(1)} %copy-done.6, ...), custom_call_target="tpu_custom_call" | custom-call | flops 100000000 | bytes 1000000 | tf_op jit(solution)/shard_map/pallas_call | solution.py:365
  59.0 11.9 %all_to_all.22 = f32[32,3,4,128]{3,2,1,0:T(4,128)S(1)} all-to-all(f32[32,3,4,128]{3,2,1,0:T(4,128)S(1)} %bitcast.20), channel_id=1, replica_groups=mesh['row'=16,'col'=32] {'col'}, dimensions={0} | all-to-all | bytes 393216 | tf_op jit(solution)/shard_map/all_to_all | solution.py:381
  70.9 0.0 copy-done
  70.9 0.5 shard_map.121
  71.5 0.0 copy-start.1
  71.5 0.0 copy-start.4
  71.5 0.0 copy-start.7
  71.5 30.4 %all_to_all.23 = f32[16,6,8,128]{3,2,1,0:T(8,128)S(1)} all-to-all(f32[16,6,8,128]{3,2,1,0:T(8,128)S(1)} %bitcast.17), channel_id=1, replica_groups=mesh['row'=16,'col'=32] {'row'}, dimensions={0} | all-to-all | bytes 786432 | tf_op jit(solution)/shard_map/all_to_all | solution.py:381
  101.9 0.0 copy-done.1
  101.9 0.0 copy-done.4
  101.9 0.0 copy-done.7
  101.9 1.3 %shard_map.122 = f32[3,64,128]{2,1,0:T(8,128)} custom-call(f32[768,128]{1,0:T(8,128)S(1)} %bitcast.18, f32[3,64,128]{2,1,0:T(8,128)S(1)} %copy-done.1, f32[64,128]{1,0:T(8,128)S(1)} %copy-done.7, f32[768,128]{1,0:T(8,128)S(1)} %bitcast.14, f32[512,128]{1,0:T(8,128)S(1)} %bitcast.16, bf16[512,256]{1,0:T(8,128)(2,1)S(1)} %copy-done.4), custom_call_target="tpu_custom_call" | custom-call | flops 100000000 | bytes 1000000 | tf_op jit(solution)/shard_map/pallas_call | solution.py:365
Async XLA Ops:
  2.3 39.1 %copy-start.3 = (bf16[512,256]{1,0:T(8,128)(2,1)S(1)}, bf16[512,256]{1,0:T(8,128)(2,1)}, u32[]{:S(2)}) copy-start(bf16[512,256]{1,0:T(8,128)(2,1)} %constant.19.clone.expand_ref) | copy-start | bytes 786436
  41.5 15.8 %copy-start.5 = (f32[2,192,128]{2,1,0:T(8,128)S(1)}, f32[2,192,128]{2,1,0:T(8,128)}, u32[]{:S(2)}) copy-start(f32[2,192,128]{2,1,0:T(8,128)} %constant.21.clone.twist_ref) | copy-start | bytes 589828
  41.5 15.8 %copy-start.8 = (bf16[128,256]{1,0:T(8,128)(2,1)S(1)}, bf16[128,256]{1,0:T(8,128)(2,1)}, u32[]{:S(2)}) copy-start(bf16[128,256]{1,0:T(8,128)(2,1)} %constant.22.clone.last_ref) | copy-start | bytes 196612
  41.5 15.8 %copy-start.9 = (bf16[64,256]{1,0:T(8,128)(2,1)S(1)}, bf16[64,256]{1,0:T(8,128)(2,1)}, u32[]{:S(2)}) copy-start(bf16[64,256]{1,0:T(8,128)(2,1)} %constant.24.clone.back_ref) | copy-start | bytes 98308
  41.5 15.8 %copy-start.10 = (bf16[128,96]{1,0:T(8,128)(2,1)S(1)}, bf16[128,96]{1,0:T(8,128)(2,1)}, u32[]{:S(2)}) copy-start(bf16[128,96]{1,0:T(8,128)(2,1)} %constant.20.clone.first_ref) | copy-start | bytes 73732
  42.0 15.3 %copy-start.2 = (f32[6,4,4096]{2,1,0:T(4,128)S(1)}, f32[6,4,4096]{2,1,0:T(4,128)}, u32[]{:S(2)}) copy-start(f32[6,4,4096]{2,1,0:T(4,128)} %param.14) | copy-start | bytes 1179652
  42.0 15.3 %copy-start.6 = (bf16[256,256]{1,0:T(8,128)(2,1)S(1)}, bf16[256,256]{1,0:T(8,128)(2,1)}, u32[]{:S(2)}) copy-start(bf16[256,256]{1,0:T(8,128)(2,1)} %constant.23.clone.lead_ref) | copy-start | bytes 393220
  57.3 13.6 %copy-start = (bf16[1024,256]{1,0:T(8,128)(2,1)S(1)}, bf16[1024,256]{1,0:T(8,128)(2,1)}, u32[]{:S(2)}) copy-start(bf16[1024,256]{1,0:T(8,128)(2,1)} %constant.25.clone.gather_ref) | copy-start | bytes 1572868
  71.5 30.4 %copy-start.1 = (f32[3,64,128]{2,1,0:T(8,128)S(1)}, f32[3,64,128]{2,1,0:T(8,128)}, u32[]{:S(2)}) copy-start(f32[3,64,128]{2,1,0:T(8,128)} %magnet_ref.1) | copy-start | bytes 294916
  71.5 30.4 %copy-start.4 = (bf16[512,256]{1,0:T(8,128)(2,1)S(1)}, bf16[512,256]{1,0:T(8,128)(2,1)}, u32[]{:S(2)}) copy-start(bf16[512,256]{1,0:T(8,128)(2,1)} %constant.26.clone.expand_ref) | copy-start | bytes 786436
  71.5 30.4 %copy-start.7 = (f32[64,128]{1,0:T(8,128)S(1)}, f32[64,128]{1,0:T(8,128)}, u32[]{:S(2)}) copy-start(f32[64,128]{1,0:T(8,128)} %stiff_ref.1) | copy-start | bytes 98308

commit v4 on v3

--- a/solution.py
+++ b/solution.py
@@ -22,7 +22,9 @@
 f32 = jnp.float32
 
 
-modes = 16
+modes = 15
+sums_rows = 3 * modes
+halo_rows = sums_rows + 2
 
 
 def wave(first, second, period):
@@ -66,20 +68,20 @@
     kept = np.argsort(-np.abs(values), kind="stable")[:count]
     side = vectors[:, kept] * np.sqrt(np.abs(values[kept]))
     weight = units[kept] * np.sign(values[kept])
-    return np.pad(side, ((0, 0), (0, modes - count))), np.pad(weight, (0, modes - count))
-
-
-def row_transform(count):
-    side, weight = factors(count)
+    return side, weight
+
+
+def row_transform():
+    side, weight = factors(modes)
     place = np.arange(lanes) - 0.5 * (lanes - 1)
     centre = lanes * np.arange(rows_n) + 0.5 * (lanes - 1)
     turn = np.exp(-2j * math.pi * np.outer(centre, place) / length)
     offset = 0.5 * (lanes - 1)
     phase = np.exp(-2j * math.pi * np.arange(rows_n) * lanes * offset / length)
     constant = np.exp(-2j * math.pi * offset * offset / length)
-    gather = side.T[None] * turn[:, None, :] * phase[:, None, None]
-    expand = (side * weight)[:, None, :] * turn.T[:, :, None] * phase[None, :, None] * constant
-    return gather.reshape(rows_n * modes, lanes), expand.reshape(lanes, rows_n * modes)
+    gather = side.T[:, None] * turn[None] * phase[None, :, None]
+    expand = (side * weight)[:, :, None] * turn.T[:, None, :] * phase * constant
+    return gather.reshape(modes * rows_n, lanes), expand.reshape(lanes, modes * rows_n)
 
 
 def parts(table):
@@ -93,10 +95,9 @@
     k2x = (2 * np.arange(32)[None, :] + np.arange(2)[:, None]).reshape(-1)
     kappa = (4 * col[None, :] + np.arange(4)[:, None]).reshape(-1)
 
-    gather, expand = row_transform(modes - 1)
+    gather, expand = row_transform()
     y_gather = deep(parts(gather))
     y_expand = tall(parts(expand[kappa]))
-    gather, expand = row_transform(modes)
     z_gather = deep(parts(gather[:, kappa]))
     z_expand = tall(parts(expand))
 
@@ -178,14 +179,13 @@
     re, im = sums[:size, :128], sums[size:, :128]
     last = jnp.concatenate([sums[:size, 128:], sums[size:, 128:]], 1)
     blocks = (jnp.where(low, re, half_turn(im)), jnp.where(low, half_turn(re), im), last)
-    for a in range(3):
-        for r in range(rows_n):
-            out_ref[48 * r + 16 * a : 48 * r + 16 * a + 16, :] = blocks[a][16 * r : 16 * r + 16]
+    store_chunks(out_ref, halo_rows, blocks)
     former = jnp.concatenate([magnet_ref[0], magnet_ref[1]], 0).T
     latter = jnp.concatenate([magnet_ref[2], stiff_ref[...]], 0).T
     after = lax.broadcasted_iota(jnp.int32, (rows_n, lanes), 0) > lax.axis_index("row")
     for n, sides in enumerate((former, latter)):
-        out_ref[pl.ds(16 * n + 15, rows_n, stride=48), :] = jnp.where(after, sides[127:], sides[:1])
+        edges = jnp.where(after, sides[127:], sides[:1])
+        out_ref[pl.ds(sums_rows + n, rows_n, stride=halo_rows), :] = edges
     for a in range(3):
         edge_ref[a : a + 1, :] = magnet_ref[a, :1, :]
         edge_ref[4 + a : 5 + a, :] = magnet_ref[a, cells - 1 :, :]
@@ -206,16 +206,24 @@
     return spread
 
 
-def chunk_blocks(in_ref):
+def store_chunks(out_ref, rows, blocks):
+    for a in range(3):
+        for n in range(modes):
+            out_ref[pl.ds(modes * a + n, rows_n, stride=rows), :] = blocks[a][
+                rows_n * n : rows_n * n + rows_n
+            ]
+
+
+def load_chunks(in_ref, rows):
     columns = []
     for a in range(3):
-        block = [in_ref[48 * r + 16 * a : 48 * r + 16 * a + 16, :] for r in range(rows_n)]
+        block = [in_ref[pl.ds(modes * a + n, rows_n, stride=rows), :] for n in range(modes)]
         columns.append(jnp.concatenate(block, 0))
     return jnp.concatenate(columns, 1)
 
 
 def forward_body(in_ref, edge_ref, expand_ref, out_ref):
-    sums = tall_product(expand_ref[...], chunk_blocks(in_ref))
+    sums = tall_product(expand_ref[...], load_chunks(in_ref, halo_rows))
     sign = half_sign(128)
     for a in range(3):
         block = sums[:, 128 * a : 128 * a + 128]
@@ -280,11 +288,11 @@
     sums = deep_product(gather_ref[...], jnp.concatenate(columns, 1), 0)
     size = rows_n * modes
     sign = half_sign(size)
+    blocks = []
     for a in range(3):
         block = sums[:, 128 * a : 128 * a + 128]
-        block = block[:size] + half_turn(block[size:]) * sign
-        for r in range(rows_n):
-            out_ref[48 * r + 16 * a : 48 * r + 16 * a + 16, :] = block[16 * r : 16 * r + 16]
+        blocks.append(block[:size] + half_turn(block[size:]) * sign)
+    store_chunks(out_ref, sums_rows, blocks)
 
 
 def cross(former, latter):
@@ -297,7 +305,7 @@
 
 def torque_body(in_ref, magnet_ref, stiff_ref, beside_y_ref, beside_x_ref, expand_ref, out_ref):
     row, col = lax.axis_index("row"), lax.axis_index("col")
-    sums = tall_product(expand_ref[...], chunk_blocks(in_ref))
+    sums = tall_product(expand_ref[...], load_chunks(in_ref, sums_rows))
     demag = []
     for a in range(3):
         block = sums[:, 128 * a : 128 * a + 128]
@@ -306,16 +314,13 @@
     former = jnp.where(low, demag[0], half_turn(demag[1])).T
     demag = [former[:64], former[64:], demag[2].T[:64]]
 
-    def side(index):
-        start = 48 * index
-        rows = [beside_y_ref[pl.ds(pl.multiple_of(start + 16 * n + 8, 8), 8), :] for n in range(2)]
-        return [block[7:8] for block in rows]
-
-    before_y = side(jnp.maximum(row - 1, 0))
-    after_y = side(jnp.minimum(row + 1, rows_n - 1))
+    start = halo_rows * jnp.maximum(row - 1, 0) + sums_rows
+    before_y = beside_y_ref[pl.ds(start, 2), :]
+    start = halo_rows * jnp.minimum(row + 1, rows_n - 1) + sums_rows
+    after_y = beside_y_ref[pl.ds(start, 2), :]
     before_x = beside_x_ref[pl.ds(pl.multiple_of(16 * jnp.maximum(col - 1, 0), 16), 16), :]
     after_x = beside_x_ref[pl.ds(pl.multiple_of(16 * jnp.minimum(col + 1, cols_n - 1), 16), 16), :]
-    edges = jnp.concatenate(before_y + after_y + [jnp.zeros((124, 128), f32)], 0).T
+    edges = jnp.concatenate([before_y, after_y, jnp.zeros((124, 128), f32)], 0).T
     stack = [magnet_ref[0], magnet_ref[1], magnet_ref[2], stiff_ref[...]]
     lane = lane_index((cells, 128))
     sub = lax.broadcasted_iota(jnp.int32, (cells, 128), 0)
@@ -385,7 +390,7 @@
     constant = {name: [jnp.asarray(t) for t in group] for name, group in tables().items()}
     packed, edge = call(
         pack_body,
-        [(768, 128), (8, 128)],
+        [(rows_n * halo_rows, 128), (8, 128)],
         magnet,
         stiffness,
         constant["y"][0],
@@ -404,7 +409,7 @@
     tensor = kern.reshape(6, 4, 32, 128).transpose(0, 2, 1, 3).reshape(768, 128)
     (inverse_x,) = call(spectral_body, [(384, 128)], columns, tensor, *constant["x"])
     inverse_x = exchange(inverse_x, "col", cols_n)
-    (coef,) = call(back_body, [(768, 128)], inverse_x, constant["z"][0])
+    (coef,) = call(back_body, [(rows_n * sums_rows, 128)], inverse_x, constant["z"][0])
     coef = exchange(coef, "row", rows_n)
     (torque,) = call(
         torque_body, [(3, 64, 128)], coef, magnet, stiffness, sums, columns, constant["z"][1]

time: 104 us -> 102 us (0.981)
  blocking collectives: 96.7 us -> 95.3 us
    all_to_all x4, blocking collectives: 96.7 us -> 95.3 us  [exchange(): lax.all_to_all(array, axis, split_axis=0, concat_axis=0, tiled=True)]
where the time goes in v4:
time: 102 us
  blocking collectives  95.3 us (93%)
  Pallas kernels  6.32 us (6%)
    all_to_all x4, blocking collectives, exchange(): lax.all_to_all(array, axis, split_axis=0, concat_axis=0, tiled=True)  95.3 us
    pallas_call x5, Pallas kernels, call(): pl.pallas_call(body, out_shape=shapes, in_specs=[in_spec] * len(args), ou...  6.32 us

profile of v4, /device:TPU:2, one launch (start us, length us, event | category | flops | bytes accessed | tf_op | source)
XLA Modules:
  0.0 101.8 jit_solution(3308250027457442779)
XLA Ops:
  0.0 2.3 %shard_map.118 = (f32[752,128]{1,0:T(8,128)}, f32[8,128]{1,0:T(8,128)S(1)}) custom-call(f32[3,64,128]{2,1,0:T(8,128)} %magnet_ref.1, f32[64,128]{1,0:T(8,128)} %stiff_ref.1, bf16[960,256]{1,0:T(8,128)(2,1)} %constant.18.clone.gather_hbm), custom_call_target="tpu_custom_call" | custom-call | flops 100000000 | bytes 1000000 | tf_op jit(solution)/shard_map/pallas_call | solution.py:370
  2.3 0.0 copy-start.3
  2.3 38.6 %all_to_all.20 = f32[16,47,1,128]{3,2,1,0:T(1,128)S(1)} all-to-all(f32[16,47,1,128]{3,2,1,0:T(1,128)} %bitcast.23), channel_id=1, replica_groups=mesh['row'=16,'col'=32] {'row'}, dimensions={0} | all-to-all | bytes 770048 | tf_op jit(solution)/shard_map/all_to_all | solution.py:386
  40.9 0.0 copy-done.3
  41.0 0.0 copy-start.5
  41.0 0.0 copy-start.8
  41.0 0.0 copy-start.9
  41.0 0.0 copy-start.10
  41.0 0.5 shard_map.119
  41.4 0.0 copy-start.2
  41.5 0.0 copy-start.6
  41.5 15.3 %all_to_all.21 = f32[32,2,8,128]{3,2,1,0:T(8,128)S(1)} all-to-all(f32[32,2,8,128]{3,2,1,0:T(8,128)S(1)} %bitcast.19), channel_id=1, replica_groups=mesh['row'=16,'col'=32] {'col'}, dimensions={0} | all-to-all | bytes 524288 | tf_op jit(solution)/shard_map/all_to_all | solution.py:386
  56.7 0.0 copy-done.5
  56.8 0.0 copy-done.8
  56.8 0.0 copy-done.9
  56.8 0.0 copy-done.10
  56.8 0.0 copy-done.2
  56.8 0.0 copy-done.6
  56.8 0.0 copy-start
  56.8 1.7 %shard_map.120 = f32[384,128]{1,0:T(8,128)S(1)} custom-call(f32[512,128]{1,0:T(8,128)S(1)} %bitcast.15, f32[768,128]{1,0:T(8,128)S(1)} %bitcast.22, bf16[128,96]{1,0:T(8,128)(2,1)S(1)} %copy-done.10, f32[2,192,128]{2,1,0:T(8,128)S(1)} %copy-done.5, bf16[128,256]{1,0:T(8,128)(2,1)S(1)} %copy-done.8, bf16[256,256]{1,0:T(8,128)(2,1)S(1)} %copy-done.6, ...), custom_call_target="tpu_custom_call" | custom-call | flops 100000000 | bytes 1000000 | tf_op jit(solution)/shard_map/pallas_call | solution.py:370
  58.5 11.9 %all_to_all.22 = f32[32,3,4,128]{3,2,1,0:T(4,128)S(1)} all-to-all(f32[32,3,4,128]{3,2,1,0:T(4,128)S(1)} %bitcast.20), channel_id=1, replica_groups=mesh['row'=16,'col'=32] {'col'}, dimensions={0} | all-to-all | bytes 393216 | tf_op jit(solution)/shard_map/all_to_all | solution.py:386
  70.4 0.0 copy-done
  70.4 0.5 shard_map.121
  70.9 0.0 copy-start.1
  70.9 0.0 copy-start.4
  70.9 0.0 copy-start.7
  71.0 29.5 %all_to_all.23 = f32[16,45,1,128]{3,2,1,0:T(1,128)S(1)} all-to-all(f32[16,45,1,128]{3,2,1,0:T(1,128)S(1)} %bitcast.18), channel_id=1, replica_groups=mesh['row'=16,'col'=32] {'row'}, dimensions={0} | all-to-all | bytes 737280 | tf_op jit(solution)/shard_map/all_to_all | solution.py:386
  100.5 0.0 copy-done.1
  100.5 0.0 copy-done.4
  100.5 0.0 copy-done.7
  100.5 1.3 %shard_map.122 = f32[3,64,128]{2,1,0:T(8,128)} custom-call(f32[720,128]{1,0:T(8,128)S(1)} %bitcast.17, f32[3,64,128]{2,1,0:T(8,128)S(1)} %copy-done.1, f32[64,128]{1,0:T(8,128)S(1)} %copy-done.7, f32[752,128]{1,0:T(8,128)S(1)} %bitcast.14, f32[512,128]{1,0:T(8,128)S(1)} %bitcast.16, bf16[512,240]{1,0:T(8,128)(2,1)S(1)} %copy-done.4), custom_call_target="tpu_custom_call" | custom-call | flops 100000000 | bytes 1000000 | tf_op jit(solution)/shard_map/pallas_call | solution.py:370
Async XLA Ops:
  2.3 38.6 %copy-start.3 = (bf16[512,240]{1,0:T(8,128)(2,1)S(1)}, bf16[512,240]{1,0:T(8,128)(2,1)}, u32[]{:S(2)}) copy-start(bf16[512,240]{1,0:T(8,128)(2,1)} %constant.19.clone.expand_ref) | copy-start | bytes 737284
  41.0 15.8 %copy-start.5 = (f32[2,192,128]{2,1,0:T(8,128)S(1)}, f32[2,192,128]{2,1,0:T(8,128)}, u32[]{:S(2)}) copy-start(f32[2,192,128]{2,1,0:T(8,128)} %constant.21.clone.twist_ref) | copy-start | bytes 589828
  41.0 15.8 %copy-start.8 = (bf16[128,256]{1,0:T(8,128)(2,1)S(1)}, bf16[128,256]{1,0:T(8,128)(2,1)}, u32[]{:S(2)}) copy-start(bf16[128,256]{1,0:T(8,128)(2,1)} %constant.22.clone.last_ref) | copy-start | bytes 196612
  41.0 15.8 %copy-start.9 = (bf16[64,256]{1,0:T(8,128)(2,1)S(1)}, bf16[64,256]{1,0:T(8,128)(2,1)}, u32[]{:S(2)}) copy-start(bf16[64,256]{1,0:T(8,128)(2,1)} %constant.24.clone.back_ref) | copy-start | bytes 98308
  41.0 15.8 %copy-start.10 = (bf16[128,96]{1,0:T(8,128)(2,1)S(1)}, bf16[128,96]{1,0:T(8,128)(2,1)}, u32[]{:S(2)}) copy-start(bf16[128,96]{1,0:T(8,128)(2,1)} %constant.20.clone.first_ref) | copy-start | bytes 73732
  41.4 15.3 %copy-start.2 = (f32[6,4,4096]{2,1,0:T(4,128)S(1)}, f32[6,4,4096]{2,1,0:T(4,128)}, u32[]{:S(2)}) copy-start(f32[6,4,4096]{2,1,0:T(4,128)} %param.14) | copy-start | bytes 1179652
  41.5 15.3 %copy-start.6 = (bf16[256,256]{1,0:T(8,128)(2,1)S(1)}, bf16[256,256]{1,0:T(8,128)(2,1)}, u32[]{:S(2)}) copy-start(bf16[256,256]{1,0:T(8,128)(2,1)} %constant.23.clone.lead_ref) | copy-start | bytes 393220
  56.8 13.6 %copy-start = (bf16[960,256]{1,0:T(8,128)(2,1)S(1)}, bf16[960,256]{1,0:T(8,128)(2,1)}, u32[]{:S(2)}) copy-start(bf16[960,256]{1,0:T(8,128)(2,1)} %constant.25.clone.gather_ref) | copy-start | bytes 1474564
  70.9 29.5 %copy-start.1 = (f32[3,64,128]{2,1,0:T(8,128)S(1)}, f32[3,64,128]{2,1,0:T(8,128)}, u32[]{:S(2)}) copy-start(f32[3,64,128]{2,1,0:T(8,128)} %magnet_ref.1) | copy-start | bytes 294916
  70.9 29.5 %copy-start.4 = (bf16[512,240]{1,0:T(8,128)(2,1)S(1)}, bf16[512,240]{1,0:T(8,128)(2,1)}, u32[]{:S(2)}) copy-start(bf16[512,240]{1,0:T(8,128)(2,1)} %constant.26.clone.expand_ref) | copy-start | bytes 737284
  70.9 29.5 %copy-start.7 = (f32[64,128]{1,0:T(8,128)S(1)}, f32[64,128]{1,0:T(8,128)}, u32[]{:S(2)}) copy-start(f32[64,128]{1,0:T(8,128)} %stiff_ref.1) | copy-start | bytes 98308

commit v5 on v4

--- a/solution.py
+++ b/solution.py
@@ -22,7 +22,7 @@
 f32 = jnp.float32
 
 
-modes = 15
+modes = 14
 sums_rows = 3 * modes
 halo_rows = sums_rows + 2
 
@@ -54,34 +54,36 @@
     )
 
 
-def factors(count):
+def factors():
     place = np.arange(lanes) - 0.5 * (lanes - 1)
     angle = 2.0 * math.pi * np.outer(place, place) / length
+    level = (1.02 - (2.0 * place / lanes) ** 2) ** -0.3
     values, vectors, units = [], [], []
     for part, unit in ((np.cos(angle), 1.0), (np.sin(angle), -1j)):
-        value, vector = np.linalg.eigh(part)
+        value, vector = np.linalg.eigh(part * np.outer(level, level))
         values.append(value)
         vectors.append(vector * np.where(vector[-1] < 0.0, -1.0, 1.0))
         units.append(np.full(lanes, unit))
     values, vectors = np.concatenate(values), np.concatenate(vectors, 1)
     units = np.concatenate(units)
-    kept = np.argsort(-np.abs(values), kind="stable")[:count]
-    side = vectors[:, kept] * np.sqrt(np.abs(values[kept]))
-    weight = units[kept] * np.sign(values[kept])
-    return side, weight
+    kept = np.argsort(-np.abs(values), kind="stable")[:modes]
+    side = vectors[:, kept] * np.sqrt(np.abs(values[kept])) / level[:, None]
+    return side, units[kept] * np.sign(values[kept])
 
 
 def row_transform():
-    side, weight = factors(modes)
+    side, weight = factors()
     place = np.arange(lanes) - 0.5 * (lanes - 1)
     centre = lanes * np.arange(rows_n) + 0.5 * (lanes - 1)
     turn = np.exp(-2j * math.pi * np.outer(centre, place) / length)
     offset = 0.5 * (lanes - 1)
     phase = np.exp(-2j * math.pi * np.arange(rows_n) * lanes * offset / length)
     constant = np.exp(-2j * math.pi * offset * offset / length)
-    gather = side.T[:, None] * turn[None] * phase[None, :, None]
+    turns = turn * phase[:, None]
+    gather = side.T[:, None] * turns[None]
     expand = (side * weight)[:, :, None] * turn.T[:, None, :] * phase * constant
-    return gather.reshape(modes * rows_n, lanes), expand.reshape(lanes, modes * rows_n)
+    gather, expand = gather.reshape(-1, lanes), expand.reshape(lanes, -1)
+    return side.T, turns, gather, expand
 
 
 def parts(table):
@@ -95,8 +97,8 @@
     k2x = (2 * np.arange(32)[None, :] + np.arange(2)[:, None]).reshape(-1)
     kappa = (4 * col[None, :] + np.arange(4)[:, None]).reshape(-1)
 
-    gather, expand = row_transform()
-    y_gather = deep(parts(gather))
+    sides, turns, gather, expand = row_transform()
+    y_gather = np.concatenate([parts(turns), sides], 0).astype(np.float32)
     y_expand = tall(parts(expand[kappa]))
     z_gather = deep(parts(gather[:, kappa]))
     z_expand = tall(parts(expand))
@@ -148,6 +150,11 @@
     return both[:size] + both[size:]
 
 
+def last_dims_product(former, latter):
+    dims = (((1,), (1,)), ((), ()))
+    return lax.dot_general(former, latter, dims, preferred_element_type=f32)
+
+
 def half_turn(values):
     return pltpu.roll(values, 64, 1)
 
@@ -173,8 +180,16 @@
     for copy in copies:
         copy.wait()
     values = jnp.concatenate([magnet_ref[0], magnet_ref[1], magnet_ref[2]], 0)
-    sums = deep_product(gather_ref[...], values, 1)
     size = rows_n * modes
+    turns = gather_ref[0 : 2 * rows_n, :]
+    sides = [gather_ref[2 * rows_n + n : 2 * rows_n + n + 1, :] for n in range(modes)]
+    re = [turns[:rows_n] * side for side in sides]
+    im = [turns[rows_n:] * side for side in sides]
+    table_high, table_low = split(jnp.concatenate(re + im, 0))
+    high, low = split(values)
+    sums = last_dims_product(
+        jnp.concatenate([table_high, table_high], 1), jnp.concatenate([high, low], 1)
+    ) + last_dims_product(table_low, high)
     low = lane_index((size, 128)) < 64
     re, im = sums[:size, :128], sums[size:, :128]
     last = jnp.concatenate([sums[:size, 128:], sums[size:, 128:]], 1)
@@ -399,7 +414,7 @@
         scratch=[
             pltpu.VMEM((3, cells, lanes), f32),
             pltpu.VMEM((cells, lanes), f32),
-            pltpu.VMEM(constant["y"][0].shape, bf16),
+            pltpu.VMEM(constant["y"][0].shape, f32),
             pltpu.SemaphoreType.DMA((3,)),
         ],
     )

time: 102 us -> 99.8 us (0.978)
  blocking collectives: 95.3 us -> 93.2 us
    all_to_all x4, blocking collectives: 95.3 us -> 93.2 us  [exchange(): lax.all_to_all(array, axis, split_axis=0, concat_axis=0, tiled=True)]
where the time goes in v5:
time: 99.8 us; the launch traced here: 99.5 us
  blocking collectives  93.2 us (93%)
  Pallas kernels  6.07 us (6%)
    all_to_all x4, blocking collectives, exchange(): lax.all_to_all(array, axis, split_axis=0, concat_axis=0, tiled=True)  93.2 us
    pallas_call x5, Pallas kernels, call(): pl.pallas_call(body, out_shape=shapes, in_specs=[in_spec] * len(args), ou...  6.07 us

profile of v5, /device:TPU:2, one launch (start us, length us, event | category | flops | bytes accessed | tf_op | source)
XLA Modules:
  0.0 99.5 jit_solution(16911761599736478296)
XLA Ops:
  0.0 2.1 %shard_map.118 = (f32[704,128]{1,0:T(8,128)}, f32[8,128]{1,0:T(8,128)S(1)}) custom-call(f32[3,64,128]{2,1,0:T(8,128)} %magnet_ref.1, f32[64,128]{1,0:T(8,128)} %stiff_ref.1, f32[46,128]{1,0:T(8,128)} %constant.18.clone.gather_hbm), custom_call_target="tpu_custom_call" | custom-call | flops 100000000 | bytes 1000000 | tf_op jit(solution)/shard_map/pallas_call | solution.py:385
  2.1 0.0 copy-start.2
  2.1 37.5 %all_to_all.20 = f32[16,11,4,128]{3,2,1,0:T(4,128)S(1)} all-to-all(f32[16,11,4,128]{3,2,1,0:T(4,128)} %bitcast.23), channel_id=1, replica_groups=mesh['row'=16,'col'=32] {'row'}, dimensions={0} | all-to-all | bytes 720896 | tf_op jit(solution)/shard_map/all_to_all | solution.py:401
  39.6 0.0 copy-done.2
  39.6 0.0 copy-start.4
  39.6 0.0 copy-start.7
  39.6 0.0 copy-start.9
  39.6 0.0 copy-start.10
  39.6 0.5 shard_map.119
  40.1 0.0 copy-start.1
  40.1 0.0 copy-start.5
  40.1 15.3 %all_to_all.21 = f32[32,2,8,128]{3,2,1,0:T(8,128)S(1)} all-to-all(f32[32,2,8,128]{3,2,1,0:T(8,128)S(1)} %bitcast.19), channel_id=1, replica_groups=mesh['row'=16,'col'=32] {'col'}, dimensions={0} | all-to-all | bytes 524288 | tf_op jit(solution)/shard_map/all_to_all | solution.py:401
  55.4 0.0 copy-done.4
  55.4 0.0 copy-done.7
  55.4 0.0 copy-done.9
  55.4 0.0 copy-done.10
  55.4 0.0 copy-done.1
  55.4 0.0 copy-done.5
  55.4 0.0 copy-start
  55.5 1.7 %shard_map.120 = f32[384,128]{1,0:T(8,128)S(1)} custom-call(f32[512,128]{1,0:T(8,128)S(1)} %bitcast.15, f32[768,128]{1,0:T(8,128)S(1)} %bitcast.22, bf16[128,96]{1,0:T(8,128)(2,1)S(1)} %copy-done.10, f32[2,192,128]{2,1,0:T(8,128)S(1)} %copy-done.4, bf16[128,256]{1,0:T(8,128)(2,1)S(1)} %copy-done.7, bf16[256,256]{1,0:T(8,128)(2,1)S(1)} %copy-done.5, ...), custom_call_target="tpu_custom_call" | custom-call | flops 100000000 | bytes 1000000 | tf_op jit(solution)/shard_map/pallas_call | solution.py:385
  57.2 11.9 %all_to_all.22 = f32[32,3,4,128]{3,2,1,0:T(4,128)S(1)} all-to-all(f32[32,3,4,128]{3,2,1,0:T(4,128)S(1)} %bitcast.20), channel_id=1, replica_groups=mesh['row'=16,'col'=32] {'col'}, dimensions={0} | all-to-all | bytes 393216 | tf_op jit(solution)/shard_map/all_to_all | solution.py:401
  69.0 0.0 copy-done
  69.0 0.5 shard_map.121
  69.5 0.0 copy-start.3
  69.6 0.0 copy-start.6
  69.6 0.0 copy-start.8
  69.6 28.6 %all_to_all.23 = f32[16,21,2,128]{3,2,1,0:T(2,128)S(1)} all-to-all(f32[16,21,2,128]{3,2,1,0:T(2,128)S(1)} %bitcast.18), channel_id=1, replica_groups=mesh['row'=16,'col'=32] {'row'}, dimensions={0} | all-to-all | bytes 688128 | tf_op jit(solution)/shard_map/all_to_all | solution.py:401
  98.2 0.0 copy-done.3
  98.2 0.0 copy-done.6
  98.2 0.0 copy-done.8
  98.2 1.3 %shard_map.122 = f32[3,64,128]{2,1,0:T(8,128)} custom-call(f32[672,128]{1,0:T(8,128)S(1)} %bitcast.17, f32[3,64,128]{2,1,0:T(8,128)S(1)} %copy-done.6, f32[64,128]{1,0:T(8,128)S(1)} %copy-done.8, f32[704,128]{1,0:T(8,128)S(1)} %bitcast.14, f32[512,128]{1,0:T(8,128)S(1)} %bitcast.16, bf16[512,224]{1,0:T(8,128)(2,1)S(1)} %copy-done.3), custom_call_target="tpu_custom_call" | custom-call | flops 100000000 | bytes 1000000 | tf_op jit(solution)/shard_map/pallas_call | solution.py:385
Async XLA Ops:
  2.1 37.5 %copy-start.2 = (bf16[512,224]{1,0:T(8,128)(2,1)S(1)}, bf16[512,224]{1,0:T(8,128)(2,1)}, u32[]{:S(2)}) copy-start(bf16[512,224]{1,0:T(8,128)(2,1)} %constant.19.clone.expand_ref) | copy-start | bytes 688132
  39.6 15.8 %copy-start.4 = (f32[2,192,128]{2,1,0:T(8,128)S(1)}, f32[2,192,128]{2,1,0:T(8,128)}, u32[]{:S(2)}) copy-start(f32[2,192,128]{2,1,0:T(8,128)} %constant.21.clone.twist_ref) | copy-start | bytes 589828
  39.6 15.8 %copy-start.7 = (bf16[128,256]{1,0:T(8,128)(2,1)S(1)}, bf16[128,256]{1,0:T(8,128)(2,1)}, u32[]{:S(2)}) copy-start(bf16[128,256]{1,0:T(8,128)(2,1)} %constant.22.clone.last_ref) | copy-start | bytes 196612
  39.6 15.8 %copy-start.9 = (bf16[64,256]{1,0:T(8,128)(2,1)S(1)}, bf16[64,256]{1,0:T(8,128)(2,1)}, u32[]{:S(2)}) copy-start(bf16[64,256]{1,0:T(8,128)(2,1)} %constant.24.clone.back_ref) | copy-start | bytes 98308
  39.6 15.8 %copy-start.10 = (bf16[128,96]{1,0:T(8,128)(2,1)S(1)}, bf16[128,96]{1,0:T(8,128)(2,1)}, u32[]{:S(2)}) copy-start(bf16[128,96]{1,0:T(8,128)(2,1)} %constant.20.clone.first_ref) | copy-start | bytes 73732
  40.1 15.3 %copy-start.1 = (f32[6,4,4096]{2,1,0:T(4,128)S(1)}, f32[6,4,4096]{2,1,0:T(4,128)}, u32[]{:S(2)}) copy-start(f32[6,4,4096]{2,1,0:T(4,128)} %param.14) | copy-start | bytes 1179652
  40.1 15.3 %copy-start.5 = (bf16[256,256]{1,0:T(8,128)(2,1)S(1)}, bf16[256,256]{1,0:T(8,128)(2,1)}, u32[]{:S(2)}) copy-start(bf16[256,256]{1,0:T(8,128)(2,1)} %constant.23.clone.lead_ref) | copy-start | bytes 393220
  55.4 13.6 %copy-start = (bf16[896,256]{1,0:T(8,128)(2,1)S(1)}, bf16[896,256]{1,0:T(8,128)(2,1)}, u32[]{:S(2)}) copy-start(bf16[896,256]{1,0:T(8,128)(2,1)} %constant.25.clone.gather_ref) | copy-start | bytes 1376260
  69.5 28.6 %copy-start.3 = (bf16[512,224]{1,0:T(8,128)(2,1)S(1)}, bf16[512,224]{1,0:T(8,128)(2,1)}, u32[]{:S(2)}) copy-start(bf16[512,224]{1,0:T(8,128)(2,1)} %constant.26.clone.expand_ref) | copy-start | bytes 688132
  69.6 28.6 %copy-start.6 = (f32[3,64,128]{2,1,0:T(8,128)S(1)}, f32[3,64,128]{2,1,0:T(8,128)}, u32[]{:S(2)}) copy-start(f32[3,64,128]{2,1,0:T(8,128)} %magnet_ref.1) | copy-start | bytes 294916
  69.6 28.6 %copy-start.8 = (f32[64,128]{1,0:T(8,128)S(1)}, f32[64,128]{1,0:T(8,128)}, u32[]{:S(2)}) copy-start(f32[64,128]{1,0:T(8,128)} %stiff_ref.1) | copy-start | bytes 98308

commit v6 on v5

--- a/solution.py
+++ b/solution.py
@@ -111,11 +111,11 @@
     cos, sin = wave(k2x, x_l, 64)
     x_last = deep(np.concatenate([cos, sin], 1))
     cos, sin = wave(x_l, k2x, 64)
-    x_lead = deep(np.concatenate([np.concatenate([cos, sin], 1)] * 2, 0))
+    x_lead = deep(np.concatenate([cos, sin], 1))
     cos, sin = wave(x_l, k1x, length)
-    own = np.concatenate([np.concatenate([cos, -cos], 1), np.concatenate([sin, -sin], 1)], 0)
-    other = np.concatenate([np.concatenate([-sin, -sin], 1), np.concatenate([cos, cos], 1)], 0)
-    x_twists = np.concatenate([x_twist, np.stack([own, other])], 1).astype(np.float32)
+    own = [np.concatenate([cos, -cos], 1), np.concatenate([sin, -sin], 1)]
+    other = [np.concatenate([-sin, -sin], 1), np.concatenate([cos, cos], 1)]
+    x_twists = np.concatenate([x_twist, np.stack(own + other)], 0).astype(np.float32)
     return {
         "y": (y_gather, y_expand),
         "x": (x_first, x_twists, x_last, x_lead, x_back),
@@ -254,45 +254,66 @@
 def spectral_body(
     in_ref, kern_ref, first_ref, twist_ref, last_ref, lead_ref, back_ref, out_ref
 ):
-    columns = [in_ref[pl.ds(j, cols_n, stride=16), :] for j in range(12)]
-    section = stacked_product(first_ref[...], jnp.concatenate(columns, 1))
     sign = half_sign(64)
-    own, other = twist_ref[0, :64, :], twist_ref[1, :64, :]
-    turned = []
-    for j in range(12):
-        block = section[:, 128 * j : 128 * j + 128]
-        block = block[:64] + half_turn(block[64:]) * sign
-        block = block * own + half_turn(block) * other
-        turned.append(block)
-        turned.append(half_turn(block) * sign)
-    freq = deep_product(last_ref[...], jnp.concatenate(turned, 0), 1)
+    own, other = twist_ref[0], twist_ref[1]
     kern = spread_kern(kern_ref)
-    sources = []
-    for target in range(3):
-        for k in range(4):
-            total = None
-            for b in range(3):
-                j = 4 * b + k
-                term = kern[tensor_slots[target][b]][k] * freq[:, 128 * j : 128 * j + 128]
-                total = term if total is None else total + term
-            sources.append(jnp.concatenate([total, -half_turn(total) * sign], 0))
-    section = deep_product(lead_ref[...], jnp.concatenate(sources, 1), 0)
-    own, other = twist_ref[0, 64:, :], twist_ref[1, 64:, :]
-    turned = []
-    for j in range(12):
-        block = section[:, 128 * j : 128 * j + 128]
-        turned.append(block * own + half_turn(block) * other)
-    result = deep_product(back_ref[...], jnp.concatenate(turned, 0), 1)
     scale = -1.0 / (length * length)
     lane = lane_index((cols_n, 128))
     zero_weight = jnp.where(lane < 64, 1.0, 0.0).astype(f32)
     is_zero = jnp.logical_and(lax.axis_index("row") == 0, lax.axis_index("col") == 0)
-    for j in range(12):
-        block = result[:, 128 * j : 128 * j + 128]
-        weight = jnp.full((cols_n, 128), 2.0, f32)
-        if j % 4 == 0:
-            weight = jnp.where(is_zero, zero_weight, weight)
-        out_ref[pl.ds(j, cols_n, stride=12), :] = block * (weight * scale)
+
+    def enter(ks):
+        columns = [in_ref[pl.ds(4 * a + k, cols_n, stride=16), :] for a in range(3) for k in ks]
+        return stacked_product(first_ref[...], jnp.concatenate(columns, 1))
+
+    def spread(section):
+        turned = []
+        for j in range(section.shape[1] // 128):
+            block = section[:, 128 * j : 128 * j + 128]
+            block = block[:64] + half_turn(block[64:]) * sign
+            block = block * own + half_turn(block) * other
+            turned.append(block)
+            turned.append(half_turn(block) * sign)
+        return deep_product(last_ref[...], jnp.concatenate(turned, 0), 1)
+
+    def multiply(freq, ks):
+        sources = []
+        for target in range(3):
+            for n, k in enumerate(ks):
+                total = None
+                for b in range(3):
+                    j = len(ks) * b + n
+                    term = kern[tensor_slots[target][b]][k] * freq[:, 128 * j : 128 * j + 128]
+                    total = term if total is None else total + term
+                sources.append(jnp.concatenate([total, -half_turn(total) * sign], 0))
+        return deep_product(lead_ref[...], jnp.concatenate(sources, 1), 0)
+
+    def leave(section):
+        turned = []
+        for j in range(section.shape[1] // 128):
+            block = section[:, 128 * j : 128 * j + 128]
+            aside = half_turn(block)
+            turned.append(block * twist_ref[2] + aside * twist_ref[4])
+            turned.append(block * twist_ref[3] + aside * twist_ref[5])
+        return deep_product(back_ref[...], jnp.concatenate(turned, 0), 1)
+
+    def store(result, ks):
+        for a in range(3):
+            for n, k in enumerate(ks):
+                j = len(ks) * a + n
+                block = result[:, 128 * j : 128 * j + 128]
+                weight = jnp.full((cols_n, 128), 2.0, f32)
+                if k == 0:
+                    weight = jnp.where(is_zero, zero_weight, weight)
+                out_ref[pl.ds(4 * a + k, cols_n, stride=12), :] = block * (weight * scale)
+
+    groups = ((0,), (1,), (2,), (3,))
+    states = [enter(ks) for ks in groups]
+    states = [spread(state) for state in states]
+    states = [multiply(state, ks) for state, ks in zip(states, groups)]
+    states = [leave(state) for state in states]
+    for state, ks in zip(states, groups):
+        store(state, ks)
 
 
 def back_body(in_ref, gather_ref, out_ref):
@@ -329,13 +350,19 @@
     former = jnp.where(low, demag[0], half_turn(demag[1])).T
     demag = [former[:64], former[64:], demag[2].T[:64]]
 
-    start = halo_rows * jnp.maximum(row - 1, 0) + sums_rows
-    before_y = beside_y_ref[pl.ds(start, 2), :]
-    start = halo_rows * jnp.minimum(row + 1, rows_n - 1) + sums_rows
-    after_y = beside_y_ref[pl.ds(start, 2), :]
+    device = lax.broadcasted_iota(jnp.int32, (rows_n, 128), 0)
+
+    def side(index):
+        rows = []
+        for n in range(2):
+            halo = beside_y_ref[pl.ds(sums_rows + n, rows_n, stride=halo_rows), :]
+            rows.append(jnp.sum(jnp.where(device == index, halo, 0.0), 0, keepdims=True))
+        return rows
+
+    before_y, after_y = side(row - 1), side(row + 1)
     before_x = beside_x_ref[pl.ds(pl.multiple_of(16 * jnp.maximum(col - 1, 0), 16), 16), :]
     after_x = beside_x_ref[pl.ds(pl.multiple_of(16 * jnp.minimum(col + 1, cols_n - 1), 16), 16), :]
-    edges = jnp.concatenate([before_y, after_y, jnp.zeros((124, 128), f32)], 0).T
+    edges = jnp.concatenate(before_y + after_y + [jnp.zeros((124, 128), f32)], 0).T
     stack = [magnet_ref[0], magnet_ref[1], magnet_ref[2], stiff_ref[...]]
     lane = lane_index((cells, 128))
     sub = lax.broadcasted_iota(jnp.int32, (cells, 128), 0)

time: 99.8 us -> 99.6 us (level)
  no operation moved by 1% of the time
where the time goes in v6:
time: 99.6 us; the launch traced here: 99.2 us
  blocking collectives  93.2 us (94%)
  Pallas kernels  5.81 us (6%)
    all_to_all x4, blocking collectives, exchange(): lax.all_to_all(array, axis, split_axis=0, concat_axis=0, tiled=True)  93.2 us
    pallas_call x5, Pallas kernels, call(): pl.pallas_call(body, out_shape=shapes, in_specs=[in_spec] * len(args), ou...  5.81 us

profile of v6, /device:TPU:2, one launch (start us, length us, event | category | flops | bytes accessed | tf_op | source)
XLA Modules:
  0.0 99.2 jit_solution(4003162777897306874)
XLA Ops:
  0.0 2.1 %shard_map.118 = (f32[704,128]{1,0:T(8,128)}, f32[8,128]{1,0:T(8,128)S(1)}) custom-call(f32[3,64,128]{2,1,0:T(8,128)} %magnet_ref.1, f32[64,128]{1,0:T(8,128)} %stiff_ref.1, f32[46,128]{1,0:T(8,128)} %constant.18.clone.gather_hbm), custom_call_target="tpu_custom_call" | custom-call | flops 100000000 | bytes 1000000 | tf_op jit(solution)/shard_map/pallas_call | solution.py:412
  2.1 0.0 copy-start.2
  2.1 37.5 %all_to_all.20 = f32[16,11,4,128]{3,2,1,0:T(4,128)S(1)} all-to-all(f32[16,11,4,128]{3,2,1,0:T(4,128)} %bitcast.23), channel_id=1, replica_groups=mesh['row'=16,'col'=32] {'row'}, dimensions={0} | all-to-all | bytes 720896 | tf_op jit(solution)/shard_map/all_to_all | solution.py:428
  39.6 0.0 copy-done.2
  39.6 0.0 copy-start.4
  39.6 0.0 copy-start.9
  39.6 0.0 copy-start.10
  39.6 0.5 shard_map.119
  40.1 0.0 copy-start.1
  40.1 0.0 copy-start.6
  40.1 0.0 copy-start.7
  40.1 15.3 %all_to_all.21 = f32[32,2,8,128]{3,2,1,0:T(8,128)S(1)} all-to-all(f32[32,2,8,128]{3,2,1,0:T(8,128)S(1)} %bitcast.19), channel_id=1, replica_groups=mesh['row'=16,'col'=32] {'col'}, dimensions={0} | all-to-all | bytes 524288 | tf_op jit(solution)/shard_map/all_to_all | solution.py:428
  55.4 0.0 copy-done.4
  55.4 0.0 copy-done.9
  55.4 0.0 copy-done.10
  55.4 0.0 copy-done.1
  55.4 0.0 copy-done.6
  55.4 0.0 copy-done.7
  55.4 0.0 copy-start
  55.5 1.5 %shard_map.120 = f32[384,128]{1,0:T(8,128)S(1)} custom-call(f32[512,128]{1,0:T(8,128)S(1)} %bitcast.15, f32[768,128]{1,0:T(8,128)S(1)} %bitcast.22, bf16[128,96]{1,0:T(8,128)(2,1)S(1)} %copy-done.10, f32[6,64,128]{2,1,0:T(8,128)S(1)} %copy-done.4, bf16[128,256]{1,0:T(8,128)(2,1)S(1)} %copy-done.7, bf16[128,256]{1,0:T(8,128)(2,1)S(1)} %copy-done.6, ...), custom_call_target="tpu_custom_call" | custom-call | flops 100000000 | bytes 1000000 | tf_op jit(solution)/shard_map/pallas_call | solution.py:412
  56.9 11.9 %all_to_all.22 = f32[32,3,4,128]{3,2,1,0:T(4,128)S(1)} all-to-all(f32[32,3,4,128]{3,2,1,0:T(4,128)S(1)} %bitcast.20), channel_id=1, replica_groups=mesh['row'=16,'col'=32] {'col'}, dimensions={0} | all-to-all | bytes 393216 | tf_op jit(solution)/shard_map/all_to_all | solution.py:428
  68.8 0.0 copy-done
  68.8 0.5 shard_map.121
  69.3 0.0 copy-start.3
  69.3 0.0 copy-start.5
  69.3 0.0 copy-start.8
  69.4 28.6 %all_to_all.23 = f32[16,21,2,128]{3,2,1,0:T(2,128)S(1)} all-to-all(f32[16,21,2,128]{3,2,1,0:T(2,128)S(1)} %bitcast.18), channel_id=1, replica_groups=mesh['row'=16,'col'=32] {'row'}, dimensions={0} | all-to-all | bytes 688128 | tf_op jit(solution)/shard_map/all_to_all | solution.py:428
  97.9 0.0 copy-done.3
  97.9 0.0 copy-done.5
  97.9 0.0 copy-done.8
  97.9 1.3 %shard_map.122 = f32[3,64,128]{2,1,0:T(8,128)} custom-call(f32[672,128]{1,0:T(8,128)S(1)} %bitcast.17, f32[3,64,128]{2,1,0:T(8,128)S(1)} %copy-done.5, f32[64,128]{1,0:T(8,128)S(1)} %copy-done.8, f32[704,128]{1,0:T(8,128)S(1)} %bitcast.14, f32[512,128]{1,0:T(8,128)S(1)} %bitcast.16, bf16[512,224]{1,0:T(8,128)(2,1)S(1)} %copy-done.3), custom_call_target="tpu_custom_call" | custom-call | flops 100000000 | bytes 1000000 | tf_op jit(solution)/shard_map/pallas_call | solution.py:412
Async XLA Ops:
  2.1 37.5 %copy-start.2 = (bf16[512,224]{1,0:T(8,128)(2,1)S(1)}, bf16[512,224]{1,0:T(8,128)(2,1)}, u32[]{:S(2)}) copy-start(bf16[512,224]{1,0:T(8,128)(2,1)} %constant.19.clone.expand_ref) | copy-start | bytes 688132
  39.6 15.8 %copy-start.4 = (f32[6,64,128]{2,1,0:T(8,128)S(1)}, f32[6,64,128]{2,1,0:T(8,128)}, u32[]{:S(2)}) copy-start(f32[6,64,128]{2,1,0:T(8,128)} %constant.21.clone.twist_ref) | copy-start | bytes 589828
  39.6 15.8 %copy-start.9 = (bf16[64,256]{1,0:T(8,128)(2,1)S(1)}, bf16[64,256]{1,0:T(8,128)(2,1)}, u32[]{:S(2)}) copy-start(bf16[64,256]{1,0:T(8,128)(2,1)} %constant.24.clone.back_ref) | copy-start | bytes 98308
  39.6 15.8 %copy-start.10 = (bf16[128,96]{1,0:T(8,128)(2,1)S(1)}, bf16[128,96]{1,0:T(8,128)(2,1)}, u32[]{:S(2)}) copy-start(bf16[128,96]{1,0:T(8,128)(2,1)} %constant.20.clone.first_ref) | copy-start | bytes 73732
  40.1 15.3 %copy-start.1 = (f32[6,4,4096]{2,1,0:T(4,128)S(1)}, f32[6,4,4096]{2,1,0:T(4,128)}, u32[]{:S(2)}) copy-start(f32[6,4,4096]{2,1,0:T(4,128)} %param.14) | copy-start | bytes 1179652
  40.1 15.3 %copy-start.6 = (bf16[128,256]{1,0:T(8,128)(2,1)S(1)}, bf16[128,256]{1,0:T(8,128)(2,1)}, u32[]{:S(2)}) copy-start(bf16[128,256]{1,0:T(8,128)(2,1)} %constant.23.clone.lead_ref) | copy-start | bytes 196612
  40.1 15.3 %copy-start.7 = (bf16[128,256]{1,0:T(8,128)(2,1)S(1)}, bf16[128,256]{1,0:T(8,128)(2,1)}, u32[]{:S(2)}) copy-start(bf16[128,256]{1,0:T(8,128)(2,1)} %constant.22.clone.last_ref) | copy-start | bytes 196612
  55.4 13.4 %copy-start = (bf16[896,256]{1,0:T(8,128)(2,1)S(1)}, bf16[896,256]{1,0:T(8,128)(2,1)}, u32[]{:S(2)}) copy-start(bf16[896,256]{1,0:T(8,128)(2,1)} %constant.25.clone.gather_ref) | copy-start | bytes 1376260
  69.3 28.6 %copy-start.3 = (bf16[512,224]{1,0:T(8,128)(2,1)S(1)}, bf16[512,224]{1,0:T(8,128)(2,1)}, u32[]{:S(2)}) copy-start(bf16[512,224]{1,0:T(8,128)(2,1)} %constant.26.clone.expand_ref) | copy-start | bytes 688132
  69.3 28.6 %copy-start.5 = (f32[3,64,128]{2,1,0:T(8,128)S(1)}, f32[3,64,128]{2,1,0:T(8,128)}, u32[]{:S(2)}) copy-start(f32[3,64,128]{2,1,0:T(8,128)} %magnet_ref.1) | copy-start | bytes 294916
  69.3 28.6 %copy-start.8 = (f32[64,128]{1,0:T(8,128)S(1)}, f32[64,128]{1,0:T(8,128)}, u32[]{:S(2)}) copy-start(f32[64,128]{1,0:T(8,128)} %stiff_ref.1) | copy-start | bytes 98308

commit v7 on v6

--- a/solution.py
+++ b/solution.py
@@ -167,19 +167,8 @@
     return jnp.where(lane_index((rows, 128)) < 64, 1.0, -1.0).astype(f32)
 
 
-def pack_body(
-    magnet_hbm, stiff_hbm, gather_hbm, out_ref, edge_ref, magnet_ref, stiff_ref, gather_ref, sems
-):
-    copies = [
-        pltpu.make_async_copy(magnet_hbm, magnet_ref, sems.at[0]),
-        pltpu.make_async_copy(stiff_hbm, stiff_ref, sems.at[1]),
-        pltpu.make_async_copy(gather_hbm, gather_ref, sems.at[2]),
-    ]
-    for copy in copies:
-        copy.start()
-    for copy in copies:
-        copy.wait()
-    values = jnp.concatenate([magnet_ref[0], magnet_ref[1], magnet_ref[2]], 0)
+def pack_body(film_ref, gather_ref, out_ref, edge_ref):
+    values = jnp.concatenate([film_ref[a] for a in range(3)], 0)
     size = rows_n * modes
     turns = gather_ref[0 : 2 * rows_n, :]
     sides = [gather_ref[2 * rows_n + n : 2 * rows_n + n + 1, :] for n in range(modes)]
@@ -195,17 +184,15 @@
     last = jnp.concatenate([sums[:size, 128:], sums[size:, 128:]], 1)
     blocks = (jnp.where(low, re, half_turn(im)), jnp.where(low, half_turn(re), im), last)
     store_chunks(out_ref, halo_rows, blocks)
-    former = jnp.concatenate([magnet_ref[0], magnet_ref[1]], 0).T
-    latter = jnp.concatenate([magnet_ref[2], stiff_ref[...]], 0).T
+    former = jnp.concatenate([film_ref[0], film_ref[1]], 0).T
+    latter = jnp.concatenate([film_ref[2], film_ref[3]], 0).T
     after = lax.broadcasted_iota(jnp.int32, (rows_n, lanes), 0) > lax.axis_index("row")
     for n, sides in enumerate((former, latter)):
         edges = jnp.where(after, sides[127:], sides[:1])
         out_ref[pl.ds(sums_rows + n, rows_n, stride=halo_rows), :] = edges
-    for a in range(3):
-        edge_ref[a : a + 1, :] = magnet_ref[a, :1, :]
-        edge_ref[4 + a : 5 + a, :] = magnet_ref[a, cells - 1 :, :]
-    edge_ref[3:4, :] = stiff_ref[:1, :]
-    edge_ref[7:8, :] = stiff_ref[cells - 1 :, :]
+    for n in range(4):
+        edge_ref[n : n + 1, :] = film_ref[n, :1, :]
+        edge_ref[4 + n : 5 + n, :] = film_ref[n, cells - 1 :, :]
 
 
 def spread_kern(kern_ref):
@@ -339,7 +326,7 @@
     )
 
 
-def torque_body(in_ref, magnet_ref, stiff_ref, beside_y_ref, beside_x_ref, expand_ref, out_ref):
+def torque_body(in_ref, film_ref, beside_y_ref, beside_x_ref, expand_ref, out_ref):
     row, col = lax.axis_index("row"), lax.axis_index("col")
     sums = tall_product(expand_ref[...], load_chunks(in_ref, sums_rows))
     demag = []
@@ -363,7 +350,7 @@
     before_x = beside_x_ref[pl.ds(pl.multiple_of(16 * jnp.maximum(col - 1, 0), 16), 16), :]
     after_x = beside_x_ref[pl.ds(pl.multiple_of(16 * jnp.minimum(col + 1, cols_n - 1), 16), 16), :]
     edges = jnp.concatenate(before_y + after_y + [jnp.zeros((124, 128), f32)], 0).T
-    stack = [magnet_ref[0], magnet_ref[1], magnet_ref[2], stiff_ref[...]]
+    stack = [film_ref[n] for n in range(4)]
     lane = lane_index((cells, 128))
     sub = lax.broadcasted_iota(jnp.int32, (cells, 128), 0)
 
@@ -430,20 +417,9 @@
 
 def local(magnet, stiffness, kern):
     constant = {name: [jnp.asarray(t) for t in group] for name, group in tables().items()}
+    film = jnp.concatenate([magnet, stiffness[None]], 0)
     packed, edge = call(
-        pack_body,
-        [(rows_n * halo_rows, 128), (8, 128)],
-        magnet,
-        stiffness,
-        constant["y"][0],
-        in_spec=in_hbm,
-        vmem=55208 * 2**10,
-        scratch=[
-            pltpu.VMEM((3, cells, lanes), f32),
-            pltpu.VMEM((cells, lanes), f32),
-            pltpu.VMEM(constant["y"][0].shape, f32),
-            pltpu.SemaphoreType.DMA((3,)),
-        ],
+        pack_body, [(rows_n * halo_rows, 128), (8, 128)], film, constant["y"][0]
     )
     sums = exchange(packed, "row", rows_n)
     (columns,) = call(forward_body, [(512, 128)], sums, edge, constant["y"][1])
@@ -454,7 +430,7 @@
     (coef,) = call(back_body, [(rows_n * sums_rows, 128)], inverse_x, constant["z"][0])
     coef = exchange(coef, "row", rows_n)
     (torque,) = call(
-        torque_body, [(3, 64, 128)], coef, magnet, stiffness, sums, columns, constant["z"][1]
+        torque_body, [(3, 64, 128)], coef, film, sums, columns, constant["z"][1]
     )
     return torque
 

time: 99.6 us -> 98.5 us (0.989)
  Pallas kernels: 5.81 us -> 4.13 us
    pallas_call x5, Pallas kernels: 5.81 us -> 4.13 us  [call(): pl.pallas_call(body, out_shape=shapes, in_specs=[in_spec] * len(args), ou...]
where the time goes in v7:
time: 98.5 us; the launch traced here: 98.3 us
  blocking collectives  93 us (94%)
  Pallas kernels  4.13 us (4%)
    all_to_all x4, blocking collectives, exchange(): lax.all_to_all(array, axis, split_axis=0, concat_axis=0, tiled=True)  93 us
    pallas_call x5, Pallas kernels, call(): pl.pallas_call(body, out_shape=shapes, in_specs=[in_spec] * len(args), ou...  4.13 us

profile of v7, /device:TPU:2, one launch (start us, length us, event | category | flops | bytes accessed | tf_op | source)
XLA Modules:
  0.0 98.3 jit_solution(4594574700857298578)
XLA Ops:
  0.0 0.0 copy-start.9
  0.0 0.9 pad_maximum_fusion.film_ref
  0.9 0.0 copy-done.9
  0.9 0.4 shard_map.118
  1.4 0.0 copy-start.2
  1.4 37.3 %all_to_all.20 = f32[16,11,4,128]{3,2,1,0:T(4,128)S(1)} all-to-all(f32[16,11,4,128]{3,2,1,0:T(4,128)S(1)} %bitcast.24), channel_id=1, replica_groups=mesh['row'=16,'col'=32] {'row'}, dimensions={0} | all-to-all | bytes 720896 | tf_op jit(solution)/shard_map/all_to_all | solution.py:415
  38.7 0.0 copy-done.2
  38.7 0.0 copy-start.4
  38.7 0.0 copy-start.7
  38.7 0.0 copy-start.8
  38.7 0.5 shard_map.119
  39.1 0.0 copy-start.1
  39.2 0.0 copy-start.5
  39.2 0.0 copy-start.6
  39.2 15.3 %all_to_all.21 = f32[32,2,8,128]{3,2,1,0:T(8,128)S(1)} all-to-all(f32[32,2,8,128]{3,2,1,0:T(8,128)S(1)} %bitcast.20), channel_id=1, replica_groups=mesh['row'=16,'col'=32] {'col'}, dimensions={0} | all-to-all | bytes 524288 | tf_op jit(solution)/shard_map/all_to_all | solution.py:415
  54.5 0.0 copy-done.4
  54.5 0.0 copy-done.7
  54.5 0.0 copy-done.8
  54.5 0.0 copy-done.1
  54.5 0.0 copy-done.5
  54.5 0.0 copy-done.6
  54.5 0.0 copy-start
  54.5 1.5 %shard_map.120 = f32[384,128]{1,0:T(8,128)S(1)} custom-call(f32[512,128]{1,0:T(8,128)S(1)} %bitcast.16, f32[768,128]{1,0:T(8,128)S(1)} %bitcast.23, bf16[128,96]{1,0:T(8,128)(2,1)S(1)} %copy-done.8, f32[6,64,128]{2,1,0:T(8,128)S(1)} %copy-done.4, bf16[128,256]{1,0:T(8,128)(2,1)S(1)} %copy-done.6, bf16[128,256]{1,0:T(8,128)(2,1)S(1)} %copy-done.5, ...), custom_call_target="tpu_custom_call" | custom-call | flops 100000000 | bytes 1000000 | tf_op jit(solution)/shard_map/pallas_call | solution.py:399
  56.0 11.9 %all_to_all.22 = f32[32,3,4,128]{3,2,1,0:T(4,128)S(1)} all-to-all(f32[32,3,4,128]{3,2,1,0:T(4,128)S(1)} %bitcast.21), channel_id=1, replica_groups=mesh['row'=16,'col'=32] {'col'}, dimensions={0} | all-to-all | bytes 393216 | tf_op jit(solution)/shard_map/all_to_all | solution.py:415
  67.8 0.0 copy-done
  67.8 0.5 shard_map.121
  68.4 0.0 copy-start.3
  68.4 28.6 %all_to_all.23 = f32[16,21,2,128]{3,2,1,0:T(2,128)S(1)} all-to-all(f32[16,21,2,128]{3,2,1,0:T(2,128)S(1)} %bitcast.19), channel_id=1, replica_groups=mesh['row'=16,'col'=32] {'row'}, dimensions={0} | all-to-all | bytes 688128 | tf_op jit(solution)/shard_map/all_to_all | solution.py:415
  97.0 0.0 copy-done.3
  97.0 1.3 %shard_map.122 = f32[3,64,128]{2,1,0:T(8,128)} custom-call(f32[672,128]{1,0:T(8,128)S(1)} %bitcast.18, f32[4,64,128]{2,1,0:T(8,128)S(1)} %pad_maximum_fusion.film_ref, f32[704,128]{1,0:T(8,128)S(1)} %bitcast.15, f32[512,128]{1,0:T(8,128)S(1)} %bitcast.17, bf16[512,224]{1,0:T(8,128)(2,1)S(1)} %copy-done.3), custom_call_target="tpu_custom_call" | custom-call | flops 100000000 | bytes 1000000 | tf_op jit(solution)/shard_map/pallas_call | solution.py:399
Async XLA Ops:
  0.0 0.9 copy-start.9
  1.4 37.3 %copy-start.2 = (bf16[512,224]{1,0:T(8,128)(2,1)S(1)}, bf16[512,224]{1,0:T(8,128)(2,1)}, u32[]{:S(2)}) copy-start(bf16[512,224]{1,0:T(8,128)(2,1)} %constant.19.clone.expand_ref) | copy-start | bytes 688132
  38.7 15.8 %copy-start.4 = (f32[6,64,128]{2,1,0:T(8,128)S(1)}, f32[6,64,128]{2,1,0:T(8,128)}, u32[]{:S(2)}) copy-start(f32[6,64,128]{2,1,0:T(8,128)} %constant.21.clone.twist_ref) | copy-start | bytes 589828
  38.7 15.8 %copy-start.7 = (bf16[64,256]{1,0:T(8,128)(2,1)S(1)}, bf16[64,256]{1,0:T(8,128)(2,1)}, u32[]{:S(2)}) copy-start(bf16[64,256]{1,0:T(8,128)(2,1)} %constant.24.clone.back_ref) | copy-start | bytes 98308
  38.7 15.8 %copy-start.8 = (bf16[128,96]{1,0:T(8,128)(2,1)S(1)}, bf16[128,96]{1,0:T(8,128)(2,1)}, u32[]{:S(2)}) copy-start(bf16[128,96]{1,0:T(8,128)(2,1)} %constant.20.clone.first_ref) | copy-start | bytes 73732
  39.1 15.3 %copy-start.1 = (f32[6,4,4096]{2,1,0:T(4,128)S(1)}, f32[6,4,4096]{2,1,0:T(4,128)}, u32[]{:S(2)}) copy-start(f32[6,4,4096]{2,1,0:T(4,128)} %param.14) | copy-start | bytes 1179652
  39.2 15.3 %copy-start.5 = (bf16[128,256]{1,0:T(8,128)(2,1)S(1)}, bf16[128,256]{1,0:T(8,128)(2,1)}, u32[]{:S(2)}) copy-start(bf16[128,256]{1,0:T(8,128)(2,1)} %constant.23.clone.lead_ref) | copy-start | bytes 196612
  39.2 15.3 %copy-start.6 = (bf16[128,256]{1,0:T(8,128)(2,1)S(1)}, bf16[128,256]{1,0:T(8,128)(2,1)}, u32[]{:S(2)}) copy-start(bf16[128,256]{1,0:T(8,128)(2,1)} %constant.22.clone.last_ref) | copy-start | bytes 196612
  54.5 13.3 %copy-start = (bf16[896,256]{1,0:T(8,128)(2,1)S(1)}, bf16[896,256]{1,0:T(8,128)(2,1)}, u32[]{:S(2)}) copy-start(bf16[896,256]{1,0:T(8,128)(2,1)} %constant.25.clone.gather_ref) | copy-start | bytes 1376260
  68.4 28.6 %copy-start.3 = (bf16[512,224]{1,0:T(8,128)(2,1)S(1)}, bf16[512,224]{1,0:T(8,128)(2,1)}, u32[]{:S(2)}) copy-start(bf16[512,224]{1,0:T(8,128)(2,1)} %constant.26.clone.expand_ref) | copy-start | bytes 688132

commit v8 on v7

--- a/solution.py
+++ b/solution.py
@@ -22,7 +22,7 @@
 f32 = jnp.float32
 
 
-modes = 14
+modes = 21
 sums_rows = 3 * modes
 halo_rows = sums_rows + 2
 

time: 98.5 us -> 115 us (1.17)
  the two profiles are of different devices: /device:TPU:2 before, /device:TPU:32 now
where the time goes in v8:
time: 115 us
  blocking collectives  109 us (95%)
  Pallas kernels  4.61 us (4%)
    all_to_all x4, blocking collectives, exchange(): lax.all_to_all(array, axis, split_axis=0, concat_axis=0, tiled=True)  109 us
    pallas_call x5, Pallas kernels, call(): pl.pallas_call(body, out_shape=shapes, in_specs=[in_spec] * len(args), ou...  4.61 us

profile of v8, /device:TPU:32, one launch (start us, length us, event | category | flops | bytes accessed | tf_op | source)
XLA Modules:
  0.0 114.9 jit_solution(5397229608624585663)
XLA Ops:
  0.0 0.0 copy-start.9
  0.0 0.9 pad_maximum_fusion.film_ref
  0.9 0.0 copy-done.9
  0.9 0.5 shard_map.118
  1.4 0.0 copy-start.2
  1.4 47.5 %all_to_all.20 = f32[16,65,1,128]{3,2,1,0:T(1,128)S(1)} all-to-all(f32[16,65,1,128]{3,2,1,0:T(1,128)S(1)} %bitcast.23), channel_id=1, replica_groups=mesh['row'=16,'col'=32] {'row'}, dimensions={0} | all-to-all | bytes 1064960 | tf_op jit(solution)/shard_map/all_to_all | solution.py:415
  48.9 0.0 copy-done.2
  48.9 0.0 copy-start.4
  48.9 0.0 copy-start.7
  48.9 0.0 copy-start.8
  48.9 0.6 shard_map.119
  49.5 0.0 copy-start.1
  49.5 0.0 copy-start.5
  49.6 0.0 copy-start.6
  49.6 16.2 %all_to_all.21 = f32[32,2,8,128]{3,2,1,0:T(8,128)S(1)} all-to-all(f32[32,2,8,128]{3,2,1,0:T(8,128)S(1)} %bitcast.20), channel_id=1, replica_groups=mesh['row'=16,'col'=32] {'col'}, dimensions={0} | all-to-all | bytes 524288 | tf_op jit(solution)/shard_map/all_to_all | solution.py:415
  65.8 0.0 copy-done.4
  65.8 0.0 copy-done.7
  65.8 0.0 copy-done.8
  65.8 0.0 copy-done.1
  65.8 0.0 copy-done.5
  65.8 0.0 copy-done.6
  65.8 0.0 copy-start
  65.8 1.5 %shard_map.120 = f32[384,128]{1,0:T(8,128)S(1)} custom-call(f32[512,128]{1,0:T(8,128)S(1)} %bitcast.16, f32[768,128]{1,0:T(8,128)S(1)} %bitcast.24, bf16[128,96]{1,0:T(8,128)(2,1)S(1)} %copy-done.8, f32[6,64,128]{2,1,0:T(8,128)S(1)} %copy-done.4, bf16[128,256]{1,0:T(8,128)(2,1)S(1)} %copy-done.6, bf16[128,256]{1,0:T(8,128)(2,1)S(1)} %copy-done.5, ...), custom_call_target="tpu_custom_call" | custom-call | flops 100000000 | bytes 1000000 | tf_op jit(solution)/shard_map/pallas_call | solution.py:399
  67.3 11.9 %all_to_all.22 = f32[32,3,4,128]{3,2,1,0:T(4,128)S(1)} all-to-all(f32[32,3,4,128]{3,2,1,0:T(4,128)S(1)} %bitcast.21), channel_id=1, replica_groups=mesh['row'=16,'col'=32] {'col'}, dimensions={0} | all-to-all | bytes 393216 | tf_op jit(solution)/shard_map/all_to_all | solution.py:415
  79.2 0.0 copy-done
  79.2 0.6 shard_map.121
  79.8 0.0 copy-start.3
  79.8 33.6 %all_to_all.23 = f32[16,63,1,128]{3,2,1,0:T(1,128)S(1)} all-to-all(f32[16,63,1,128]{3,2,1,0:T(1,128)S(1)} %bitcast.19), channel_id=1, replica_groups=mesh['row'=16,'col'=32] {'row'}, dimensions={0} | all-to-all | bytes 1032192 | tf_op jit(solution)/shard_map/all_to_all | solution.py:415
  113.4 0.0 copy-done.3
  113.4 1.4 %shard_map.122 = f32[3,64,128]{2,1,0:T(8,128)} custom-call(f32[1008,128]{1,0:T(8,128)S(1)} %bitcast.18, f32[4,64,128]{2,1,0:T(8,128)S(1)} %pad_maximum_fusion.film_ref, f32[1040,128]{1,0:T(8,128)S(1)} %bitcast.15, f32[512,128]{1,0:T(8,128)S(1)} %bitcast.17, bf16[512,336]{1,0:T(8,128)(2,1)S(1)} %copy-done.3), custom_call_target="tpu_custom_call" | custom-call | flops 100000000 | bytes 1000000 | tf_op jit(solution)/shard_map/pallas_call | solution.py:399
Async XLA Ops:
  0.0 0.9 copy-start.9
  1.4 47.5 %copy-start.2 = (bf16[512,336]{1,0:T(8,128)(2,1)S(1)}, bf16[512,336]{1,0:T(8,128)(2,1)}, u32[]{:S(2)}) copy-start(bf16[512,336]{1,0:T(8,128)(2,1)} %constant.19.clone.expand_ref) | copy-start | bytes 1032196
  48.9 16.9 %copy-start.4 = (f32[6,64,128]{2,1,0:T(8,128)S(1)}, f32[6,64,128]{2,1,0:T(8,128)}, u32[]{:S(2)}) copy-start(f32[6,64,128]{2,1,0:T(8,128)} %constant.21.clone.twist_ref) | copy-start | bytes 589828
  48.9 16.9 %copy-start.7 = (bf16[64,256]{1,0:T(8,128)(2,1)S(1)}, bf16[64,256]{1,0:T(8,128)(2,1)}, u32[]{:S(2)}) copy-start(bf16[64,256]{1,0:T(8,128)(2,1)} %constant.24.clone.back_ref) | copy-start | bytes 98308
  48.9 16.9 %copy-start.8 = (bf16[128,96]{1,0:T(8,128)(2,1)S(1)}, bf16[128,96]{1,0:T(8,128)(2,1)}, u32[]{:S(2)}) copy-start(bf16[128,96]{1,0:T(8,128)(2,1)} %constant.20.clone.first_ref) | copy-start | bytes 73732
  49.5 16.2 %copy-start.1 = (f32[6,4,4096]{2,1,0:T(4,128)S(1)}, f32[6,4,4096]{2,1,0:T(4,128)}, u32[]{:S(2)}) copy-start(f32[6,4,4096]{2,1,0:T(4,128)} %param.14) | copy-start | bytes 1179652
  49.5 16.2 %copy-start.5 = (bf16[128,256]{1,0:T(8,128)(2,1)S(1)}, bf16[128,256]{1,0:T(8,128)(2,1)}, u32[]{:S(2)}) copy-start(bf16[128,256]{1,0:T(8,128)(2,1)} %constant.23.clone.lead_ref) | copy-start | bytes 196612
  49.6 16.2 %copy-start.6 = (bf16[128,256]{1,0:T(8,128)(2,1)S(1)}, bf16[128,256]{1,0:T(8,128)(2,1)}, u32[]{:S(2)}) copy-start(bf16[128,256]{1,0:T(8,128)(2,1)} %constant.22.clone.last_ref) | copy-start | bytes 196612
  65.8 13.4 %copy-start = (bf16[1344,256]{1,0:T(8,128)(2,1)S(1)}, bf16[1344,256]{1,0:T(8,128)(2,1)}, u32[]{:S(2)}) copy-start(bf16[1344,256]{1,0:T(8,128)(2,1)} %constant.25.clone.gather_ref) | copy-start | bytes 2064388
  79.8 33.6 %copy-start.3 = (bf16[512,336]{1,0:T(8,128)(2,1)S(1)}, bf16[512,336]{1,0:T(8,128)(2,1)}, u32[]{:S(2)}) copy-start(bf16[512,336]{1,0:T(8,128)(2,1)} %constant.26.clone.expand_ref) | copy-start | bytes 1032196

commit v9 on v7

--- a/solution.py
+++ b/solution.py
@@ -40,7 +40,7 @@
 
 def thick(table):
     high, low = split_table(table)
-    return np.concatenate([high, low, high], 1)
+    return np.concatenate([high, low, high, low], 1)
 
 
 def tall(table):
@@ -49,9 +49,7 @@
 
 def deep(table):
     high, low = split_table(table)
-    return np.concatenate(
-        [np.concatenate([high, high], 1), np.concatenate([low, np.zeros_like(low)], 1)], 0
-    )
+    return np.concatenate([np.tile(high, (1, 2)), np.tile(low, (1, 2))], 0)
 
 
 def factors():
@@ -131,7 +129,7 @@
 
 def stacked_product(table, values):
     high, low = split(values)
-    return jnp.dot(table, jnp.concatenate([high, high, low], 0), preferred_element_type=f32)
+    return jnp.dot(table, jnp.concatenate([high, high, low, low], 0), preferred_element_type=f32)
 
 
 def tall_product(table, values):
@@ -148,11 +146,6 @@
     both = lax.dot_general(table, both, dims, preferred_element_type=f32)
     size = table.shape[0] // 2
     return both[:size] + both[size:]
-
-
-def last_dims_product(former, latter):
-    dims = (((1,), (1,)), ((), ()))
-    return lax.dot_general(former, latter, dims, preferred_element_type=f32)
 
 
 def half_turn(values):
@@ -175,10 +168,8 @@
     re = [turns[:rows_n] * side for side in sides]
     im = [turns[rows_n:] * side for side in sides]
     table_high, table_low = split(jnp.concatenate(re + im, 0))
-    high, low = split(values)
-    sums = last_dims_product(
-        jnp.concatenate([table_high, table_high], 1), jnp.concatenate([high, low], 1)
-    ) + last_dims_product(table_low, high)
+    table = jnp.concatenate([table_high, table_low], 0)
+    sums = deep_product(jnp.concatenate([table, table], 1), values, 1)
     low = lane_index((size, 128)) < 64
     re, im = sums[:size, :128], sums[size:, :128]
     last = jnp.concatenate([sums[:size, 128:], sums[size:, 128:]], 1)

time: 98.5 us -> 98.6 us (level)
  no operation moved by 1% of the time
where the time goes in v9:
time: 98.6 us; the launch traced here: 98.3 us
  blocking collectives  93 us (94%)
  Pallas kernels  4.14 us (4%)
    all_to_all x4, blocking collectives, exchange(): lax.all_to_all(array, axis, split_axis=0, concat_axis=0, tiled=True)  93 us
    pallas_call x5, Pallas kernels, call(): pl.pallas_call(body, out_shape=shapes, in_specs=[in_spec] * len(args), ou...  4.14 us

profile of v9, /device:TPU:2, one launch (start us, length us, event | category | flops | bytes accessed | tf_op | source)
XLA Modules:
  0.0 98.3 jit_solution(4942116252289078072)
XLA Ops:
  0.0 0.0 copy-start.9
  0.0 0.9 pad_maximum_fusion.film_ref
  0.9 0.0 copy-done.9
  0.9 0.4 shard_map.118
  1.4 0.0 copy-start.2
  1.4 37.3 %all_to_all.20 = f32[16,11,4,128]{3,2,1,0:T(4,128)S(1)} all-to-all(f32[16,11,4,128]{3,2,1,0:T(4,128)S(1)} %bitcast.24), channel_id=1, replica_groups=mesh['row'=16,'col'=32] {'row'}, dimensions={0} | all-to-all | bytes 720896 | tf_op jit(solution)/shard_map/all_to_all | solution.py:406
  38.7 0.0 copy-done.2
  38.7 0.0 copy-start.4
  38.7 0.0 copy-start.7
  38.7 0.0 copy-start.8
  38.7 0.5 shard_map.119
  39.2 0.0 copy-start.1
  39.2 0.0 copy-start.5
  39.2 0.0 copy-start.6
  39.2 15.3 %all_to_all.21 = f32[32,2,8,128]{3,2,1,0:T(8,128)S(1)} all-to-all(f32[32,2,8,128]{3,2,1,0:T(8,128)S(1)} %bitcast.20), channel_id=1, replica_groups=mesh['row'=16,'col'=32] {'col'}, dimensions={0} | all-to-all | bytes 524288 | tf_op jit(solution)/shard_map/all_to_all | solution.py:406
  54.5 0.0 copy-done.4
  54.5 0.0 copy-done.7
  54.5 0.0 copy-done.8
  54.5 0.0 copy-done.1
  54.5 0.0 copy-done.5
  54.5 0.0 copy-done.6
  54.5 0.0 copy-start
  54.5 1.5 %shard_map.120 = f32[384,128]{1,0:T(8,128)S(1)} custom-call(f32[512,128]{1,0:T(8,128)S(1)} %bitcast.16, f32[768,128]{1,0:T(8,128)S(1)} %bitcast.23, bf16[128,128]{1,0:T(8,128)(2,1)S(1)} %copy-done.8, f32[6,64,128]{2,1,0:T(8,128)S(1)} %copy-done.4, bf16[128,256]{1,0:T(8,128)(2,1)S(1)} %copy-done.6, bf16[128,256]{1,0:T(8,128)(2,1)S(1)} %copy-done.5, ...), custom_call_target="tpu_custom_call" | custom-call | flops 100000000 | bytes 1000000 | tf_op jit(solution)/shard_map/pallas_call | solution.py:390
  56.0 11.9 %all_to_all.22 = f32[32,3,4,128]{3,2,1,0:T(4,128)S(1)} all-to-all(f32[32,3,4,128]{3,2,1,0:T(4,128)S(1)} %bitcast.21), channel_id=1, replica_groups=mesh['row'=16,'col'=32] {'col'}, dimensions={0} | all-to-all | bytes 393216 | tf_op jit(solution)/shard_map/all_to_all | solution.py:406
  67.9 0.0 copy-done
  67.9 0.5 shard_map.121
  68.4 0.0 copy-start.3
  68.4 28.6 %all_to_all.23 = f32[16,21,2,128]{3,2,1,0:T(2,128)S(1)} all-to-all(f32[16,21,2,128]{3,2,1,0:T(2,128)S(1)} %bitcast.19), channel_id=1, replica_groups=mesh['row'=16,'col'=32] {'row'}, dimensions={0} | all-to-all | bytes 688128 | tf_op jit(solution)/shard_map/all_to_all | solution.py:406
  97.0 0.0 copy-done.3
  97.0 1.3 %shard_map.122 = f32[3,64,128]{2,1,0:T(8,128)} custom-call(f32[672,128]{1,0:T(8,128)S(1)} %bitcast.18, f32[4,64,128]{2,1,0:T(8,128)S(1)} %pad_maximum_fusion.film_ref, f32[704,128]{1,0:T(8,128)S(1)} %bitcast.15, f32[512,128]{1,0:T(8,128)S(1)} %bitcast.17, bf16[512,224]{1,0:T(8,128)(2,1)S(1)} %copy-done.3), custom_call_target="tpu_custom_call" | custom-call | flops 100000000 | bytes 1000000 | tf_op jit(solution)/shard_map/pallas_call | solution.py:390
Async XLA Ops:
  0.0 0.9 copy-start.9
  1.4 37.3 %copy-start.2 = (bf16[512,224]{1,0:T(8,128)(2,1)S(1)}, bf16[512,224]{1,0:T(8,128)(2,1)}, u32[]{:S(2)}) copy-start(bf16[512,224]{1,0:T(8,128)(2,1)} %constant.19.clone.expand_ref) | copy-start | bytes 688132
  38.7 15.8 %copy-start.4 = (f32[6,64,128]{2,1,0:T(8,128)S(1)}, f32[6,64,128]{2,1,0:T(8,128)}, u32[]{:S(2)}) copy-start(f32[6,64,128]{2,1,0:T(8,128)} %constant.21.clone.twist_ref) | copy-start | bytes 589828
  38.7 15.8 %copy-start.7 = (bf16[64,256]{1,0:T(8,128)(2,1)S(1)}, bf16[64,256]{1,0:T(8,128)(2,1)}, u32[]{:S(2)}) copy-start(bf16[64,256]{1,0:T(8,128)(2,1)} %constant.24.clone.back_ref) | copy-start | bytes 98308
  38.7 15.8 %copy-start.8 = (bf16[128,128]{1,0:T(8,128)(2,1)S(1)}, bf16[128,128]{1,0:T(8,128)(2,1)}, u32[]{:S(2)}) copy-start(bf16[128,128]{1,0:T(8,128)(2,1)} %constant.20.clone.first_ref) | copy-start | bytes 98308
  39.2 15.3 %copy-start.1 = (f32[6,4,4096]{2,1,0:T(4,128)S(1)}, f32[6,4,4096]{2,1,0:T(4,128)}, u32[]{:S(2)}) copy-start(f32[6,4,4096]{2,1,0:T(4,128)} %param.14) | copy-start | bytes 1179652
  39.2 15.3 %copy-start.5 = (bf16[128,256]{1,0:T(8,128)(2,1)S(1)}, bf16[128,256]{1,0:T(8,128)(2,1)}, u32[]{:S(2)}) copy-start(bf16[128,256]{1,0:T(8,128)(2,1)} %constant.23.clone.lead_ref) | copy-start | bytes 196612
  39.2 15.3 %copy-start.6 = (bf16[128,256]{1,0:T(8,128)(2,1)S(1)}, bf16[128,256]{1,0:T(8,128)(2,1)}, u32[]{:S(2)}) copy-start(bf16[128,256]{1,0:T(8,128)(2,1)} %constant.22.clone.last_ref) | copy-start | bytes 196612
  54.5 13.4 %copy-start = (bf16[896,256]{1,0:T(8,128)(2,1)S(1)}, bf16[896,256]{1,0:T(8,128)(2,1)}, u32[]{:S(2)}) copy-start(bf16[896,256]{1,0:T(8,128)(2,1)} %constant.25.clone.gather_ref) | copy-start | bytes 1376260
  68.4 28.6 %copy-start.3 = (bf16[512,224]{1,0:T(8,128)(2,1)S(1)}, bf16[512,224]{1,0:T(8,128)(2,1)}, u32[]{:S(2)}) copy-start(bf16[512,224]{1,0:T(8,128)(2,1)} %constant.26.clone.expand_ref) | copy-start | bytes 688132

commit v10 on v9

--- a/solution.py
+++ b/solution.py
@@ -99,7 +99,7 @@
     y_gather = np.concatenate([parts(turns), sides], 0).astype(np.float32)
     y_expand = tall(parts(expand[kappa]))
     z_gather = deep(parts(gather[:, kappa]))
-    z_expand = tall(parts(expand))
+    z_expand = np.ascontiguousarray(tall(parts(expand)).T)
 
     cos, sin = wave(k1x, col, 64)
     x_first = thick(np.concatenate([cos, sin], 0))
@@ -319,14 +319,14 @@
 
 def torque_body(in_ref, film_ref, beside_y_ref, beside_x_ref, expand_ref, out_ref):
     row, col = lax.axis_index("row"), lax.axis_index("col")
-    sums = tall_product(expand_ref[...], load_chunks(in_ref, sums_rows))
+    high, low = split(load_chunks(in_ref, sums_rows).T)
+    both = jnp.dot(high, expand_ref[...], preferred_element_type=f32)
+    rest = jnp.dot(low, expand_ref[:, :256], preferred_element_type=f32)
+    sums = both[:, :256] + both[:, 256:] + rest
     demag = []
     for a in range(3):
-        block = sums[:, 128 * a : 128 * a + 128]
-        demag.append(block[:128] + half_turn(block[128:]))
-    low = lane_index((128, 128)) < 64
-    former = jnp.where(low, demag[0], half_turn(demag[1])).T
-    demag = [former[:64], former[64:], demag[2].T[:64]]
+        block = sums[128 * a : 128 * a + 128]
+        demag.append(block[:64, :128] + block[64:, 128:])
 
     device = lax.broadcasted_iota(jnp.int32, (rows_n, 128), 0)
 

time: 98.6 us -> 98.4 us (level)
  no operation moved by 1% of the time
where the time goes in v10:
time: 98.4 us; the launch traced here: 98.1 us
  blocking collectives  93 us (95%)
  Pallas kernels  3.97 us (4%)
    all_to_all x4, blocking collectives, exchange(): lax.all_to_all(array, axis, split_axis=0, concat_axis=0, tiled=True)  93 us
    pallas_call x5, Pallas kernels, call(): pl.pallas_call(body, out_shape=shapes, in_specs=[in_spec] * len(args), ou...  3.97 us

profile of v10, /device:TPU:2, one launch (start us, length us, event | category | flops | bytes accessed | tf_op | source)
XLA Modules:
  0.0 98.1 jit_solution(16991598045058741677)
XLA Ops:
  0.0 0.0 copy-start.9
  0.0 0.9 pad_maximum_fusion.film_ref
  0.9 0.0 copy-done.9
  0.9 0.4 shard_map.118
  1.4 0.0 copy-start.2
  1.4 37.3 %all_to_all.20 = f32[16,11,4,128]{3,2,1,0:T(4,128)S(1)} all-to-all(f32[16,11,4,128]{3,2,1,0:T(4,128)S(1)} %bitcast.24), channel_id=1, replica_groups=mesh['row'=16,'col'=32] {'row'}, dimensions={0} | all-to-all | bytes 720896 | tf_op jit(solution)/shard_map/all_to_all | solution.py:406
  38.7 0.0 copy-done.2
  38.7 0.0 copy-start.4
  38.7 0.0 copy-start.7
  38.7 0.0 copy-start.8
  38.7 0.5 shard_map.119
  39.2 0.0 copy-start.1
  39.2 0.0 copy-start.5
  39.2 0.0 copy-start.6
  39.2 15.3 %all_to_all.21 = f32[32,2,8,128]{3,2,1,0:T(8,128)S(1)} all-to-all(f32[32,2,8,128]{3,2,1,0:T(8,128)S(1)} %bitcast.20), channel_id=1, replica_groups=mesh['row'=16,'col'=32] {'col'}, dimensions={0} | all-to-all | bytes 524288 | tf_op jit(solution)/shard_map/all_to_all | solution.py:406
  54.5 0.0 copy-done.4
  54.5 0.0 copy-done.7
  54.5 0.0 copy-done.8
  54.5 0.0 copy-done.1
  54.5 0.0 copy-done.5
  54.5 0.0 copy-done.6
  54.5 0.0 copy-start
  54.5 1.5 %shard_map.120 = f32[384,128]{1,0:T(8,128)S(1)} custom-call(f32[512,128]{1,0:T(8,128)S(1)} %bitcast.16, f32[768,128]{1,0:T(8,128)S(1)} %bitcast.23, bf16[128,128]{1,0:T(8,128)(2,1)S(1)} %copy-done.8, f32[6,64,128]{2,1,0:T(8,128)S(1)} %copy-done.4, bf16[128,256]{1,0:T(8,128)(2,1)S(1)} %copy-done.6, bf16[128,256]{1,0:T(8,128)(2,1)S(1)} %copy-done.5, ...), custom_call_target="tpu_custom_call" | custom-call | flops 100000000 | bytes 1000000 | tf_op jit(solution)/shard_map/pallas_call | solution.py:390
  56.0 11.9 %all_to_all.22 = f32[32,3,4,128]{3,2,1,0:T(4,128)S(1)} all-to-all(f32[32,3,4,128]{3,2,1,0:T(4,128)S(1)} %bitcast.21), channel_id=1, replica_groups=mesh['row'=16,'col'=32] {'col'}, dimensions={0} | all-to-all | bytes 393216 | tf_op jit(solution)/shard_map/all_to_all | solution.py:406
  67.9 0.0 copy-done
  67.9 0.5 shard_map.121
  68.4 0.0 copy-start.3
  68.4 28.6 %all_to_all.23 = f32[16,21,2,128]{3,2,1,0:T(2,128)S(1)} all-to-all(f32[16,21,2,128]{3,2,1,0:T(2,128)S(1)} %bitcast.19), channel_id=1, replica_groups=mesh['row'=16,'col'=32] {'row'}, dimensions={0} | all-to-all | bytes 688128 | tf_op jit(solution)/shard_map/all_to_all | solution.py:406
  97.0 0.0 copy-done.3
  97.0 1.1 %shard_map.122 = f32[3,64,128]{2,1,0:T(8,128)} custom-call(f32[672,128]{1,0:T(8,128)S(1)} %bitcast.18, f32[4,64,128]{2,1,0:T(8,128)S(1)} %pad_maximum_fusion.film_ref, f32[704,128]{1,0:T(8,128)S(1)} %bitcast.15, f32[512,128]{1,0:T(8,128)S(1)} %bitcast.17, bf16[224,512]{1,0:T(8,128)(2,1)S(1)} %copy-done.3), custom_call_target="tpu_custom_call" | custom-call | flops 100000000 | bytes 1000000 | tf_op jit(solution)/shard_map/pallas_call | solution.py:390
Async XLA Ops:
  0.0 0.9 copy-start.9
  1.4 37.3 %copy-start.2 = (bf16[512,224]{1,0:T(8,128)(2,1)S(1)}, bf16[512,224]{1,0:T(8,128)(2,1)}, u32[]{:S(2)}) copy-start(bf16[512,224]{1,0:T(8,128)(2,1)} %constant.19.clone.expand_ref) | copy-start | bytes 688132
  38.7 15.8 %copy-start.4 = (f32[6,64,128]{2,1,0:T(8,128)S(1)}, f32[6,64,128]{2,1,0:T(8,128)}, u32[]{:S(2)}) copy-start(f32[6,64,128]{2,1,0:T(8,128)} %constant.21.clone.twist_ref) | copy-start | bytes 589828
  38.7 15.8 %copy-start.7 = (bf16[64,256]{1,0:T(8,128)(2,1)S(1)}, bf16[64,256]{1,0:T(8,128)(2,1)}, u32[]{:S(2)}) copy-start(bf16[64,256]{1,0:T(8,128)(2,1)} %constant.24.clone.back_ref) | copy-start | bytes 98308
  38.7 15.8 %copy-start.8 = (bf16[128,128]{1,0:T(8,128)(2,1)S(1)}, bf16[128,128]{1,0:T(8,128)(2,1)}, u32[]{:S(2)}) copy-start(bf16[128,128]{1,0:T(8,128)(2,1)} %constant.20.clone.first_ref) | copy-start | bytes 98308
  39.2 15.3 %copy-start.1 = (f32[6,4,4096]{2,1,0:T(4,128)S(1)}, f32[6,4,4096]{2,1,0:T(4,128)}, u32[]{:S(2)}) copy-start(f32[6,4,4096]{2,1,0:T(4,128)} %param.14) | copy-start | bytes 1179652
  39.2 15.3 %copy-start.5 = (bf16[128,256]{1,0:T(8,128)(2,1)S(1)}, bf16[128,256]{1,0:T(8,128)(2,1)}, u32[]{:S(2)}) copy-start(bf16[128,256]{1,0:T(8,128)(2,1)} %constant.23.clone.lead_ref) | copy-start | bytes 196612
  39.2 15.3 %copy-start.6 = (bf16[128,256]{1,0:T(8,128)(2,1)S(1)}, bf16[128,256]{1,0:T(8,128)(2,1)}, u32[]{:S(2)}) copy-start(bf16[128,256]{1,0:T(8,128)(2,1)} %constant.22.clone.last_ref) | copy-start | bytes 196612
  54.5 13.4 %copy-start = (bf16[896,256]{1,0:T(8,128)(2,1)S(1)}, bf16[896,256]{1,0:T(8,128)(2,1)}, u32[]{:S(2)}) copy-start(bf16[896,256]{1,0:T(8,128)(2,1)} %constant.25.clone.gather_ref) | copy-start | bytes 1376260
  68.4 28.6 %copy-start.3 = (bf16[224,512]{1,0:T(8,128)(2,1)S(1)}, bf16[224,512]{1,0:T(8,128)(2,1)}, u32[]{:S(2)}) copy-start(bf16[224,512]{1,0:T(8,128)(2,1)} %constant.26.clone.expand_ref) | copy-start | bytes 688132

commit v11 on v10

--- a/solution.py
+++ b/solution.py
@@ -98,7 +98,8 @@
     sides, turns, gather, expand = row_transform()
     y_gather = np.concatenate([parts(turns), sides], 0).astype(np.float32)
     y_expand = tall(parts(expand[kappa]))
-    z_gather = deep(parts(gather[:, kappa]))
+    gather = gather[:, kappa]
+    z_gather = deep(np.concatenate([gather.real, gather.imag], 1))
     z_expand = np.ascontiguousarray(tall(parts(expand)).T)
 
     cos, sin = wave(k1x, col, 64)
@@ -252,7 +253,7 @@
             block = block * own + half_turn(block) * other
             turned.append(block)
             turned.append(half_turn(block) * sign)
-        return deep_product(last_ref[...], jnp.concatenate(turned, 0), 1)
+        return jnp.concatenate(turned, 0)
 
     def multiply(freq, ks):
         sources = []
@@ -264,7 +265,7 @@
                     term = kern[tensor_slots[target][b]][k] * freq[:, 128 * j : 128 * j + 128]
                     total = term if total is None else total + term
                 sources.append(jnp.concatenate([total, -half_turn(total) * sign], 0))
-        return deep_product(lead_ref[...], jnp.concatenate(sources, 1), 0)
+        return jnp.concatenate(sources, 1)
 
     def leave(section):
         turned = []
@@ -273,7 +274,7 @@
             aside = half_turn(block)
             turned.append(block * twist_ref[2] + aside * twist_ref[4])
             turned.append(block * twist_ref[3] + aside * twist_ref[5])
-        return deep_product(back_ref[...], jnp.concatenate(turned, 0), 1)
+        return jnp.concatenate(turned, 0)
 
     def store(result, ks):
         for a in range(3):
@@ -288,8 +289,11 @@
     groups = ((0,), (1,), (2,), (3,))
     states = [enter(ks) for ks in groups]
     states = [spread(state) for state in states]
+    states = [deep_product(last_ref[...], state, 1) for state in states]
     states = [multiply(state, ks) for state, ks in zip(states, groups)]
+    states = [deep_product(lead_ref[...], state, 0) for state in states]
     states = [leave(state) for state in states]
+    states = [deep_product(back_ref[...], state, 1) for state in states]
     for state, ks in zip(states, groups):
         store(state, ks)
 
@@ -299,13 +303,10 @@
     for a in range(3):
         block = [in_ref[pl.ds(4 * a + k, cols_n, stride=12), :] for k in range(4)]
         columns.append(jnp.concatenate(block, 0))
+    sign = half_sign(128)
+    columns = [jnp.concatenate([block, half_turn(block) * sign], 0) for block in columns]
     sums = deep_product(gather_ref[...], jnp.concatenate(columns, 1), 0)
-    size = rows_n * modes
-    sign = half_sign(size)
-    blocks = []
-    for a in range(3):
-        block = sums[:, 128 * a : 128 * a + 128]
-        blocks.append(block[:size] + half_turn(block[size:]) * sign)
+    blocks = [sums[:, 128 * a : 128 * a + 128] for a in range(3)]
     store_chunks(out_ref, sums_rows, blocks)
 
 

time: 98.4 us -> 98.4 us (level)
  no operation moved by 1% of the time
where the time goes in v11:
time: 98.4 us; the launch traced here: 98.1 us
  blocking collectives  93 us (95%)
  Pallas kernels  3.93 us (4%)
    all_to_all x4, blocking collectives, exchange(): lax.all_to_all(array, axis, split_axis=0, concat_axis=0, tiled=True)  93 us
    pallas_call x5, Pallas kernels, call(): pl.pallas_call(body, out_shape=shapes, in_specs=[in_spec] * len(args), ou...  3.93 us

profile of v11, /device:TPU:2, one launch (start us, length us, event | category | flops | bytes accessed | tf_op | source)
XLA Modules:
  0.0 98.1 jit_solution(9698593440686392298)
XLA Ops:
  0.0 0.0 copy-start.9
  0.0 0.9 pad_maximum_fusion.film_ref
  0.9 0.0 copy-done.9
  0.9 0.4 shard_map.118
  1.4 0.0 copy-start.2
  1.4 37.3 %all_to_all.20 = f32[16,11,4,128]{3,2,1,0:T(4,128)S(1)} all-to-all(f32[16,11,4,128]{3,2,1,0:T(4,128)S(1)} %bitcast.24), channel_id=1, replica_groups=mesh['row'=16,'col'=32] {'row'}, dimensions={0} | all-to-all | bytes 720896 | tf_op jit(solution)/shard_map/all_to_all | solution.py:407
  38.7 0.0 copy-done.2
  38.7 0.0 copy-start.4
  38.7 0.0 copy-start.7
  38.7 0.0 copy-start.8
  38.7 0.5 shard_map.119
  39.2 0.0 copy-start.1
  39.2 0.0 copy-start.5
  39.2 0.0 copy-start.6
  39.2 15.3 %all_to_all.21 = f32[32,2,8,128]{3,2,1,0:T(8,128)S(1)} all-to-all(f32[32,2,8,128]{3,2,1,0:T(8,128)S(1)} %bitcast.20), channel_id=1, replica_groups=mesh['row'=16,'col'=32] {'col'}, dimensions={0} | all-to-all | bytes 524288 | tf_op jit(solution)/shard_map/all_to_all | solution.py:407
  54.5 0.0 copy-done.4
  54.5 0.0 copy-done.7
  54.5 0.0 copy-done.8
  54.5 0.0 copy-done.1
  54.5 0.0 copy-done.5
  54.5 0.0 copy-done.6
  54.5 0.0 copy-start
  54.5 1.5 %shard_map.120 = f32[384,128]{1,0:T(8,128)S(1)} custom-call(f32[512,128]{1,0:T(8,128)S(1)} %bitcast.16, f32[768,128]{1,0:T(8,128)S(1)} %bitcast.23, bf16[128,128]{1,0:T(8,128)(2,1)S(1)} %copy-done.8, f32[6,64,128]{2,1,0:T(8,128)S(1)} %copy-done.4, bf16[128,256]{1,0:T(8,128)(2,1)S(1)} %copy-done.6, bf16[128,256]{1,0:T(8,128)(2,1)S(1)} %copy-done.5, ...), custom_call_target="tpu_custom_call" | custom-call | flops 100000000 | bytes 1000000 | tf_op jit(solution)/shard_map/pallas_call | solution.py:391
  56.0 11.9 %all_to_all.22 = f32[32,3,4,128]{3,2,1,0:T(4,128)S(1)} all-to-all(f32[32,3,4,128]{3,2,1,0:T(4,128)S(1)} %bitcast.21), channel_id=1, replica_groups=mesh['row'=16,'col'=32] {'col'}, dimensions={0} | all-to-all | bytes 393216 | tf_op jit(solution)/shard_map/all_to_all | solution.py:407
  67.9 0.0 copy-done
  67.9 0.5 shard_map.121
  68.4 0.0 copy-start.3
  68.4 28.6 %all_to_all.23 = f32[16,21,2,128]{3,2,1,0:T(2,128)S(1)} all-to-all(f32[16,21,2,128]{3,2,1,0:T(2,128)S(1)} %bitcast.19), channel_id=1, replica_groups=mesh['row'=16,'col'=32] {'row'}, dimensions={0} | all-to-all | bytes 688128 | tf_op jit(solution)/shard_map/all_to_all | solution.py:407
  97.0 0.0 copy-done.3
  97.0 1.1 %shard_map.122 = f32[3,64,128]{2,1,0:T(8,128)} custom-call(f32[672,128]{1,0:T(8,128)S(1)} %bitcast.18, f32[4,64,128]{2,1,0:T(8,128)S(1)} %pad_maximum_fusion.film_ref, f32[704,128]{1,0:T(8,128)S(1)} %bitcast.15, f32[512,128]{1,0:T(8,128)S(1)} %bitcast.17, bf16[224,512]{1,0:T(8,128)(2,1)S(1)} %copy-done.3), custom_call_target="tpu_custom_call" | custom-call | flops 100000000 | bytes 1000000 | tf_op jit(solution)/shard_map/pallas_call | solution.py:391
Async XLA Ops:
  0.0 0.9 copy-start.9
  1.4 37.3 %copy-start.2 = (bf16[512,224]{1,0:T(8,128)(2,1)S(1)}, bf16[512,224]{1,0:T(8,128)(2,1)}, u32[]{:S(2)}) copy-start(bf16[512,224]{1,0:T(8,128)(2,1)} %constant.19.clone.expand_ref) | copy-start | bytes 688132
  38.7 15.8 %copy-start.4 = (f32[6,64,128]{2,1,0:T(8,128)S(1)}, f32[6,64,128]{2,1,0:T(8,128)}, u32[]{:S(2)}) copy-start(f32[6,64,128]{2,1,0:T(8,128)} %constant.21.clone.twist_ref) | copy-start | bytes 589828
  38.7 15.8 %copy-start.7 = (bf16[64,256]{1,0:T(8,128)(2,1)S(1)}, bf16[64,256]{1,0:T(8,128)(2,1)}, u32[]{:S(2)}) copy-start(bf16[64,256]{1,0:T(8,128)(2,1)} %constant.24.clone.back_ref) | copy-start | bytes 98308
  38.7 15.8 %copy-start.8 = (bf16[128,128]{1,0:T(8,128)(2,1)S(1)}, bf16[128,128]{1,0:T(8,128)(2,1)}, u32[]{:S(2)}) copy-start(bf16[128,128]{1,0:T(8,128)(2,1)} %constant.20.clone.first_ref) | copy-start | bytes 98308
  39.2 15.3 %copy-start.1 = (f32[6,4,4096]{2,1,0:T(4,128)S(1)}, f32[6,4,4096]{2,1,0:T(4,128)}, u32[]{:S(2)}) copy-start(f32[6,4,4096]{2,1,0:T(4,128)} %param.14) | copy-start | bytes 1179652
  39.2 15.3 %copy-start.5 = (bf16[128,256]{1,0:T(8,128)(2,1)S(1)}, bf16[128,256]{1,0:T(8,128)(2,1)}, u32[]{:S(2)}) copy-start(bf16[128,256]{1,0:T(8,128)(2,1)} %constant.23.clone.lead_ref) | copy-start | bytes 196612
  39.2 15.3 %copy-start.6 = (bf16[128,256]{1,0:T(8,128)(2,1)S(1)}, bf16[128,256]{1,0:T(8,128)(2,1)}, u32[]{:S(2)}) copy-start(bf16[128,256]{1,0:T(8,128)(2,1)} %constant.22.clone.last_ref) | copy-start | bytes 196612
  54.5 13.4 %copy-start = (bf16[448,512]{1,0:T(8,128)(2,1)S(1)}, bf16[448,512]{1,0:T(8,128)(2,1)}, u32[]{:S(2)}) copy-start(bf16[448,512]{1,0:T(8,128)(2,1)} %constant.25.clone.gather_ref) | copy-start | bytes 1376260
  68.4 28.6 %copy-start.3 = (bf16[224,512]{1,0:T(8,128)(2,1)S(1)}, bf16[224,512]{1,0:T(8,128)(2,1)}, u32[]{:S(2)}) copy-start(bf16[224,512]{1,0:T(8,128)(2,1)} %constant.26.clone.expand_ref) | copy-start | bytes 688132

commit v12 on v10

--- a/solution.py
+++ b/solution.py
@@ -135,9 +135,10 @@
 def tall_product(table, values):
     high, low = split(values)
     size = table.shape[0] // 2
-    both = jnp.dot(table, high, preferred_element_type=f32)
-    rest = jnp.dot(table[:size], low, preferred_element_type=f32)
-    return both[:size] + both[size:] + rest
+    width = values.shape[1]
+    both = jnp.dot(table, jnp.concatenate([high, low], 1), preferred_element_type=f32)
+    rest = both[size:, :width] + both[:size, width:] + both[size:, width:]
+    return both[:size, :width] + rest
 
 
 def deep_product(table, values, contract):

time: 98.4 us -> 98.4 us (level)
  no operation moved by 1% of the time
where the time goes in v12:
time: 98.4 us; the launch traced here: 98.1 us
  blocking collectives  93 us (95%)
  Pallas kernels  3.96 us (4%)
    all_to_all x4, blocking collectives, exchange(): lax.all_to_all(array, axis, split_axis=0, concat_axis=0, tiled=True)  93 us
    pallas_call x5, Pallas kernels, call(): pl.pallas_call(body, out_shape=shapes, in_specs=[in_spec] * len(args), ou...  3.96 us

profile of v12, /device:TPU:2, one launch (start us, length us, event | category | flops | bytes accessed | tf_op | source)
XLA Modules:
  0.0 98.1 jit_solution(4051269520305075739)
XLA Ops:
  0.0 0.0 copy-start.9
  0.0 0.9 pad_maximum_fusion.film_ref
  0.9 0.0 copy-done.9
  0.9 0.4 shard_map.118
  1.4 0.0 copy-start.2
  1.4 37.3 %all_to_all.20 = f32[16,11,4,128]{3,2,1,0:T(4,128)S(1)} all-to-all(f32[16,11,4,128]{3,2,1,0:T(4,128)S(1)} %bitcast.24), channel_id=1, replica_groups=mesh['row'=16,'col'=32] {'row'}, dimensions={0} | all-to-all | bytes 720896 | tf_op jit(solution)/shard_map/all_to_all | solution.py:407
  38.7 0.0 copy-done.2
  38.7 0.0 copy-start.4
  38.7 0.0 copy-start.7
  38.7 0.0 copy-start.8
  38.7 0.5 shard_map.119
  39.2 0.0 copy-start.1
  39.2 0.0 copy-start.5
  39.2 0.0 copy-start.6
  39.2 15.3 %all_to_all.21 = f32[32,2,8,128]{3,2,1,0:T(8,128)S(1)} all-to-all(f32[32,2,8,128]{3,2,1,0:T(8,128)S(1)} %bitcast.20), channel_id=1, replica_groups=mesh['row'=16,'col'=32] {'col'}, dimensions={0} | all-to-all | bytes 524288 | tf_op jit(solution)/shard_map/all_to_all | solution.py:407
  54.5 0.0 copy-done.4
  54.5 0.0 copy-done.7
  54.5 0.0 copy-done.8
  54.5 0.0 copy-done.1
  54.5 0.0 copy-done.5
  54.5 0.0 copy-done.6
  54.5 0.0 copy-start
  54.5 1.5 %shard_map.120 = f32[384,128]{1,0:T(8,128)S(1)} custom-call(f32[512,128]{1,0:T(8,128)S(1)} %bitcast.16, f32[768,128]{1,0:T(8,128)S(1)} %bitcast.23, bf16[128,128]{1,0:T(8,128)(2,1)S(1)} %copy-done.8, f32[6,64,128]{2,1,0:T(8,128)S(1)} %copy-done.4, bf16[128,256]{1,0:T(8,128)(2,1)S(1)} %copy-done.6, bf16[128,256]{1,0:T(8,128)(2,1)S(1)} %copy-done.5, ...), custom_call_target="tpu_custom_call" | custom-call | flops 100000000 | bytes 1000000 | tf_op jit(solution)/shard_map/pallas_call | solution.py:391
  56.0 11.9 %all_to_all.22 = f32[32,3,4,128]{3,2,1,0:T(4,128)S(1)} all-to-all(f32[32,3,4,128]{3,2,1,0:T(4,128)S(1)} %bitcast.21), channel_id=1, replica_groups=mesh['row'=16,'col'=32] {'col'}, dimensions={0} | all-to-all | bytes 393216 | tf_op jit(solution)/shard_map/all_to_all | solution.py:407
  67.9 0.0 copy-done
  67.9 0.5 shard_map.121
  68.4 0.0 copy-start.3
  68.4 28.6 %all_to_all.23 = f32[16,21,2,128]{3,2,1,0:T(2,128)S(1)} all-to-all(f32[16,21,2,128]{3,2,1,0:T(2,128)S(1)} %bitcast.19), channel_id=1, replica_groups=mesh['row'=16,'col'=32] {'row'}, dimensions={0} | all-to-all | bytes 688128 | tf_op jit(solution)/shard_map/all_to_all | solution.py:407
  97.0 0.0 copy-done.3
  97.0 1.1 %shard_map.122 = f32[3,64,128]{2,1,0:T(8,128)} custom-call(f32[672,128]{1,0:T(8,128)S(1)} %bitcast.18, f32[4,64,128]{2,1,0:T(8,128)S(1)} %pad_maximum_fusion.film_ref, f32[704,128]{1,0:T(8,128)S(1)} %bitcast.15, f32[512,128]{1,0:T(8,128)S(1)} %bitcast.17, bf16[224,512]{1,0:T(8,128)(2,1)S(1)} %copy-done.3), custom_call_target="tpu_custom_call" | custom-call | flops 100000000 | bytes 1000000 | tf_op jit(solution)/shard_map/pallas_call | solution.py:391
Async XLA Ops:
  0.0 0.9 copy-start.9
  1.4 37.3 %copy-start.2 = (bf16[512,224]{1,0:T(8,128)(2,1)S(1)}, bf16[512,224]{1,0:T(8,128)(2,1)}, u32[]{:S(2)}) copy-start(bf16[512,224]{1,0:T(8,128)(2,1)} %constant.19.clone.expand_ref) | copy-start | bytes 688132
  38.7 15.8 %copy-start.4 = (f32[6,64,128]{2,1,0:T(8,128)S(1)}, f32[6,64,128]{2,1,0:T(8,128)}, u32[]{:S(2)}) copy-start(f32[6,64,128]{2,1,0:T(8,128)} %constant.21.clone.twist_ref) | copy-start | bytes 589828
  38.7 15.8 %copy-start.7 = (bf16[64,256]{1,0:T(8,128)(2,1)S(1)}, bf16[64,256]{1,0:T(8,128)(2,1)}, u32[]{:S(2)}) copy-start(bf16[64,256]{1,0:T(8,128)(2,1)} %constant.24.clone.back_ref) | copy-start | bytes 98308
  38.7 15.8 %copy-start.8 = (bf16[128,128]{1,0:T(8,128)(2,1)S(1)}, bf16[128,128]{1,0:T(8,128)(2,1)}, u32[]{:S(2)}) copy-start(bf16[128,128]{1,0:T(8,128)(2,1)} %constant.20.clone.first_ref) | copy-start | bytes 98308
  39.2 15.3 %copy-start.1 = (f32[6,4,4096]{2,1,0:T(4,128)S(1)}, f32[6,4,4096]{2,1,0:T(4,128)}, u32[]{:S(2)}) copy-start(f32[6,4,4096]{2,1,0:T(4,128)} %param.14) | copy-start | bytes 1179652
  39.2 15.3 %copy-start.5 = (bf16[128,256]{1,0:T(8,128)(2,1)S(1)}, bf16[128,256]{1,0:T(8,128)(2,1)}, u32[]{:S(2)}) copy-start(bf16[128,256]{1,0:T(8,128)(2,1)} %constant.23.clone.lead_ref) | copy-start | bytes 196612
  39.2 15.3 %copy-start.6 = (bf16[128,256]{1,0:T(8,128)(2,1)S(1)}, bf16[128,256]{1,0:T(8,128)(2,1)}, u32[]{:S(2)}) copy-start(bf16[128,256]{1,0:T(8,128)(2,1)} %constant.22.clone.last_ref) | copy-start | bytes 196612
  54.5 13.4 %copy-start = (bf16[896,256]{1,0:T(8,128)(2,1)S(1)}, bf16[896,256]{1,0:T(8,128)(2,1)}, u32[]{:S(2)}) copy-start(bf16[896,256]{1,0:T(8,128)(2,1)} %constant.25.clone.gather_ref) | copy-start | bytes 1376260
  68.4 28.6 %copy-start.3 = (bf16[224,512]{1,0:T(8,128)(2,1)S(1)}, bf16[224,512]{1,0:T(8,128)(2,1)}, u32[]{:S(2)}) copy-start(bf16[224,512]{1,0:T(8,128)(2,1)} %constant.26.clone.expand_ref) | copy-start | bytes 688132

commit v13 on v12

--- a/solution.py
+++ b/solution.py
@@ -253,7 +253,7 @@
             block = block * own + half_turn(block) * other
             turned.append(block)
             turned.append(half_turn(block) * sign)
-        return deep_product(last_ref[...], jnp.concatenate(turned, 0), 1)
+        return jnp.concatenate(turned, 0)
 
     def multiply(freq, ks):
         sources = []
@@ -265,7 +265,7 @@
                     term = kern[tensor_slots[target][b]][k] * freq[:, 128 * j : 128 * j + 128]
                     total = term if total is None else total + term
                 sources.append(jnp.concatenate([total, -half_turn(total) * sign], 0))
-        return deep_product(lead_ref[...], jnp.concatenate(sources, 1), 0)
+        return jnp.concatenate(sources, 1)
 
     def leave(section):
         turned = []
@@ -274,7 +274,7 @@
             aside = half_turn(block)
             turned.append(block * twist_ref[2] + aside * twist_ref[4])
             turned.append(block * twist_ref[3] + aside * twist_ref[5])
-        return deep_product(back_ref[...], jnp.concatenate(turned, 0), 1)
+        return jnp.concatenate(turned, 0)
 
     def store(result, ks):
         for a in range(3):
@@ -289,8 +289,11 @@
     groups = ((0,), (1,), (2,), (3,))
     states = [enter(ks) for ks in groups]
     states = [spread(state) for state in states]
+    states = [deep_product(last_ref[...], state, 1) for state in states]
     states = [multiply(state, ks) for state, ks in zip(states, groups)]
+    states = [deep_product(lead_ref[...], state, 0) for state in states]
     states = [leave(state) for state in states]
+    states = [deep_product(back_ref[...], state, 1) for state in states]
     for state, ks in zip(states, groups):
         store(state, ks)
 

time: 98.4 us -> 98.4 us (level)
  no operation moved by 1% of the time
where the time goes in v13:
time: 98.4 us; the launch traced here: 98.1 us
  blocking collectives  93 us (95%)
  Pallas kernels  3.95 us (4%)
    all_to_all x4, blocking collectives, exchange(): lax.all_to_all(array, axis, split_axis=0, concat_axis=0, tiled=True)  93 us
    pallas_call x5, Pallas kernels, call(): pl.pallas_call(body, out_shape=shapes, in_specs=[in_spec] * len(args), ou...  3.95 us

profile of v13, /device:TPU:2, one launch (start us, length us, event | category | flops | bytes accessed | tf_op | source)
XLA Modules:
  0.0 98.1 jit_solution(2949792116078282418)
XLA Ops:
  0.0 0.0 copy-start.9
  0.0 0.9 pad_maximum_fusion.film_ref
  0.9 0.0 copy-done.9
  0.9 0.4 shard_map.118
  1.4 0.0 copy-start.2
  1.4 37.3 %all_to_all.20 = f32[16,11,4,128]{3,2,1,0:T(4,128)S(1)} all-to-all(f32[16,11,4,128]{3,2,1,0:T(4,128)S(1)} %bitcast.24), channel_id=1, replica_groups=mesh['row'=16,'col'=32] {'row'}, dimensions={0} | all-to-all | bytes 720896 | tf_op jit(solution)/shard_map/all_to_all | solution.py:410
  38.7 0.0 copy-done.2
  38.7 0.0 copy-start.4
  38.7 0.0 copy-start.7
  38.7 0.0 copy-start.8
  38.7 0.5 shard_map.119
  39.2 0.0 copy-start.1
  39.2 0.0 copy-start.5
  39.2 0.0 copy-start.6
  39.2 15.3 %all_to_all.21 = f32[32,2,8,128]{3,2,1,0:T(8,128)S(1)} all-to-all(f32[32,2,8,128]{3,2,1,0:T(8,128)S(1)} %bitcast.20), channel_id=1, replica_groups=mesh['row'=16,'col'=32] {'col'}, dimensions={0} | all-to-all | bytes 524288 | tf_op jit(solution)/shard_map/all_to_all | solution.py:410
  54.5 0.0 copy-done.4
  54.5 0.0 copy-done.7
  54.5 0.0 copy-done.8
  54.5 0.0 copy-done.1
  54.5 0.0 copy-done.5
  54.5 0.0 copy-done.6
  54.5 0.0 copy-start
  54.5 1.5 %shard_map.120 = f32[384,128]{1,0:T(8,128)S(1)} custom-call(f32[512,128]{1,0:T(8,128)S(1)} %bitcast.16, f32[768,128]{1,0:T(8,128)S(1)} %bitcast.23, bf16[128,128]{1,0:T(8,128)(2,1)S(1)} %copy-done.8, f32[6,64,128]{2,1,0:T(8,128)S(1)} %copy-done.4, bf16[128,256]{1,0:T(8,128)(2,1)S(1)} %copy-done.6, bf16[128,256]{1,0:T(8,128)(2,1)S(1)} %copy-done.5, ...), custom_call_target="tpu_custom_call" | custom-call | flops 100000000 | bytes 1000000 | tf_op jit(solution)/shard_map/pallas_call | solution.py:394
  56.0 11.9 %all_to_all.22 = f32[32,3,4,128]{3,2,1,0:T(4,128)S(1)} all-to-all(f32[32,3,4,128]{3,2,1,0:T(4,128)S(1)} %bitcast.21), channel_id=1, replica_groups=mesh['row'=16,'col'=32] {'col'}, dimensions={0} | all-to-all | bytes 393216 | tf_op jit(solution)/shard_map/all_to_all | solution.py:410
  67.9 0.0 copy-done
  67.9 0.5 shard_map.121
  68.4 0.0 copy-start.3
  68.4 28.6 %all_to_all.23 = f32[16,21,2,128]{3,2,1,0:T(2,128)S(1)} all-to-all(f32[16,21,2,128]{3,2,1,0:T(2,128)S(1)} %bitcast.19), channel_id=1, replica_groups=mesh['row'=16,'col'=32] {'row'}, dimensions={0} | all-to-all | bytes 688128 | tf_op jit(solution)/shard_map/all_to_all | solution.py:410
  97.0 0.0 copy-done.3
  97.0 1.1 %shard_map.122 = f32[3,64,128]{2,1,0:T(8,128)} custom-call(f32[672,128]{1,0:T(8,128)S(1)} %bitcast.18, f32[4,64,128]{2,1,0:T(8,128)S(1)} %pad_maximum_fusion.film_ref, f32[704,128]{1,0:T(8,128)S(1)} %bitcast.15, f32[512,128]{1,0:T(8,128)S(1)} %bitcast.17, bf16[224,512]{1,0:T(8,128)(2,1)S(1)} %copy-done.3), custom_call_target="tpu_custom_call" | custom-call | flops 100000000 | bytes 1000000 | tf_op jit(solution)/shard_map/pallas_call | solution.py:394
Async XLA Ops:
  0.0 0.9 copy-start.9
  1.4 37.3 %copy-start.2 = (bf16[512,224]{1,0:T(8,128)(2,1)S(1)}, bf16[512,224]{1,0:T(8,128)(2,1)}, u32[]{:S(2)}) copy-start(bf16[512,224]{1,0:T(8,128)(2,1)} %constant.19.clone.expand_ref) | copy-start | bytes 688132
  38.7 15.8 %copy-start.4 = (f32[6,64,128]{2,1,0:T(8,128)S(1)}, f32[6,64,128]{2,1,0:T(8,128)}, u32[]{:S(2)}) copy-start(f32[6,64,128]{2,1,0:T(8,128)} %constant.21.clone.twist_ref) | copy-start | bytes 589828
  38.7 15.8 %copy-start.7 = (bf16[64,256]{1,0:T(8,128)(2,1)S(1)}, bf16[64,256]{1,0:T(8,128)(2,1)}, u32[]{:S(2)}) copy-start(bf16[64,256]{1,0:T(8,128)(2,1)} %constant.24.clone.back_ref) | copy-start | bytes 98308
  38.7 15.8 %copy-start.8 = (bf16[128,128]{1,0:T(8,128)(2,1)S(1)}, bf16[128,128]{1,0:T(8,128)(2,1)}, u32[]{:S(2)}) copy-start(bf16[128,128]{1,0:T(8,128)(2,1)} %constant.20.clone.first_ref) | copy-start | bytes 98308
  39.2 15.3 %copy-start.1 = (f32[6,4,4096]{2,1,0:T(4,128)S(1)}, f32[6,4,4096]{2,1,0:T(4,128)}, u32[]{:S(2)}) copy-start(f32[6,4,4096]{2,1,0:T(4,128)} %param.14) | copy-start | bytes 1179652
  39.2 15.3 %copy-start.5 = (bf16[128,256]{1,0:T(8,128)(2,1)S(1)}, bf16[128,256]{1,0:T(8,128)(2,1)}, u32[]{:S(2)}) copy-start(bf16[128,256]{1,0:T(8,128)(2,1)} %constant.23.clone.lead_ref) | copy-start | bytes 196612
  39.2 15.3 %copy-start.6 = (bf16[128,256]{1,0:T(8,128)(2,1)S(1)}, bf16[128,256]{1,0:T(8,128)(2,1)}, u32[]{:S(2)}) copy-start(bf16[128,256]{1,0:T(8,128)(2,1)} %constant.22.clone.last_ref) | copy-start | bytes 196612
  54.5 13.4 %copy-start = (bf16[896,256]{1,0:T(8,128)(2,1)S(1)}, bf16[896,256]{1,0:T(8,128)(2,1)}, u32[]{:S(2)}) copy-start(bf16[896,256]{1,0:T(8,128)(2,1)} %constant.25.clone.gather_ref) | copy-start | bytes 1376260
  68.4 28.6 %copy-start.3 = (bf16[224,512]{1,0:T(8,128)(2,1)S(1)}, bf16[224,512]{1,0:T(8,128)(2,1)}, u32[]{:S(2)}) copy-start(bf16[224,512]{1,0:T(8,128)(2,1)} %constant.26.clone.expand_ref) | copy-start | bytes 688132

commit v14 on v11

--- a/solution.py
+++ b/solution.py
@@ -136,9 +136,10 @@
 def tall_product(table, values):
     high, low = split(values)
     size = table.shape[0] // 2
-    both = jnp.dot(table, high, preferred_element_type=f32)
-    rest = jnp.dot(table[:size], low, preferred_element_type=f32)
-    return both[:size] + both[size:] + rest
+    width = values.shape[1]
+    both = jnp.dot(table, jnp.concatenate([high, low], 1), preferred_element_type=f32)
+    rest = both[size:, :width] + both[:size, width:] + both[size:, width:]
+    return both[:size, :width] + rest
 
 
 def deep_product(table, values, contract):

time: 98.4 us -> 98.4 us (level)
  no operation moved by 1% of the time
where the time goes in v14:
time: 98.4 us; the launch traced here: 98.1 us
  blocking collectives  93 us (95%)
  Pallas kernels  3.93 us (4%)
    all_to_all x4, blocking collectives, exchange(): lax.all_to_all(array, axis, split_axis=0, concat_axis=0, tiled=True)  93 us
    pallas_call x5, Pallas kernels, call(): pl.pallas_call(body, out_shape=shapes, in_specs=[in_spec] * len(args), ou...  3.93 us

profile of v14, /device:TPU:2, one launch (start us, length us, event | category | flops | bytes accessed | tf_op | source)
XLA Modules:
  0.0 98.1 jit_solution(8314458542865780982)
XLA Ops:
  0.0 0.0 copy-start.9
  0.0 0.9 pad_maximum_fusion.film_ref
  0.9 0.0 copy-done.9
  0.9 0.4 shard_map.118
  1.4 0.0 copy-start.2
  1.4 37.3 %all_to_all.20 = f32[16,11,4,128]{3,2,1,0:T(4,128)S(1)} all-to-all(f32[16,11,4,128]{3,2,1,0:T(4,128)S(1)} %bitcast.24), channel_id=1, replica_groups=mesh['row'=16,'col'=32] {'row'}, dimensions={0} | all-to-all | bytes 720896 | tf_op jit(solution)/shard_map/all_to_all | solution.py:408
  38.7 0.0 copy-done.2
  38.7 0.0 copy-start.4
  38.7 0.0 copy-start.7
  38.7 0.0 copy-start.8
  38.7 0.5 shard_map.119
  39.2 0.0 copy-start.1
  39.2 0.0 copy-start.5
  39.2 0.0 copy-start.6
  39.2 15.3 %all_to_all.21 = f32[32,2,8,128]{3,2,1,0:T(8,128)S(1)} all-to-all(f32[32,2,8,128]{3,2,1,0:T(8,128)S(1)} %bitcast.20), channel_id=1, replica_groups=mesh['row'=16,'col'=32] {'col'}, dimensions={0} | all-to-all | bytes 524288 | tf_op jit(solution)/shard_map/all_to_all | solution.py:408
  54.5 0.0 copy-done.4
  54.5 0.0 copy-done.7
  54.5 0.0 copy-done.8
  54.5 0.0 copy-done.1
  54.5 0.0 copy-done.5
  54.5 0.0 copy-done.6
  54.5 0.0 copy-start
  54.5 1.5 %shard_map.120 = f32[384,128]{1,0:T(8,128)S(1)} custom-call(f32[512,128]{1,0:T(8,128)S(1)} %bitcast.16, f32[768,128]{1,0:T(8,128)S(1)} %bitcast.23, bf16[128,128]{1,0:T(8,128)(2,1)S(1)} %copy-done.8, f32[6,64,128]{2,1,0:T(8,128)S(1)} %copy-done.4, bf16[128,256]{1,0:T(8,128)(2,1)S(1)} %copy-done.6, bf16[128,256]{1,0:T(8,128)(2,1)S(1)} %copy-done.5, ...), custom_call_target="tpu_custom_call" | custom-call | flops 100000000 | bytes 1000000 | tf_op jit(solution)/shard_map/pallas_call | solution.py:392
  56.0 11.9 %all_to_all.22 = f32[32,3,4,128]{3,2,1,0:T(4,128)S(1)} all-to-all(f32[32,3,4,128]{3,2,1,0:T(4,128)S(1)} %bitcast.21), channel_id=1, replica_groups=mesh['row'=16,'col'=32] {'col'}, dimensions={0} | all-to-all | bytes 393216 | tf_op jit(solution)/shard_map/all_to_all | solution.py:408
  67.9 0.0 copy-done
  67.9 0.5 shard_map.121
  68.4 0.0 copy-start.3
  68.4 28.6 %all_to_all.23 = f32[16,21,2,128]{3,2,1,0:T(2,128)S(1)} all-to-all(f32[16,21,2,128]{3,2,1,0:T(2,128)S(1)} %bitcast.19), channel_id=1, replica_groups=mesh['row'=16,'col'=32] {'row'}, dimensions={0} | all-to-all | bytes 688128 | tf_op jit(solution)/shard_map/all_to_all | solution.py:408
  97.0 0.0 copy-done.3
  97.0 1.1 %shard_map.122 = f32[3,64,128]{2,1,0:T(8,128)} custom-call(f32[672,128]{1,0:T(8,128)S(1)} %bitcast.18, f32[4,64,128]{2,1,0:T(8,128)S(1)} %pad_maximum_fusion.film_ref, f32[704,128]{1,0:T(8,128)S(1)} %bitcast.15, f32[512,128]{1,0:T(8,128)S(1)} %bitcast.17, bf16[224,512]{1,0:T(8,128)(2,1)S(1)} %copy-done.3), custom_call_target="tpu_custom_call" | custom-call | flops 100000000 | bytes 1000000 | tf_op jit(solution)/shard_map/pallas_call | solution.py:392
Async XLA Ops:
  0.0 0.9 copy-start.9
  1.4 37.3 %copy-start.2 = (bf16[512,224]{1,0:T(8,128)(2,1)S(1)}, bf16[512,224]{1,0:T(8,128)(2,1)}, u32[]{:S(2)}) copy-start(bf16[512,224]{1,0:T(8,128)(2,1)} %constant.19.clone.expand_ref) | copy-start | bytes 688132
  38.7 15.8 %copy-start.4 = (f32[6,64,128]{2,1,0:T(8,128)S(1)}, f32[6,64,128]{2,1,0:T(8,128)}, u32[]{:S(2)}) copy-start(f32[6,64,128]{2,1,0:T(8,128)} %constant.21.clone.twist_ref) | copy-start | bytes 589828
  38.7 15.8 %copy-start.7 = (bf16[64,256]{1,0:T(8,128)(2,1)S(1)}, bf16[64,256]{1,0:T(8,128)(2,1)}, u32[]{:S(2)}) copy-start(bf16[64,256]{1,0:T(8,128)(2,1)} %constant.24.clone.back_ref) | copy-start | bytes 98308
  38.7 15.8 %copy-start.8 = (bf16[128,128]{1,0:T(8,128)(2,1)S(1)}, bf16[128,128]{1,0:T(8,128)(2,1)}, u32[]{:S(2)}) copy-start(bf16[128,128]{1,0:T(8,128)(2,1)} %constant.20.clone.first_ref) | copy-start | bytes 98308
  39.2 15.3 %copy-start.1 = (f32[6,4,4096]{2,1,0:T(4,128)S(1)}, f32[6,4,4096]{2,1,0:T(4,128)}, u32[]{:S(2)}) copy-start(f32[6,4,4096]{2,1,0:T(4,128)} %param.14) | copy-start | bytes 1179652
  39.2 15.3 %copy-start.5 = (bf16[128,256]{1,0:T(8,128)(2,1)S(1)}, bf16[128,256]{1,0:T(8,128)(2,1)}, u32[]{:S(2)}) copy-start(bf16[128,256]{1,0:T(8,128)(2,1)} %constant.23.clone.lead_ref) | copy-start | bytes 196612
  39.2 15.3 %copy-start.6 = (bf16[128,256]{1,0:T(8,128)(2,1)S(1)}, bf16[128,256]{1,0:T(8,128)(2,1)}, u32[]{:S(2)}) copy-start(bf16[128,256]{1,0:T(8,128)(2,1)} %constant.22.clone.last_ref) | copy-start | bytes 196612
  54.5 13.4 %copy-start = (bf16[448,512]{1,0:T(8,128)(2,1)S(1)}, bf16[448,512]{1,0:T(8,128)(2,1)}, u32[]{:S(2)}) copy-start(bf16[448,512]{1,0:T(8,128)(2,1)} %constant.25.clone.gather_ref) | copy-start | bytes 1376260
  68.4 28.6 %copy-start.3 = (bf16[224,512]{1,0:T(8,128)(2,1)S(1)}, bf16[224,512]{1,0:T(8,128)(2,1)}, u32[]{:S(2)}) copy-start(bf16[224,512]{1,0:T(8,128)(2,1)} %constant.26.clone.expand_ref) | copy-start | bytes 688132
